TPU v7x, 32 devices: a whole 2x2x4 slice. The times are simulated.
32 devices in a mesh: inner: 4 (over y, x), outer: 8 (over z, core).
Axes of the slice: x: 2, y: 2, z: 4, core: 2. Of those that a mesh axis runs over, the one named last changes fastest.
Arguments:
- queries: bfloat16 [4096, 512], P(('inner', 'outer')), may hold values from -6 to 6
- keys_values: bfloat16 [4096, 256], P(('inner', 'outer')), may hold values from -6 to 6
- outputs: bfloat16 [4096, 512], P(('inner', 'outer')), may hold values from -3 to 3
- d_out: bfloat16 [4096, 512], P(('inner', 'outer')), may hold values from -6 to 6
- lse: float32 [4096, 4], P(('inner', 'outer'))
- doc_start: int32 [4096], P(('inner', 'outer')), may hold values from 0 to 4095, as said below
Outputs:
- d_queries: bfloat16 [4096, 512], P(('inner', 'outer'))
- d_keys_values: bfloat16 [4096, 256], P(('inner', 'outer'))
Inputs may be any that keep to these rules, and one draw needn't show every extreme that they name: doc_start of a token is the first sequence position of the document that holds it; documents are 8 or fewer runs of consecutive positions, the first starting at position 0.
All inputs are finite; a program needn't handle non-finite values.
Results may differ from a plain program's by a relative error of at most 0.0047.
Values may be sent and summed in bfloat16 or wider, within the bound.
No kernel may reach another device: no remote copies, remote signals or barrier semaphores. Data moves between devices by JAX's collectives and lax.ppermute only.
A program may use at most 64 MiB of HBM per device.

v0:
```python
import jax
import jax.numpy as jnp
from jax import lax
from jax.sharding import PartitionSpec as P


def from_behind(value, axis, steps):
    count = lax.axis_size(axis)
    pairs = [(source, (source + steps) % count) for source in range(count)]
    return lax.ppermute(value, axis, pairs)


def on_device(queries, keys_values, outputs, d_out, lse, doc_start):
    group_size = lax.axis_size("inner")
    loop_size = lax.axis_size("outer")
    tok_rows = queries.shape[0]
    half_rows = tok_rows // 2
    head_width = keys_values.shape[1] // 2
    head_count = lse.shape[1]
    query_cols = head_count * head_width
    score_scale = head_width ** (-0.5)
    inner_place = lax.axis_index("inner")
    outer_place = lax.axis_index("outer")
    band_len = group_size * half_rows
    row_ids = jnp.arange(tok_rows, dtype=jnp.int32)
    key_ids = jnp.arange(group_size * tok_rows, dtype=jnp.int32)
    key_member = key_ids // tok_rows
    key_offset = key_ids % tok_rows

    def query_positions(source):
        band = jnp.where(row_ids < half_rows, source, 2 * loop_size - 1 - source)
        return band * band_len + inner_place * half_rows + row_ids % half_rows

    def key_positions(source):
        band = jnp.where(key_offset < half_rows, source, 2 * loop_size - 1 - source)
        return band * band_len + key_member * half_rows + key_offset % half_rows

    grad_heads_all = d_out.reshape(tok_rows, head_count, head_width)
    out_heads = outputs.reshape(tok_rows, head_count, head_width)
    delta_rows = jnp.sum(
        grad_heads_all.astype(jnp.float32) * out_heads.astype(jnp.float32), axis=2
    ).T
    own_pack = jnp.concatenate([queries, d_out], axis=1)
    own_stats = jnp.concatenate([lse.T, delta_rows], axis=0)

    def block_grads(pack, stats, starts, pos_rows, first, count, kv_block, key_pos):
        rows = pack[first : first + count]
        query_part = rows[:, :query_cols].reshape(count, head_count, head_width)
        grad_part = rows[:, query_cols:].reshape(count, head_count, head_width)
        pos_part = pos_rows[first : first + count]
        start_part = starts[first : first + count]
        log_part = stats[:head_count, first : first + count]
        delta_part = stats[head_count:, first : first + count]
        key_part = kv_block[:, :head_width]
        value_part = kv_block[:, head_width:]
        mask = jnp.logical_and(
            key_pos[None, :] <= pos_part[:, None], key_pos[None, :] >= start_part[:, None]
        )
        score = (
            jnp.einsum("qhd,kd->hqk", query_part, key_part, preferred_element_type=jnp.float32)
            * score_scale
        )
        prob = jnp.where(mask[None], jnp.exp(score - log_part[:, :, None]), 0.0)
        dprob = jnp.einsum("qhd,kd->hqk", grad_part, value_part, preferred_element_type=jnp.float32)
        dscore = (prob * (dprob - delta_part[:, :, None])).astype(jnp.bfloat16)
        prob_half = prob.astype(jnp.bfloat16)
        query_grad = (
            jnp.einsum("hqk,kd->qhd", dscore, key_part, preferred_element_type=jnp.float32)
            * score_scale
        )
        key_grad = (
            jnp.einsum("hqk,qhd->kd", dscore, query_part, preferred_element_type=jnp.float32)
            * score_scale
        )
        value_grad = jnp.einsum(
            "hqk,qhd->kd", prob_half, grad_part, preferred_element_type=jnp.float32
        )
        return (
            query_grad.reshape(count, query_cols),
            jnp.concatenate([key_grad, value_grad], axis=1),
        )

    def front_half(kv_block, key_pos):
        shaped = kv_block.reshape(group_size, 2, half_rows, 2 * head_width)
        front = shaped[:, 0].reshape(group_size * half_rows, 2 * head_width)
        front_pos = key_pos.reshape(group_size, 2, half_rows)[:, 0].reshape(group_size * half_rows)
        return (front, front_pos)

    def spread_front(pair_grad):
        empty = jnp.zeros((group_size, half_rows, 2 * head_width), jnp.float32)
        spread = jnp.stack(
            [pair_grad.reshape(group_size, half_rows, 2 * head_width), empty], axis=1
        )
        return spread.reshape(group_size * tok_rows, 2 * head_width)

    def visit(pack, stats, starts, query_source, kv_block, key_source):
        key_pos = key_positions(key_source)
        pos_rows = query_positions(query_source)

        def early_keys(kv_now):
            front, front_pos = front_half(kv_now, key_pos)
            query_grad, pair_grad = block_grads(
                pack, stats, starts, pos_rows, 0, tok_rows, front, front_pos
            )
            return (query_grad, spread_front(pair_grad))

        def late_queries(kv_now):
            query_grad, pair_grad = block_grads(
                pack, stats, starts, pos_rows, half_rows, half_rows, kv_now, key_pos
            )
            empty = jnp.zeros((half_rows, query_cols), jnp.float32)
            return (jnp.concatenate([empty, query_grad], axis=0), pair_grad)

        return lax.cond(key_source < query_source, early_keys, late_queries, kv_block)

    gathered = lax.all_gather(keys_values, "inner", axis=0, tiled=True)
    home_query, home_pairs = block_grads(
        own_pack,
        own_stats,
        doc_start,
        query_positions(outer_place),
        0,
        tok_rows,
        gathered,
        key_positions(outer_place),
    )

    def onward_rows(turn_index, carry):
        pack, stats, starts, query_acc, pair_totals = carry
        pack = from_behind(pack, "outer", 1)
        query_acc, stats = from_behind((query_acc, stats), "outer", 1)
        starts = from_behind(starts, "outer", 1)
        source = (outer_place - turn_index) % loop_size
        query_part, pair_part = visit(pack, stats, starts, source, gathered, outer_place)
        return (pack, stats, starts, query_acc + query_part, pair_totals + pair_part)

    final = lax.fori_loop(
        1, loop_size, onward_rows, (own_pack, own_stats, doc_start, home_query, home_pairs)
    )
    query_total = from_behind(final[3].astype(jnp.bfloat16), "outer", 1).astype(jnp.float32)
    collected = final[4]
    own_pairs = lax.psum_scatter(collected, "inner", scatter_dimension=0, tiled=True)
    return (query_total.astype(jnp.bfloat16), own_pairs.astype(jnp.bfloat16))


def solution(mesh):
    return jax.shard_map(
        on_device,
        mesh=mesh,
        in_specs=(
            P(("inner", "outer"), None),
            P(("inner", "outer"), None),
            P(("inner", "outer"), None),
            P(("inner", "outer"), None),
            P(("inner", "outer"), None),
            P(("inner", "outer")),
        ),
        out_specs=(P(("inner", "outer"), None), P(("inner", "outer"), None)),
        check_vma=False,
    )
```

profile of v0, /device:TPU:0, one launch (start us, length us, event | category | flops | bytes accessed | tf_op | source)
XLA Modules:
  0.0 143.8 jit_solution(5038407010746571814)
XLA Ops:
  7.9 10.9 %all_gather.3 = bf16[512,256]{1,0:T(8,128)(2,1)S(1)} all-gather(bf16[128,256]{1,0:T(8,128)(2,1)} %param.11), channel_id=1, replica_groups=mesh['inner'=4,'outer'=8] {'inner'}, dimensions={0}, use_global_device_ids=true | all-gather | bytes 327680 | tf_op jit(solution)/shard_map/all_gather | solution.py:116
  19.7 0.9 copy-done.2
  23.9 87.9 %while.27 = (s32[]{:T(128)}, bf16[128,1024]{0,1:T(8,128)(2,1)S(1)}, f32[8,128]{1,0:T(8,128)S(1)}, s32[128]{0:T(128)S(1)}, f32[128,512]{0,1:T(8,128)S(1)}, /*inde...) while((s32[]{:T(128)}, bf16[128,1024]{0,1:T(8,128)(2,1)S(1)}, ...), condition=%wide.region_4.5_spmd.clone.clone, body=%wide.region_1.4_spmd.clone.clone.sunk | while | flops 169230224 | bytes 12297752 | solution.py:137
  23.9 1.7 %collective-permute-start.3 = (f32[128,512]{0,1:T(8,128)S(1)}, f32[128,512]{0,1:T(8,128)S(1)}, u32[]{:S(2)}, u32[]{:S(2)}) collective-permute-start(f32[128,512]{0,1:T(8,128)S(1)} %get-tuple-element.711), channel_id=1, source_target_pairs={{0,1},{1,2},{2,3},{3,4},{4,5},{5,6},{6,7},{7,0},{8,9},{9,10},{10,1... | collective-permute-start | bytes 786440 | tf_op jit(solution)/shard_map/while/body/eval_jaxpr/ppermute | solution.py:10
  25.7 1.6 %collective-permute-start.2 = (s32[128]{0:T(128)S(1)}, s32[128]{0:T(128)S(1)}, u32[]{:S(2)}, u32[]{:S(2)}) collective-permute-start(s32[128]{0:T(128)S(1)} %get-tuple-element.710), channel_id=1, source_target_pairs={{0,1},{1,2},{2,3},{3,4},{4,5},{5,6},{6,7},{7,0},{8,9},{9,10},{10,1... | collective-permute-start | bytes 1544 | tf_op jit(solution)/shard_map/while/body/eval_jaxpr/ppermute | solution.py:10
  27.3 7.1 %collective-permute-done.2 = s32[128]{0:T(128)S(1)} collective-permute-done((s32[128]{0:T(128)S(1)}, s32[128]{0:T(128)S(1)}, u32[]{:S(2)}, u32[]{:S(2)}) %collective-permute-start.2) | collective-permute-done | bytes 544 | tf_op jit(solution)/shard_map/while/body/eval_jaxpr/ppermute | solution.py:10
  34.5 1.8 %conditional.4 = (f32[128,512]{0,1:T(8,128)S(1)}, f32[512,256]{1,0:T(8,128)S(1)}) conditional(s32[]{:T(128)} %convert_element_type.68, (s32[512]{0:T(512)S(1)}, s32[128]{0:T(128)S(1)}, s32[128]{0:T(128)S(1)}, bf16[512,256]{1,0:T(8,128)(2,1)S(1)}, bf16[128,1024]{0,1:T(8,128)(2,1)S(1)}, /*index=5*/f32[8,128]{1,0:T(8,128)S(1)}) %tuple.82, ...), branch_computations={%region_2.2_spmd, %region_3.3_spmd} | conditional | flops 169017344 | bytes 7286292 | solution.py:114
  36.9 1.6 %collective-permute-start.2 = (s32[128]{0:T(128)S(1)}, s32[128]{0:T(128)S(1)}, u32[]{:S(2)}, u32[]{:S(2)}) collective-permute-start(s32[128]{0:T(128)S(1)} %get-tuple-element.710), channel_id=1, source_target_pairs={{0,1},{1,2},{2,3},{3,4},{4,5},{5,6},{6,7},{7,0},{8,9},{9,10},{10,1... | collective-permute-start | bytes 1544 | tf_op jit(solution)/shard_map/while/body/eval_jaxpr/ppermute | solution.py:10
  38.6 8.4 %collective-permute-done.2 = s32[128]{0:T(128)S(1)} collective-permute-done((s32[128]{0:T(128)S(1)}, s32[128]{0:T(128)S(1)}, u32[]{:S(2)}, u32[]{:S(2)}) %collective-permute-start.2) | collective-permute-done | bytes 544 | tf_op jit(solution)/shard_map/while/body/eval_jaxpr/ppermute | solution.py:10
  47.0 1.8 %conditional.4 = (f32[128,512]{0,1:T(8,128)S(1)}, f32[512,256]{1,0:T(8,128)S(1)}) conditional(s32[]{:T(128)} %convert_element_type.68, (s32[512]{0:T(512)S(1)}, s32[128]{0:T(128)S(1)}, s32[128]{0:T(128)S(1)}, bf16[512,256]{1,0:T(8,128)(2,1)S(1)}, bf16[128,1024]{0,1:T(8,128)(2,1)S(1)}, /*index=5*/f32[8,128]{1,0:T(8,128)S(1)}) %tuple.82, ...), branch_computations={%region_2.2_spmd, %region_3.3_spmd} | conditional | flops 169017344 | bytes 7286292 | solution.py:114
  49.8 9.8 %collective-permute-done.2 = s32[128]{0:T(128)S(1)} collective-permute-done((s32[128]{0:T(128)S(1)}, s32[128]{0:T(128)S(1)}, u32[]{:S(2)}, u32[]{:S(2)}) %collective-permute-start.2) | collective-permute-done | bytes 544 | tf_op jit(solution)/shard_map/while/body/eval_jaxpr/ppermute | solution.py:10
  59.6 1.8 %conditional.4 = (f32[128,512]{0,1:T(8,128)S(1)}, f32[512,256]{1,0:T(8,128)S(1)}) conditional(s32[]{:T(128)} %convert_element_type.68, (s32[512]{0:T(512)S(1)}, s32[128]{0:T(128)S(1)}, s32[128]{0:T(128)S(1)}, bf16[512,256]{1,0:T(8,128)(2,1)S(1)}, bf16[128,1024]{0,1:T(8,128)(2,1)S(1)}, /*index=5*/f32[8,128]{1,0:T(8,128)S(1)}) %tuple.82, ...), branch_computations={%region_2.2_spmd, %region_3.3_spmd} | conditional | flops 169017344 | bytes 7286292 | solution.py:114
  61.9 10.2 %collective-permute-done.2 = s32[128]{0:T(128)S(1)} collective-permute-done((s32[128]{0:T(128)S(1)}, s32[128]{0:T(128)S(1)}, u32[]{:S(2)}, u32[]{:S(2)}) %collective-permute-start.2) | collective-permute-done | bytes 544 | tf_op jit(solution)/shard_map/while/body/eval_jaxpr/ppermute | solution.py:10
  72.1 1.8 %conditional.4 = (f32[128,512]{0,1:T(8,128)S(1)}, f32[512,256]{1,0:T(8,128)S(1)}) conditional(s32[]{:T(128)} %convert_element_type.68, (s32[512]{0:T(512)S(1)}, s32[128]{0:T(128)S(1)}, s32[128]{0:T(128)S(1)}, bf16[512,256]{1,0:T(8,128)(2,1)S(1)}, bf16[128,1024]{0,1:T(8,128)(2,1)S(1)}, /*index=5*/f32[8,128]{1,0:T(8,128)S(1)}) %tuple.82, ...), branch_computations={%region_2.2_spmd, %region_3.3_spmd} | conditional | flops 169017344 | bytes 7286292 | solution.py:114
  74.5 10.2 %collective-permute-done.2 = s32[128]{0:T(128)S(1)} collective-permute-done((s32[128]{0:T(128)S(1)}, s32[128]{0:T(128)S(1)}, u32[]{:S(2)}, u32[]{:S(2)}) %collective-permute-start.2) | collective-permute-done | bytes 544 | tf_op jit(solution)/shard_map/while/body/eval_jaxpr/ppermute | solution.py:10
  84.7 1.8 %conditional.4 = (f32[128,512]{0,1:T(8,128)S(1)}, f32[512,256]{1,0:T(8,128)S(1)}) conditional(s32[]{:T(128)} %convert_element_type.68, (s32[512]{0:T(512)S(1)}, s32[128]{0:T(128)S(1)}, s32[128]{0:T(128)S(1)}, bf16[512,256]{1,0:T(8,128)(2,1)S(1)}, bf16[128,1024]{0,1:T(8,128)(2,1)S(1)}, /*index=5*/f32[8,128]{1,0:T(8,128)S(1)}) %tuple.82, ...), branch_computations={%region_2.2_spmd, %region_3.3_spmd} | conditional | flops 169017344 | bytes 7286292 | solution.py:114
  87.0 10.2 %collective-permute-done.2 = s32[128]{0:T(128)S(1)} collective-permute-done((s32[128]{0:T(128)S(1)}, s32[128]{0:T(128)S(1)}, u32[]{:S(2)}, u32[]{:S(2)}) %collective-permute-start.2) | collective-permute-done | bytes 544 | tf_op jit(solution)/shard_map/while/body/eval_jaxpr/ppermute | solution.py:10
  97.3 1.8 %conditional.4 = (f32[128,512]{0,1:T(8,128)S(1)}, f32[512,256]{1,0:T(8,128)S(1)}) conditional(s32[]{:T(128)} %convert_element_type.68, (s32[512]{0:T(512)S(1)}, s32[128]{0:T(128)S(1)}, s32[128]{0:T(128)S(1)}, bf16[512,256]{1,0:T(8,128)(2,1)S(1)}, bf16[128,1024]{0,1:T(8,128)(2,1)S(1)}, /*index=5*/f32[8,128]{1,0:T(8,128)S(1)}) %tuple.82, ...), branch_computations={%region_2.2_spmd, %region_3.3_spmd} | conditional | flops 169017344 | bytes 7286292 | solution.py:114
  99.6 10.2 %collective-permute-done.2 = s32[128]{0:T(128)S(1)} collective-permute-done((s32[128]{0:T(128)S(1)}, s32[128]{0:T(128)S(1)}, u32[]{:S(2)}, u32[]{:S(2)}) %collective-permute-start.2) | collective-permute-done | bytes 544 | tf_op jit(solution)/shard_map/while/body/eval_jaxpr/ppermute | solution.py:10
  109.8 1.8 %conditional.4 = (f32[128,512]{0,1:T(8,128)S(1)}, f32[512,256]{1,0:T(8,128)S(1)}) conditional(s32[]{:T(128)} %convert_element_type.68, (s32[512]{0:T(512)S(1)}, s32[128]{0:T(128)S(1)}, s32[128]{0:T(128)S(1)}, bf16[512,256]{1,0:T(8,128)(2,1)S(1)}, bf16[128,1024]{0,1:T(8,128)(2,1)S(1)}, /*index=5*/f32[8,128]{1,0:T(8,128)S(1)}) %tuple.82, ...), branch_computations={%region_2.2_spmd, %region_3.3_spmd} | conditional | flops 169017344 | bytes 7286292 | solution.py:114
  111.8 0.8 copy-done
  112.8 6.2 %collective-permute-done.4 = bf16[128,512]{1,0:T(8,128)(2,1)S(1)} collective-permute-done((bf16[128,512]{1,0:T(8,128)(2,1)S(1)}, bf16[128,512]{1,0:T(8,128)(2,1)S(1)}, u32[]{:S(2)}, u32[]{:S(2)}) %collective-permute-start.4) | collective-permute-done | bytes 131104 | tf_op jit(solution)/shard_map/ppermute | solution.py:10
  119.0 15.8 %reduce-scatter.2.cloned.1.call-done = f32[128,256]{1,0:T(8,128)} async-done(((f32[512,256]{1,0:T(8,128)}), f32[128,256]{1,0:T(8,128)}) %reduce-scatter.2.cloned.1.call-update) | async-done | bytes 131088 | tf_op jit(solution)/shard_map/reduce_scatter | solution.py:142
  134.8 1.5 %convert_element_type.53 = bf16[128,256]{1,0:T(8,128)(2,1)} convert(f32[128,256]{1,0:T(8,128)} %reduce-scatter.2.cloned.1.call-done) | non-fusion elementwise | flops 32768 | bytes 196608 | tf_op jit(solution)/shard_map/convert_element_type | solution.py:143
  (233 shorter events, 20.9 us)
Async XLA Ops:
  7.2 127.6 %reduce-scatter.2.cloned.1.call-start = ((), (), s32[]{:S(2)}) async-start(), calls=%async_computation.1 | async-start | bytes 655360 | tf_op jit(solution)/shard_map/reduce_scatter | solution.py:142
  23.9 10.6 %collective-permute-start = (bf16[128,1024]{0,1:T(8,128)(2,1)S(1)}, bf16[128,1024]{0,1:T(8,128)(2,1)S(1)}, u32[]{:S(2)}, u32[]{:S(2)}) collective-permute-start(bf16[128,1024]{0,1:T(8,128)(2,1)S(1)} %get-tuple-element.708), channel_id=1, source_target_pairs={{0,1},{1,2},{2,3},{3,4},{4,5},{5,6},{6,7},{7,0},{8,9},{9,10},{10,1... | collective-permute-start | bytes 786440 | tf_op jit(solution)/shard_map/while/body/eval_jaxpr/ppermute | solution.py:10
  23.9 12.4 %collective-permute-start.3 = (f32[128,512]{0,1:T(8,128)S(1)}, f32[128,512]{0,1:T(8,128)S(1)}, u32[]{:S(2)}, u32[]{:S(2)}) collective-permute-start(f32[128,512]{0,1:T(8,128)S(1)} %get-tuple-element.711), channel_id=1, source_target_pairs={{0,1},{1,2},{2,3},{3,4},{4,5},{5,6},{6,7},{7,0},{8,9},{9,10},{10,1... | collective-permute-start | bytes 786440 | tf_op jit(solution)/shard_map/while/body/eval_jaxpr/ppermute | solution.py:10
  36.4 10.6 %collective-permute-start = (bf16[128,1024]{0,1:T(8,128)(2,1)S(1)}, bf16[128,1024]{0,1:T(8,128)(2,1)S(1)}, u32[]{:S(2)}, u32[]{:S(2)}) collective-permute-start(bf16[128,1024]{0,1:T(8,128)(2,1)S(1)} %get-tuple-element.708), channel_id=1, source_target_pairs={{0,1},{1,2},{2,3},{3,4},{4,5},{5,6},{6,7},{7,0},{8,9},{9,10},{10,1... | collective-permute-start | bytes 786440 | tf_op jit(solution)/shard_map/while/body/eval_jaxpr/ppermute | solution.py:10
  36.5 12.4 %collective-permute-start.3 = (f32[128,512]{0,1:T(8,128)S(1)}, f32[128,512]{0,1:T(8,128)S(1)}, u32[]{:S(2)}, u32[]{:S(2)}) collective-permute-start(f32[128,512]{0,1:T(8,128)S(1)} %get-tuple-element.711), channel_id=1, source_target_pairs={{0,1},{1,2},{2,3},{3,4},{4,5},{5,6},{6,7},{7,0},{8,9},{9,10},{10,1... | collective-permute-start | bytes 786440 | tf_op jit(solution)/shard_map/while/body/eval_jaxpr/ppermute | solution.py:10
  49.0 10.6 %collective-permute-start = (bf16[128,1024]{0,1:T(8,128)(2,1)S(1)}, bf16[128,1024]{0,1:T(8,128)(2,1)S(1)}, u32[]{:S(2)}, u32[]{:S(2)}) collective-permute-start(bf16[128,1024]{0,1:T(8,128)(2,1)S(1)} %get-tuple-element.708), channel_id=1, source_target_pairs={{0,1},{1,2},{2,3},{3,4},{4,5},{5,6},{6,7},{7,0},{8,9},{9,10},{10,1... | collective-permute-start | bytes 786440 | tf_op jit(solution)/shard_map/while/body/eval_jaxpr/ppermute | solution.py:10
  49.1 12.4 %collective-permute-start.3 = (f32[128,512]{0,1:T(8,128)S(1)}, f32[128,512]{0,1:T(8,128)S(1)}, u32[]{:S(2)}, u32[]{:S(2)}) collective-permute-start(f32[128,512]{0,1:T(8,128)S(1)} %get-tuple-element.711), channel_id=1, source_target_pairs={{0,1},{1,2},{2,3},{3,4},{4,5},{5,6},{6,7},{7,0},{8,9},{9,10},{10,1... | collective-permute-start | bytes 786440 | tf_op jit(solution)/shard_map/while/body/eval_jaxpr/ppermute | solution.py:10
  49.1 10.4 %collective-permute-start.1 = (f32[8,128]{1,0:T(8,128)S(1)}, f32[8,128]{1,0:T(8,128)S(1)}, u32[]{:S(2)}, u32[]{:S(2)}) collective-permute-start(f32[8,128]{1,0:T(8,128)S(1)} %get-tuple-element.709), channel_id=1, source_target_pairs={{0,1},{1,2},{2,3},{3,4},{4,5},{5,6},{6,7},{7,0},{8,9},{9,10},{10,1... | collective-permute-start | bytes 12296 | tf_op jit(solution)/shard_map/while/body/eval_jaxpr/ppermute | solution.py:10
  49.2 10.4 %collective-permute-start.2 = (s32[128]{0:T(128)S(1)}, s32[128]{0:T(128)S(1)}, u32[]{:S(2)}, u32[]{:S(2)}) collective-permute-start(s32[128]{0:T(128)S(1)} %get-tuple-element.710), channel_id=1, source_target_pairs={{0,1},{1,2},{2,3},{3,4},{4,5},{5,6},{6,7},{7,0},{8,9},{9,10},{10,1... | collective-permute-start | bytes 1544 | tf_op jit(solution)/shard_map/while/body/eval_jaxpr/ppermute | solution.py:10
  61.6 10.6 %collective-permute-start = (bf16[128,1024]{0,1:T(8,128)(2,1)S(1)}, bf16[128,1024]{0,1:T(8,128)(2,1)S(1)}, u32[]{:S(2)}, u32[]{:S(2)}) collective-permute-start(bf16[128,1024]{0,1:T(8,128)(2,1)S(1)} %get-tuple-element.708), channel_id=1, source_target_pairs={{0,1},{1,2},{2,3},{3,4},{4,5},{5,6},{6,7},{7,0},{8,9},{9,10},{10,1... | collective-permute-start | bytes 786440 | tf_op jit(solution)/shard_map/while/body/eval_jaxpr/ppermute | solution.py:10
  61.6 12.4 %collective-permute-start.3 = (f32[128,512]{0,1:T(8,128)S(1)}, f32[128,512]{0,1:T(8,128)S(1)}, u32[]{:S(2)}, u32[]{:S(2)}) collective-permute-start(f32[128,512]{0,1:T(8,128)S(1)} %get-tuple-element.711), channel_id=1, source_target_pairs={{0,1},{1,2},{2,3},{3,4},{4,5},{5,6},{6,7},{7,0},{8,9},{9,10},{10,1... | collective-permute-start | bytes 786440 | tf_op jit(solution)/shard_map/while/body/eval_jaxpr/ppermute | solution.py:10
  61.7 10.4 %collective-permute-start.1 = (f32[8,128]{1,0:T(8,128)S(1)}, f32[8,128]{1,0:T(8,128)S(1)}, u32[]{:S(2)}, u32[]{:S(2)}) collective-permute-start(f32[8,128]{1,0:T(8,128)S(1)} %get-tuple-element.709), channel_id=1, source_target_pairs={{0,1},{1,2},{2,3},{3,4},{4,5},{5,6},{6,7},{7,0},{8,9},{9,10},{10,1... | collective-permute-start | bytes 12296 | tf_op jit(solution)/shard_map/while/body/eval_jaxpr/ppermute | solution.py:10
  61.8 10.4 %collective-permute-start.2 = (s32[128]{0:T(128)S(1)}, s32[128]{0:T(128)S(1)}, u32[]{:S(2)}, u32[]{:S(2)}) collective-permute-start(s32[128]{0:T(128)S(1)} %get-tuple-element.710), channel_id=1, source_target_pairs={{0,1},{1,2},{2,3},{3,4},{4,5},{5,6},{6,7},{7,0},{8,9},{9,10},{10,1... | collective-permute-start | bytes 1544 | tf_op jit(solution)/shard_map/while/body/eval_jaxpr/ppermute | solution.py:10
  74.1 10.6 %collective-permute-start = (bf16[128,1024]{0,1:T(8,128)(2,1)S(1)}, bf16[128,1024]{0,1:T(8,128)(2,1)S(1)}, u32[]{:S(2)}, u32[]{:S(2)}) collective-permute-start(bf16[128,1024]{0,1:T(8,128)(2,1)S(1)} %get-tuple-element.708), channel_id=1, source_target_pairs={{0,1},{1,2},{2,3},{3,4},{4,5},{5,6},{6,7},{7,0},{8,9},{9,10},{10,1... | collective-permute-start | bytes 786440 | tf_op jit(solution)/shard_map/while/body/eval_jaxpr/ppermute | solution.py:10
  74.2 12.4 %collective-permute-start.3 = (f32[128,512]{0,1:T(8,128)S(1)}, f32[128,512]{0,1:T(8,128)S(1)}, u32[]{:S(2)}, u32[]{:S(2)}) collective-permute-start(f32[128,512]{0,1:T(8,128)S(1)} %get-tuple-element.711), channel_id=1, source_target_pairs={{0,1},{1,2},{2,3},{3,4},{4,5},{5,6},{6,7},{7,0},{8,9},{9,10},{10,1... | collective-permute-start | bytes 786440 | tf_op jit(solution)/shard_map/while/body/eval_jaxpr/ppermute | solution.py:10
  74.3 10.4 %collective-permute-start.1 = (f32[8,128]{1,0:T(8,128)S(1)}, f32[8,128]{1,0:T(8,128)S(1)}, u32[]{:S(2)}, u32[]{:S(2)}) collective-permute-start(f32[8,128]{1,0:T(8,128)S(1)} %get-tuple-element.709), channel_id=1, source_target_pairs={{0,1},{1,2},{2,3},{3,4},{4,5},{5,6},{6,7},{7,0},{8,9},{9,10},{10,1... | collective-permute-start | bytes 12296 | tf_op jit(solution)/shard_map/while/body/eval_jaxpr/ppermute | solution.py:10
  74.3 10.4 %collective-permute-start.2 = (s32[128]{0:T(128)S(1)}, s32[128]{0:T(128)S(1)}, u32[]{:S(2)}, u32[]{:S(2)}) collective-permute-start(s32[128]{0:T(128)S(1)} %get-tuple-element.710), channel_id=1, source_target_pairs={{0,1},{1,2},{2,3},{3,4},{4,5},{5,6},{6,7},{7,0},{8,9},{9,10},{10,1... | collective-permute-start | bytes 1544 | tf_op jit(solution)/shard_map/while/body/eval_jaxpr/ppermute | solution.py:10
  86.7 10.6 %collective-permute-start = (bf16[128,1024]{0,1:T(8,128)(2,1)S(1)}, bf16[128,1024]{0,1:T(8,128)(2,1)S(1)}, u32[]{:S(2)}, u32[]{:S(2)}) collective-permute-start(bf16[128,1024]{0,1:T(8,128)(2,1)S(1)} %get-tuple-element.708), channel_id=1, source_target_pairs={{0,1},{1,2},{2,3},{3,4},{4,5},{5,6},{6,7},{7,0},{8,9},{9,10},{10,1... | collective-permute-start | bytes 786440 | tf_op jit(solution)/shard_map/while/body/eval_jaxpr/ppermute | solution.py:10
  86.8 12.4 %collective-permute-start.3 = (f32[128,512]{0,1:T(8,128)S(1)}, f32[128,512]{0,1:T(8,128)S(1)}, u32[]{:S(2)}, u32[]{:S(2)}) collective-permute-start(f32[128,512]{0,1:T(8,128)S(1)} %get-tuple-element.711), channel_id=1, source_target_pairs={{0,1},{1,2},{2,3},{3,4},{4,5},{5,6},{6,7},{7,0},{8,9},{9,10},{10,1... | collective-permute-start | bytes 786440 | tf_op jit(solution)/shard_map/while/body/eval_jaxpr/ppermute | solution.py:10
  86.8 10.4 %collective-permute-start.1 = (f32[8,128]{1,0:T(8,128)S(1)}, f32[8,128]{1,0:T(8,128)S(1)}, u32[]{:S(2)}, u32[]{:S(2)}) collective-permute-start(f32[8,128]{1,0:T(8,128)S(1)} %get-tuple-element.709), channel_id=1, source_target_pairs={{0,1},{1,2},{2,3},{3,4},{4,5},{5,6},{6,7},{7,0},{8,9},{9,10},{10,1... | collective-permute-start | bytes 12296 | tf_op jit(solution)/shard_map/while/body/eval_jaxpr/ppermute | solution.py:10
  99.3 10.6 %collective-permute-start = (bf16[128,1024]{0,1:T(8,128)(2,1)S(1)}, bf16[128,1024]{0,1:T(8,128)(2,1)S(1)}, u32[]{:S(2)}, u32[]{:S(2)}) collective-permute-start(bf16[128,1024]{0,1:T(8,128)(2,1)S(1)} %get-tuple-element.708), channel_id=1, source_target_pairs={{0,1},{1,2},{2,3},{3,4},{4,5},{5,6},{6,7},{7,0},{8,9},{9,10},{10,1... | collective-permute-start | bytes 786440 | tf_op jit(solution)/shard_map/while/body/eval_jaxpr/ppermute | solution.py:10
  99.3 12.4 %collective-permute-start.3 = (f32[128,512]{0,1:T(8,128)S(1)}, f32[128,512]{0,1:T(8,128)S(1)}, u32[]{:S(2)}, u32[]{:S(2)}) collective-permute-start(f32[128,512]{0,1:T(8,128)S(1)} %get-tuple-element.711), channel_id=1, source_target_pairs={{0,1},{1,2},{2,3},{3,4},{4,5},{5,6},{6,7},{7,0},{8,9},{9,10},{10,1... | collective-permute-start | bytes 786440 | tf_op jit(solution)/shard_map/while/body/eval_jaxpr/ppermute | solution.py:10
  99.4 10.4 %collective-permute-start.1 = (f32[8,128]{1,0:T(8,128)S(1)}, f32[8,128]{1,0:T(8,128)S(1)}, u32[]{:S(2)}, u32[]{:S(2)}) collective-permute-start(f32[8,128]{1,0:T(8,128)S(1)} %get-tuple-element.709), channel_id=1, source_target_pairs={{0,1},{1,2},{2,3},{3,4},{4,5},{5,6},{6,7},{7,0},{8,9},{9,10},{10,1... | collective-permute-start | bytes 12296 | tf_op jit(solution)/shard_map/while/body/eval_jaxpr/ppermute | solution.py:10
  99.5 10.4 %collective-permute-start.2 = (s32[128]{0:T(128)S(1)}, s32[128]{0:T(128)S(1)}, u32[]{:S(2)}, u32[]{:S(2)}) collective-permute-start(s32[128]{0:T(128)S(1)} %get-tuple-element.710), channel_id=1, source_target_pairs={{0,1},{1,2},{2,3},{3,4},{4,5},{5,6},{6,7},{7,0},{8,9},{9,10},{10,1... | collective-permute-start | bytes 1544 | tf_op jit(solution)/shard_map/while/body/eval_jaxpr/ppermute | solution.py:10
  (11 other events, 68.6 us)
Sparse Core Ops, SparseCore 0:
  112.8 21.9 reduce-scatter.1
where the time goes:
time: 144 us
  waiting for transfers between devices  88.4 us (61%)
  between operations  14.2 us (10%)
  blocking collectives  10.9 us (8%)
  matrix products  9.52 us (7%)
  local copies, waits for them, and re-layouts  8.18 us (6%)
  starting transfers between devices  7.27 us (5%)
  other arithmetic  4.02 us (3%)
  loops' own time  1.44 us (1%)
    ppermute x29, waiting for transfers between devices, from_behind(): return lax.ppermute(value, axis, pairs)  72.5 us
    reduce_scatter x1, waiting for transfers between devices, on_device(): lax.psum_scatter(collected, 'inner', scatter_dimension=0, tiled=True)  15.8 us
    all_gather x1, blocking collectives, on_device(): gathered = lax.all_gather(keys_values, 'inner', axis=0, tiled=True)  10.9 us
    ppermute x29, starting transfers between devices, from_behind(): return lax.ppermute(value, axis, pairs)  7.24 us
    unnamed x15, local copies, waits for them, and re-layouts  4.85 us
  transfers between devices with their start and end apart: 30, of which 9 were waited for; matrix products, arithmetic and copies ran while one was open for 9% of the time, Pallas kernels for 0%

commit v1 on v0

v1 whole, which is shorter than its diff:
```python
import functools
import math

import jax
import jax.numpy as jnp
from jax import lax
from jax.experimental import pallas as pl
from jax.experimental.pallas import tpu as pltpu
from jax.sharding import Mesh
from jax.sharding import PartitionSpec as P

LOG2E = math.log2(math.e)
STAT_ROWS = 32
VMEM_LIMIT = 48 * 1024 * 1024
BF16 = jnp.bfloat16
F32 = jnp.float32
VMEM = pl.BlockSpec(memory_space=pltpu.VMEM)


def peer(place, step, count):
    if count & (count - 1) == 0:
        return place ^ step
    return (place + count - step) % count


def fetch(value, axis, step):
    count = lax.axis_size(axis)
    return lax.ppermute(value, axis, [(peer(i, step, count), i) for i in range(count)])


def give_back(value, axis, step):
    count = lax.axis_size(axis)
    return lax.ppermute(value, axis, [(i, peer(i, step, count)) for i in range(count)])


def three_parts(value):
    high = value.astype(BF16).astype(F32)
    rest = value - high
    middle = rest.astype(BF16).astype(F32)
    return [high, middle, rest - middle]


def pack_kernel(heads, q_ref, g_ref, o_ref, lse_ref, start_ref, pack_ref):
    tok = q_ref.shape[0]
    width = q_ref.shape[1] // heads
    deltas = []
    for h in range(heads):
        cols = slice(h * width, (h + 1) * width)
        q, g = q_ref[:, cols], g_ref[:, cols]
        pack_ref[h * tok : (h + 1) * tok, :] = q
        pack_ref[(heads + h) * tok : (heads + h + 1) * tok, :] = g
        product = g.astype(F32) * o_ref[:, cols].astype(F32)
        deltas.append(jnp.sum(product.T, axis=0, keepdims=True))
    delta = jnp.concatenate(deltas, axis=0)
    starts = start_ref[...]
    rows = three_parts(lse_ref[...]) + three_parts(delta)
    rows += [(starts >> 8).astype(F32), (starts & 255).astype(F32)]
    used = 6 * heads + 2
    rows.append(jnp.zeros((STAT_ROWS - used, tok), F32))
    pack_ref[2 * heads * tok :, :] = jnp.concatenate(rows, axis=0).astype(BF16)


def pack(queries, d_out, outputs, lse, doc_start, heads):
    tok = queries.shape[0]
    width = queries.shape[1] // heads
    return pl.pallas_call(
        functools.partial(pack_kernel, heads),
        out_shape=jax.ShapeDtypeStruct((2 * heads * tok + STAT_ROWS, width), BF16),
        in_specs=[VMEM] * 5,
        out_specs=VMEM,
        name="pack",
    )(queries, d_out, outputs, lse.T, doc_start.reshape(1, tok))


def part_kernel(steps, first, last, heads, sizes, *refs):
    inner, zed = sizes
    packs, refs = refs[: len(steps)], refs[len(steps) :]
    mine, refs = refs[:zed], refs[zed:]
    others, refs = refs[:zed], refs[zed:]
    if first:
        acc = None
    else:
        acc, refs = refs[:2], refs[2:]
    dq_refs, refs = refs[: len(steps)], refs[len(steps) :]
    totals = refs
    me = lax.axis_index("inner")
    z_me = lax.axis_index("z")
    core = lax.axis_index("core")
    tok, width = mine[0].shape[0], mine[0].shape[1] // 2
    half = tok // 2
    band_len = inner * half
    outer = 2 * z_me + core
    scale = width**-0.5
    lane = lax.broadcasted_iota(jnp.int32, (1, tok), 1)
    row = lax.broadcasted_iota(jnp.int32, (tok, 1), 0)

    def position(index, source, member):
        band = jnp.where(index < half, source, 4 * zed - 1 - source)
        return band * band_len + member * half + index % half

    q_info = []
    for step, pack_ref in zip(steps, packs):
        stats = pack_ref[2 * heads * tok :, :].astype(F32)
        lse = stats[:heads] + stats[heads : 2 * heads] + stats[2 * heads : 3 * heads]
        delta = stats[3 * heads : 4 * heads] + stats[4 * heads : 5 * heads] + stats[5 * heads : 6 * heads]
        starts = stats[6 * heads : 6 * heads + 1] * 256.0 + stats[6 * heads + 1 : 6 * heads + 2]
        q_pos = position(lane, outer, peer(me, step, inner))
        q_info.append((lse * LOG2E, delta, starts.astype(jnp.int32), q_pos))

    dq_t = [None] * len(steps)
    chunk = 4 if zed % 4 == 0 else 1
    for side, blocks in enumerate((mine, others)):
        for c0 in range(0, zed, chunk):
            group = blocks[c0 : c0 + chunk]
            keys = jnp.concatenate([b[:, :width] for b in group], axis=0)
            values = jnp.concatenate([b[:, width:] for b in group], axis=0)
            keys_t = keys.T
            k_pos = jnp.concatenate(
                [
                    position(row, 2 * peer(z_me, c0 + j, zed) + (core if side == 0 else 1 - core), me)
                    for j in range(chunk)
                ],
                axis=0,
            )
            dk_sum, dv_sum = None, None
            for n, pack_ref in enumerate(packs):
                lse, delta, starts, q_pos = q_info[n]
                mask = jnp.logical_and(k_pos <= q_pos, k_pos >= starts)
                probs, dscores = [], []
                for h in range(heads):
                    q = pack_ref[h * tok : (h + 1) * tok, :]
                    g = pack_ref[(heads + h) * tok : (heads + h + 1) * tok, :]
                    nt = (((1,), (1,)), ((), ()))
                    s = lax.dot_general(keys, q, nt, preferred_element_type=F32)
                    dp = lax.dot_general(values, g, nt, preferred_element_type=F32)
                    p = jnp.where(mask, jnp.exp2(s * (scale * LOG2E) - lse[h : h + 1]), 0.0)
                    ds = p * (dp - delta[h : h + 1])
                    probs.append(p.astype(BF16))
                    dscores.append(ds.astype(BF16))
                prob = jnp.concatenate(probs, axis=1)
                dscore = jnp.concatenate(dscores, axis=1)
                dv = jnp.dot(prob, pack_ref[heads * tok : 2 * heads * tok, :], preferred_element_type=F32)
                dk = jnp.dot(dscore, pack_ref[: heads * tok, :], preferred_element_type=F32)
                dq = jnp.dot(keys_t, dscore, preferred_element_type=F32)
                dq_t[n] = dq if dq_t[n] is None else dq_t[n] + dq
                dk_sum = dk if dk_sum is None else dk_sum + dk
                dv_sum = dv if dv_sum is None else dv_sum + dv
            here = slice(c0 * tok, (c0 + chunk) * tok)
            dk_sum = dk_sum * scale
            if not first:
                dk_sum = dk_sum + acc[side][here, :width]
                dv_sum = dv_sum + acc[side][here, width:]
            totals[side][here, :width] = dk_sum.astype(totals[side].dtype)
            totals[side][here, width:] = dv_sum.astype(totals[side].dtype)
    for n, dq_ref in enumerate(dq_refs):
        for h in range(heads):
            block = dq_t[n][:, h * tok : (h + 1) * tok] * scale
            dq_ref[:, h * width : (h + 1) * width] = block.T.astype(dq_ref.dtype)


def part(steps, packs, mine, others, acc, last, heads, sizes):
    tok, two = mine[0].shape
    width = two // 2
    zed = sizes[1]
    dq_types = [F32 if s == 0 else BF16 for s in steps]
    outs = [jax.ShapeDtypeStruct((tok, heads * width), t) for t in dq_types]
    outs += [jax.ShapeDtypeStruct((zed * tok, two), F32), jax.ShapeDtypeStruct((zed * tok, two), BF16 if last else F32)]
    args = list(packs) + list(mine) + list(others) + list(acc or [])
    elements = len(steps) * heads * tok * 2 * zed * tok
    result = pl.pallas_call(
        functools.partial(part_kernel, steps, acc is None, last, heads, sizes),
        out_shape=outs,
        in_specs=[VMEM] * len(args),
        out_specs=[VMEM] * len(outs),
        compiler_params=pltpu.CompilerParams(vmem_limit_bytes=VMEM_LIMIT),
        cost_estimate=pl.CostEstimate(flops=elements * width * 10, bytes_accessed=1 << 20, transcendentals=elements),
        name="part",
    )(*args)
    return result[: len(steps)], result[len(steps) :]


def join_kernel(kept_ref, other_ref, *outs):
    tok = outs[0].shape[0]
    for s, out in enumerate(outs):
        here = slice(s * tok, (s + 1) * tok)
        out[...] = (kept_ref[here, :] + other_ref[here, :].astype(F32)).astype(out.dtype)


def join(kept, other, zed):
    tok, two = kept.shape[0] // zed, kept.shape[1]
    outs = [jax.ShapeDtypeStruct((tok, two), F32 if s == 0 else BF16) for s in range(zed)]
    return pl.pallas_call(
        join_kernel, out_shape=outs, in_specs=[VMEM] * 2, out_specs=[VMEM] * zed, name="join"
    )(kept, other)


def total_kernel(*refs):
    out = refs[-1]
    total = refs[0][...]
    for ref in refs[1:-1]:
        total = total + ref[...].astype(F32)
    out[...] = total.astype(out.dtype)


def total(values):
    return pl.pallas_call(
        total_kernel,
        out_shape=jax.ShapeDtypeStruct(values[0].shape, BF16),
        in_specs=[VMEM] * len(values),
        out_specs=VMEM,
        name="total",
    )(*values)


def on_device(queries, keys_values, outputs, d_out, lse, doc_start):
    inner = lax.axis_size("inner")
    zed = lax.axis_size("z")
    heads = lse.shape[1]
    sizes = (inner, zed)
    own = pack(queries, d_out, outputs, lse, doc_start, heads)
    packs = [own] + [fetch(own, "inner", s) for s in range(1, inner)]
    mine = [keys_values] + [fetch(keys_values, "z", s) for s in range(1, zed)]
    others = [fetch(kv, "core", 1) for kv in mine]
    groups = [[s] for s in range(inner)]
    acc = None
    dqs = []
    for steps in groups:
        got, acc = part(steps, [packs[s] for s in steps], mine, others, acc, steps is groups[-1], heads, sizes)
        dqs += got
    dq_home = [dqs[0]] + [give_back(dqs[s], "inner", s) for s in range(1, inner)]
    kept, sent = acc
    joined = join(kept, fetch(sent, "core", 1), zed)
    dkv_home = [joined[0]] + [give_back(joined[s], "z", s) for s in range(1, zed)]
    return (total(dq_home), total(dkv_home))


def solution(mesh):
    inner, outer = mesh.shape["inner"], mesh.shape["outer"]
    split = Mesh(mesh.devices.reshape(inner, outer // 2, 2), ("inner", "z", "core"))
    rows = P(("inner", "z", "core"), None)
    return jax.shard_map(
        on_device,
        mesh=split,
        in_specs=(rows, rows, rows, rows, rows, P(("inner", "z", "core"))),
        out_specs=(rows, rows),
        check_vma=False,
    )
```

time: 144 us -> 45.2 us (0.31)
  waiting for transfers between devices: 88.4 us -> 6.78 us
  Pallas kernels: 0 us -> 13.9 us
  between operations: 14.2 us -> 0.74 us
  starting transfers between devices: 7.27 us -> 19.1 us
  blocking collectives: 10.9 us -> 0 us
  matrix products: 9.52 us -> 0 us
  other arithmetic: 4.02 us -> 0 us
  local copies, waits for them, and re-layouts: 8.18 us -> 4.48 us
  loops' own time: 1.44 us -> 0 us
    ppermute x29 -> x17, waiting for transfers between devices: 72.5 us -> 6.78 us  [the longest x11 5.23 us: fetch(): lax.ppermute(value, axis, [(peer(i, step, count), i) for i in range(count)])]
    reduce_scatter x1 -> x0, waiting for transfers between devices: 15.8 us -> none  [on_device(): lax.psum_scatter(collected, 'inner', scatter_dimension=0, tiled=True)]
    pallas_call x0 -> x8, Pallas kernels: none -> 13.9 us  [the longest x4 6.66 us: part(): pl.pallas_call(functools.partial(part_kernel, steps, acc is None, last, h...]
    ppermute x29 -> x17, starting transfers between devices: 7.24 us -> 19.1 us  [the longest x11 11.2 us: fetch(): lax.ppermute(value, axis, [(peer(i, step, count), i) for i in range(count)])]
    all_gather x1 -> x0, blocking collectives: 10.9 us -> none  [on_device(): gathered = lax.all_gather(keys_values, 'inner', axis=0, tiled=True)]
    dot_general x40 -> x0, matrix products: 9.52 us -> none  [the longest x8 2.05 us: block_grads(): jnp.einsum('qhd,kd->hqk', query_part, key_part, preferred_element_type=jn...]
    convert_element_type x1 -> x0, other arithmetic: 1.54 us -> none  [on_device(): return (query_total.astype(jnp.bfloat16), own_pairs.astype(jnp.bfloat16))]
    unnamed x15 -> x22, local copies, waits for them, and re-layouts: 4.85 us -> 4.48 us
  transfers between devices with their start and end apart: 30 -> 17, of which waited for: 9 -> 6; matrix products, arithmetic and copies ran while one was open for 9% -> 0% of each run, Pallas kernels for 0% -> 19%
where the time goes in v1:
time: 45.2 us; the launch traced here: 45 us
  starting transfers between devices  19.1 us (42%)
  Pallas kernels  13.9 us (31%)
  waiting for transfers between devices  6.78 us (15%)
  local copies, waits for them, and re-layouts  4.48 us (10%)
  between operations  0.74 us (2%)
    ppermute x11, starting transfers between devices, fetch(): lax.ppermute(value, axis, [(peer(i, step, count), i) for i in range(count)])  11.2 us
    ppermute x6, starting transfers between devices, give_back(): lax.ppermute(value, axis, [(i, peer(i, step, count)) for i in range(count)])  7.88 us
    pallas_call x4, Pallas kernels, part(): pl.pallas_call(functools.partial(part_kernel, steps, acc is None, last, h...  6.66 us
    ppermute x11, waiting for transfers between devices, fetch(): lax.ppermute(value, axis, [(peer(i, step, count), i) for i in range(count)])  5.23 us
    unnamed x22, local copies, waits for them, and re-layouts  4.48 us
    pallas_call x2, Pallas kernels, total(): pl.pallas_call(total_kernel, out_shape=jax.ShapeDtypeStruct(values[0].sha...  3.46 us
    pallas_call x1, Pallas kernels, pack(): pl.pallas_call(functools.partial(pack_kernel, heads), out_shape=jax.Shape...  1.94 us
    pallas_call x1, Pallas kernels, join(): pl.pallas_call(join_kernel, out_shape=outs, in_specs=[VMEM] * 2, out_spec...  1.83 us
  transfers between devices with their start and end apart: 17, of which 6 were waited for; matrix products, arithmetic and copies ran while one was open for 0% of the time, Pallas kernels for 19%

profile of v1, /device:TPU:0, one launch (start us, length us, event | category | flops | bytes accessed | tf_op | source)
XLA Modules:
  0.0 45.0 jit_solution(18366747101477686235)
XLA Ops:
  0.6 1.9 %pack.1.refs_0_ = bf16[1056,128]{1,0:T(8,128)(2,1)} custom-call(bf16[128,512]{1,0:T(8,128)(2,1)} %q_ref.1, bf16[128,512]{1,0:T(8,128)(2,1)} %g_ref.1, bf16[128,512]{1,0:T(8,128)(2,1)} %o_ref.1, f32[4,128]{1,0:T(4,128)} %bitcast.2, s32[1,128]{1,0:T(1,128)} %bitcast.3), custom_call_target="tpu_custom_call" | custom-call | tf_op jit(solution)/shard_map/pack/pallas_call | solution.py:66
  2.6 2.9 %collective-permute-start.7 = (bf16[1056,128]{1,0:T(8,128)(2,1)}, bf16[1056,128]{1,0:T(8,128)(2,1)S(1)}, u32[]{:S(2)}, u32[]{:S(2)}) collective-permute-start(bf16[1056,128]{1,0:T(8,128)(2,1)} %pack.1.refs_0_), channel_id=1, source_target_pairs={{8,0},{0,8},{24,16},{16,24},{9,1},{1,9},{25,17},{17,25},{10,2},{2,... | collective-permute-start | bytes 811016 | tf_op jit(solution)/shard_map/ppermute | solution.py:28
  5.5 1.6 %collective-permute-start = (bf16[128,256]{1,0:T(8,128)(2,1)S(1)}, bf16[128,256]{1,0:T(8,128)(2,1)S(1)}, u32[]{:S(2)}, u32[]{:S(2)}) collective-permute-start(bf16[128,256]{1,0:T(8,128)(2,1)S(1)} %copy-done.3), channel_id=1, source_target_pairs={{2,0},{0,2},{6,4},{4,6},{3,1},{1,3},{7,5},{5,7},{10,8},{8,10},{14,... | collective-permute-start | bytes 196616 | tf_op jit(solution)/shard_map/ppermute | solution.py:28
  7.1 2.6 %collective-permute-start.1 = (bf16[128,256]{1,0:T(8,128)(2,1)S(1)}, bf16[128,256]{1,0:T(8,128)(2,1)S(1)}, u32[]{:S(2)}, u32[]{:S(2)}) collective-permute-start(bf16[128,256]{1,0:T(8,128)(2,1)S(1)} %copy-done.3), channel_id=1, source_target_pairs={{4,0},{6,2},{0,4},{2,6},{5,1},{7,3},{1,5},{3,7},{12,8},{14,10},{8,... | collective-permute-start | bytes 196616 | tf_op jit(solution)/shard_map/ppermute | solution.py:28
  9.9 1.5 %collective-permute-start.9 = (bf16[1056,128]{1,0:T(8,128)(2,1)}, bf16[1056,128]{1,0:T(8,128)(2,1)S(1)}, u32[]{:S(2)}, u32[]{:S(2)}) collective-permute-start(bf16[1056,128]{1,0:T(8,128)(2,1)} %pack.1.refs_0_), channel_id=1, source_target_pairs={{16,0},{24,8},{0,16},{8,24},{17,1},{25,9},{1,17},{9,25},{18,2},{26... | collective-permute-start | bytes 811016 | tf_op jit(solution)/shard_map/ppermute | solution.py:28
  11.4 2.6 %collective-permute-done.1.refs_3_ = bf16[128,256]{1,0:T(8,128)(2,1)S(1)} collective-permute-done((bf16[128,256]{1,0:T(8,128)(2,1)S(1)}, bf16[128,256]{1,0:T(8,128)(2,1)S(1)}, u32[]{:S(2)}, u32[]{:S(2)}) %collective-permute-start.1) | collective-permute-done | bytes 65568 | tf_op jit(solution)/shard_map/ppermute | solution.py:28
  14.1 1.7 %collective-permute-done.2.refs_4_ = bf16[128,256]{1,0:T(8,128)(2,1)S(1)} collective-permute-done((bf16[128,256]{1,0:T(8,128)(2,1)S(1)}, bf16[128,256]{1,0:T(8,128)(2,1)S(1)}, u32[]{:S(2)}, u32[]{:S(2)}) %collective-permute-start.2) | collective-permute-done | bytes 65568 | tf_op jit(solution)/shard_map/ppermute | solution.py:28
  15.7 1.5 %collective-permute-start.11 = (bf16[1056,128]{1,0:T(8,128)(2,1)}, bf16[1056,128]{1,0:T(8,128)(2,1)S(1)}, u32[]{:S(2)}, u32[]{:S(2)}) collective-permute-start(bf16[1056,128]{1,0:T(8,128)(2,1)} %pack.1.refs_0_), channel_id=1, source_target_pairs={{24,0},{16,8},{8,16},{0,24},{25,1},{17,9},{9,17},{1,25},{26,2},{18... | collective-permute-start | bytes 811016 | tf_op jit(solution)/shard_map/ppermute | solution.py:28
  17.8 0.7 %collective-permute-done.5.refs_7_ = bf16[128,256]{1,0:T(8,128)(2,1)S(1)} collective-permute-done((bf16[128,256]{1,0:T(8,128)(2,1)S(1)}, bf16[128,256]{1,0:T(8,128)(2,1)S(1)}, u32[]{:S(2)}, u32[]{:S(2)}) %collective-permute-start.5) | collective-permute-done | bytes 65568 | tf_op jit(solution)/shard_map/ppermute | solution.py:28
  18.7 1.0 %copy-done.1 = bf16[1056,128]{1,0:T(8,128)(2,1)S(1)} copy-done((bf16[1056,128]{1,0:T(8,128)(2,1)S(1)}, bf16[1056,128]{1,0:T(8,128)(2,1)}, u32[]{:S(2)}) %copy-start.1) | copy-done | bytes 270360
  19.6 1.6 %part.4 = (f32[128,512]{1,0:T(8,128)S(1)}, f32[512,256]{1,0:T(8,128)S(1)}, f32[512,256]{1,0:T(8,128)S(1)}) custom-call(bf16[1056,128]{1,0:T(8,128)(2,1)S(1)} %copy-done.1, bf16[128,256]{1,0:T(8,128)(2,1)S(1)} %copy-done.3, bf16[128,256]{1,0:T(8,128)(2,1)S(1)} %collective-permute-done.refs_2_, bf16[128,256]{1,0:T(8,128)(2,1)S(1)} %collective-permute-done.1.refs_3_, ...), custom_call_target="tpu_custom_call" | custom-call | flops 671088640 | bytes 1048576 | tf_op jit(solution)/shard_map/part/pallas_call | solution.py:170
  21.9 1.7 %part.5 = (bf16[128,512]{1,0:T(8,128)(2,1)S(1)}, f32[512,256]{1,0:T(8,128)S(1)}, f32[512,256]{1,0:T(8,128)S(1)}) custom-call(bf16[1056,128]{1,0:T(8,128)(2,1)S(1)} %collective-permute-done.7.refs_0_, bf16[128,256]{1,0:T(8,128)(2,1)S(1)} %copy-done.3, bf16[128,256]{1,0:T(8,128)(2,1)S(1)} %collective-permute-done.refs_2_, ...), custom_call_target="tpu_custom_call" | custom-call | flops 671088640 | bytes 1048576 | tf_op jit(solution)/shard_map/part/pallas_call | solution.py:170
  23.6 1.7 %part.6 = (bf16[128,512]{1,0:T(8,128)(2,1)S(1)}, f32[512,256]{1,0:T(8,128)S(1)}, f32[512,256]{1,0:T(8,128)S(1)}) custom-call(bf16[1056,128]{1,0:T(8,128)(2,1)S(1)} %collective-permute-done.9.refs_0_, bf16[128,256]{1,0:T(8,128)(2,1)S(1)} %copy-done.3, bf16[128,256]{1,0:T(8,128)(2,1)S(1)} %collective-permute-done.refs_2_, ...), custom_call_target="tpu_custom_call" | custom-call | flops 671088640 | bytes 1048576 | tf_op jit(solution)/shard_map/part/pallas_call | solution.py:170
  25.3 1.7 %part.7 = (bf16[128,512]{1,0:T(8,128)(2,1)S(1)}, f32[512,256]{1,0:T(8,128)S(1)}, bf16[512,256]{1,0:T(8,128)(2,1)S(1)}) custom-call(bf16[1056,128]{1,0:T(8,128)(2,1)S(1)} %collective-permute-done.11.refs_0_, bf16[128,256]{1,0:T(8,128)(2,1)S(1)} %copy-done.3, bf16[128,256]{1,0:T(8,128)(2,1)S(1)} %collective-permute-done.refs_2_, ...), custom_call_target="tpu_custom_call" | custom-call | flops 671088640 | bytes 1048576 | tf_op jit(solution)/shard_map/part/pallas_call | solution.py:170
  27.0 0.8 %copy-done = f32[512,256]{1,0:T(8,128)} copy-done((f32[512,256]{1,0:T(8,128)}, f32[512,256]{1,0:T(8,128)S(1)}, u32[]{:S(2)}) %copy-start) | copy-done | bytes 524312
  28.2 1.5 %collective-permute-start.8 = (bf16[128,512]{1,0:T(8,128)(2,1)S(1)}, bf16[128,512]{1,0:T(8,128)(2,1)S(1)}, u32[]{:S(2)}, u32[]{:S(2)}) collective-permute-start(bf16[128,512]{1,0:T(8,128)(2,1)S(1)} %get-tuple-element.21), channel_id=1, source_target_pairs={{0,8},{8,0},{16,24},{24,16},{1,9},{9,1},{17,25},{25,17},{2,10},{10... | collective-permute-start | bytes 393224 | tf_op jit(solution)/shard_map/ppermute | solution.py:33
  30.2 1.5 %collective-permute-start.12 = (bf16[128,512]{1,0:T(8,128)(2,1)S(1)}, bf16[128,512]{1,0:T(8,128)(2,1)S(1)}, u32[]{:S(2)}, u32[]{:S(2)}) collective-permute-start(bf16[128,512]{1,0:T(8,128)(2,1)S(1)} %get-tuple-element.27), channel_id=1, source_target_pairs={{0,24},{8,16},{16,8},{24,0},{1,25},{9,17},{17,9},{25,1},{2,26},{10... | collective-permute-start | bytes 393224 | tf_op jit(solution)/shard_map/ppermute | solution.py:33
  32.4 1.8 %join.1 = (f32[128,256]{1,0:T(8,128)}, bf16[128,256]{1,0:T(8,128)(2,1)}, bf16[128,256]{1,0:T(8,128)(2,1)}, bf16[128,256]{1,0:T(8,128)(2,1)}) custom-call(f32[512,256]{1,0:T(8,128)} %copy-done, bf16[512,256]{1,0:T(8,128)(2,1)} %copy-done.4), custom_call_target="tpu_custom_call" | custom-call | tf_op jit(solution)/shard_map/join/pallas_call | solution.py:192
  34.2 2.1 %collective-permute-start.15 = (bf16[128,256]{1,0:T(8,128)(2,1)}, bf16[128,256]{1,0:T(8,128)(2,1)S(1)}, u32[]{:S(2)}, u32[]{:S(2)}) collective-permute-start(bf16[128,256]{1,0:T(8,128)(2,1)} %get-tuple-element.32), channel_id=1, source_target_pairs={{0,4},{2,6},{4,0},{6,2},{1,5},{3,7},{5,1},{7,3},{8,12},{10,14},{12... | collective-permute-start | bytes 196616 | tf_op jit(solution)/shard_map/ppermute | solution.py:33
  36.4 2.3 %collective-permute-start.16 = (bf16[128,256]{1,0:T(8,128)(2,1)}, bf16[128,256]{1,0:T(8,128)(2,1)S(1)}, u32[]{:S(2)}, u32[]{:S(2)}) collective-permute-start(bf16[128,256]{1,0:T(8,128)(2,1)} %get-tuple-element.33), channel_id=1, source_target_pairs={{0,6},{2,4},{4,2},{6,0},{1,7},{3,5},{5,3},{7,1},{8,14},{10,12},{12... | collective-permute-start | bytes 196616 | tf_op jit(solution)/shard_map/ppermute | solution.py:33
  39.3 1.8 %total.2 = bf16[128,512]{1,0:T(8,128)(2,1)} custom-call(f32[128,512]{1,0:T(8,128)} %copy-done.2, bf16[128,512]{1,0:T(8,128)(2,1)} %copy-done.5, bf16[128,512]{1,0:T(8,128)(2,1)} %copy-done.6, bf16[128,512]{1,0:T(8,128)(2,1)} %copy-done.7), custom_call_target="tpu_custom_call" | custom-call | tf_op jit(solution)/shard_map/total/pallas_call | solution.py:206
  41.2 0.8 %collective-permute-done.15.refs_2_ = bf16[128,256]{1,0:T(8,128)(2,1)S(1)} collective-permute-done((bf16[128,256]{1,0:T(8,128)(2,1)}, bf16[128,256]{1,0:T(8,128)(2,1)S(1)}, u32[]{:S(2)}, u32[]{:S(2)}) %collective-permute-start.15) | collective-permute-done | bytes 65568 | tf_op jit(solution)/shard_map/ppermute | solution.py:33
  42.0 0.8 %collective-permute-done.16.refs_3_ = bf16[128,256]{1,0:T(8,128)(2,1)S(1)} collective-permute-done((bf16[128,256]{1,0:T(8,128)(2,1)}, bf16[128,256]{1,0:T(8,128)(2,1)S(1)}, u32[]{:S(2)}, u32[]{:S(2)}) %collective-permute-start.16) | collective-permute-done | bytes 65568 | tf_op jit(solution)/shard_map/ppermute | solution.py:33
  43.3 1.6 %total.3 = bf16[128,256]{1,0:T(8,128)(2,1)} custom-call(f32[128,256]{1,0:T(8,128)} %get-tuple-element.30.refs_0_, bf16[128,256]{1,0:T(8,128)(2,1)} %copy-done.8, bf16[128,256]{1,0:T(8,128)(2,1)} %copy-done.9, bf16[128,256]{1,0:T(8,128)(2,1)} %copy-done.10), custom_call_target="tpu_custom_call" | custom-call | tf_op jit(solution)/shard_map/total/pallas_call | solution.py:206
  (40 shorter events, 4.5 us)
Async XLA Ops:
  0.6 4.9 %copy-start.3 = (bf16[128,256]{1,0:T(8,128)(2,1)S(1)}, bf16[128,256]{1,0:T(8,128)(2,1)}, u32[]{:S(2)}) copy-start(bf16[128,256]{1,0:T(8,128)(2,1)} %refs_1_.7) | copy-start | bytes 196612
  2.6 19.4 %collective-permute-start.7 = (bf16[1056,128]{1,0:T(8,128)(2,1)}, bf16[1056,128]{1,0:T(8,128)(2,1)S(1)}, u32[]{:S(2)}, u32[]{:S(2)}) collective-permute-start(bf16[1056,128]{1,0:T(8,128)(2,1)} %pack.1.refs_0_), channel_id=1, source_target_pairs={{8,0},{0,8},{24,16},{16,24},{9,1},{1,9},{25,17},{17,25},{10,2},{2,... | collective-permute-start | bytes 811016 | tf_op jit(solution)/shard_map/ppermute | solution.py:28
  5.5 5.9 %collective-permute-start = (bf16[128,256]{1,0:T(8,128)(2,1)S(1)}, bf16[128,256]{1,0:T(8,128)(2,1)S(1)}, u32[]{:S(2)}, u32[]{:S(2)}) collective-permute-start(bf16[128,256]{1,0:T(8,128)(2,1)S(1)} %copy-done.3), channel_id=1, source_target_pairs={{2,0},{0,2},{6,4},{4,6},{3,1},{1,3},{7,5},{5,7},{10,8},{8,10},{14,... | collective-permute-start | bytes 196616 | tf_op jit(solution)/shard_map/ppermute | solution.py:28
  7.1 7.0 %collective-permute-start.1 = (bf16[128,256]{1,0:T(8,128)(2,1)S(1)}, bf16[128,256]{1,0:T(8,128)(2,1)S(1)}, u32[]{:S(2)}, u32[]{:S(2)}) collective-permute-start(bf16[128,256]{1,0:T(8,128)(2,1)S(1)} %copy-done.3), channel_id=1, source_target_pairs={{4,0},{6,2},{0,4},{2,6},{5,1},{7,3},{1,5},{3,7},{12,8},{14,10},{8,... | collective-permute-start | bytes 196616 | tf_op jit(solution)/shard_map/ppermute | solution.py:28
  9.7 6.1 %collective-permute-start.2 = (bf16[128,256]{1,0:T(8,128)(2,1)S(1)}, bf16[128,256]{1,0:T(8,128)(2,1)S(1)}, u32[]{:S(2)}, u32[]{:S(2)}) collective-permute-start(bf16[128,256]{1,0:T(8,128)(2,1)S(1)} %copy-done.3), channel_id=1, source_target_pairs={{6,0},{4,2},{2,4},{0,6},{7,1},{5,3},{3,5},{1,7},{14,8},{12,10},{10... | collective-permute-start | bytes 196616 | tf_op jit(solution)/shard_map/ppermute | solution.py:28
  9.9 13.7 %collective-permute-start.9 = (bf16[1056,128]{1,0:T(8,128)(2,1)}, bf16[1056,128]{1,0:T(8,128)(2,1)S(1)}, u32[]{:S(2)}, u32[]{:S(2)}) collective-permute-start(bf16[1056,128]{1,0:T(8,128)(2,1)} %pack.1.refs_0_), channel_id=1, source_target_pairs={{16,0},{24,8},{0,16},{8,24},{17,1},{25,9},{1,17},{9,25},{18,2},{26... | collective-permute-start | bytes 811016 | tf_op jit(solution)/shard_map/ppermute | solution.py:28
  11.4 5.8 %collective-permute-start.3 = (bf16[128,256]{1,0:T(8,128)(2,1)S(1)}, bf16[128,256]{1,0:T(8,128)(2,1)S(1)}, u32[]{:S(2)}, u32[]{:S(2)}) collective-permute-start(bf16[128,256]{1,0:T(8,128)(2,1)S(1)} %copy-done.3), channel_id=1, source_target_pairs={{1,0},{0,1},{3,2},{2,3},{5,4},{4,5},{7,6},{6,7},{9,8},{8,9},{11,10... | collective-permute-start | bytes 196616 | tf_op jit(solution)/shard_map/ppermute | solution.py:28
  14.1 3.2 %collective-permute-start.4 = (bf16[128,256]{1,0:T(8,128)(2,1)S(1)}, bf16[128,256]{1,0:T(8,128)(2,1)S(1)}, u32[]{:S(2)}, u32[]{:S(2)}) collective-permute-start(bf16[128,256]{1,0:T(8,128)(2,1)S(1)} %collective-permute-done.refs_2_), channel_id=1, source_target_pairs={{1,0},{0,1},{3,2},{2,3},{5,4},{4,5},{7,6},{6,7},{9,8},{8,9},{11,10... | collective-permute-start | bytes 196616 | tf_op jit(solution)/shard_map/ppermute | solution.py:28
  15.7 9.6 %collective-permute-start.11 = (bf16[1056,128]{1,0:T(8,128)(2,1)}, bf16[1056,128]{1,0:T(8,128)(2,1)S(1)}, u32[]{:S(2)}, u32[]{:S(2)}) collective-permute-start(bf16[1056,128]{1,0:T(8,128)(2,1)} %pack.1.refs_0_), channel_id=1, source_target_pairs={{24,0},{16,8},{8,16},{0,24},{25,1},{17,9},{9,17},{1,25},{26,2},{18... | collective-permute-start | bytes 811016 | tf_op jit(solution)/shard_map/ppermute | solution.py:28
  17.2 1.3 %collective-permute-start.5 = (bf16[128,256]{1,0:T(8,128)(2,1)S(1)}, bf16[128,256]{1,0:T(8,128)(2,1)S(1)}, u32[]{:S(2)}, u32[]{:S(2)}) collective-permute-start(bf16[128,256]{1,0:T(8,128)(2,1)S(1)} %collective-permute-done.1.refs_3_), channel_id=1, source_target_pairs={{1,0},{0,1},{3,2},{2,3},{5,4},{4,5},{7,6},{6,7},{9,8},{8,9},{11,10... | collective-permute-start | bytes 196616 | tf_op jit(solution)/shard_map/ppermute | solution.py:28
  17.3 1.4 %collective-permute-start.6 = (bf16[128,256]{1,0:T(8,128)(2,1)S(1)}, bf16[128,256]{1,0:T(8,128)(2,1)S(1)}, u32[]{:S(2)}, u32[]{:S(2)}) collective-permute-start(bf16[128,256]{1,0:T(8,128)(2,1)S(1)} %collective-permute-done.2.refs_4_), channel_id=1, source_target_pairs={{1,0},{0,1},{3,2},{2,3},{5,4},{4,5},{7,6},{6,7},{9,8},{8,9},{11,10... | collective-permute-start | bytes 196616 | tf_op jit(solution)/shard_map/ppermute | solution.py:28
  18.7 1.0 %copy-start.1 = (bf16[1056,128]{1,0:T(8,128)(2,1)S(1)}, bf16[1056,128]{1,0:T(8,128)(2,1)}, u32[]{:S(2)}) copy-start(bf16[1056,128]{1,0:T(8,128)(2,1)} %pack.1.refs_0_) | copy-start | bytes 811012
  27.0 0.8 %copy-start = (f32[512,256]{1,0:T(8,128)}, f32[512,256]{1,0:T(8,128)S(1)}, u32[]{:S(2)}) copy-start(f32[512,256]{1,0:T(8,128)S(1)} %get-tuple-element.28.kept_ref) | copy-start | bytes 1572868
  27.8 3.9 %collective-permute-start.13 = (bf16[512,256]{1,0:T(8,128)(2,1)S(1)}, bf16[512,256]{1,0:T(8,128)(2,1)S(1)}, u32[]{:S(2)}, u32[]{:S(2)}) collective-permute-start(bf16[512,256]{1,0:T(8,128)(2,1)S(1)} %get-tuple-element.29), channel_id=1, source_target_pairs={{1,0},{0,1},{3,2},{2,3},{5,4},{4,5},{7,6},{6,7},{9,8},{8,9},{11,10... | collective-permute-start | bytes 786440 | tf_op jit(solution)/shard_map/ppermute | solution.py:28
  28.2 8.2 %collective-permute-start.8 = (bf16[128,512]{1,0:T(8,128)(2,1)S(1)}, bf16[128,512]{1,0:T(8,128)(2,1)S(1)}, u32[]{:S(2)}, u32[]{:S(2)}) collective-permute-start(bf16[128,512]{1,0:T(8,128)(2,1)S(1)} %get-tuple-element.21), channel_id=1, source_target_pairs={{0,8},{8,0},{16,24},{24,16},{1,9},{9,1},{17,25},{25,17},{2,10},{10... | collective-permute-start | bytes 393224 | tf_op jit(solution)/shard_map/ppermute | solution.py:33
  29.7 9.0 %collective-permute-start.10 = (bf16[128,512]{1,0:T(8,128)(2,1)S(1)}, bf16[128,512]{1,0:T(8,128)(2,1)S(1)}, u32[]{:S(2)}, u32[]{:S(2)}) collective-permute-start(bf16[128,512]{1,0:T(8,128)(2,1)S(1)} %get-tuple-element.24), channel_id=1, source_target_pairs={{0,16},{8,24},{16,0},{24,8},{1,17},{9,25},{17,1},{25,9},{2,18},{10... | collective-permute-start | bytes 393224 | tf_op jit(solution)/shard_map/ppermute | solution.py:33
  30.2 8.4 %collective-permute-start.12 = (bf16[128,512]{1,0:T(8,128)(2,1)S(1)}, bf16[128,512]{1,0:T(8,128)(2,1)S(1)}, u32[]{:S(2)}, u32[]{:S(2)}) collective-permute-start(bf16[128,512]{1,0:T(8,128)(2,1)S(1)} %get-tuple-element.27), channel_id=1, source_target_pairs={{0,24},{8,16},{16,8},{24,0},{1,25},{9,17},{17,9},{25,1},{2,26},{10... | collective-permute-start | bytes 393224 | tf_op jit(solution)/shard_map/ppermute | solution.py:33
  31.7 0.7 %copy-start.4 = (bf16[512,256]{1,0:T(8,128)(2,1)}, bf16[512,256]{1,0:T(8,128)(2,1)S(1)}, u32[]{:S(2)}) copy-start(bf16[512,256]{1,0:T(8,128)(2,1)S(1)} %collective-permute-done.13.other_ref) | copy-start | bytes 786436
  34.2 6.9 %collective-permute-start.14 = (bf16[128,256]{1,0:T(8,128)(2,1)}, bf16[128,256]{1,0:T(8,128)(2,1)S(1)}, u32[]{:S(2)}, u32[]{:S(2)}) collective-permute-start(bf16[128,256]{1,0:T(8,128)(2,1)} %get-tuple-element.31), channel_id=1, source_target_pairs={{0,2},{2,0},{4,6},{6,4},{1,3},{3,1},{5,7},{7,5},{8,10},{10,8},{12,... | collective-permute-start | bytes 196616 | tf_op jit(solution)/shard_map/ppermute | solution.py:33
  34.2 7.7 %collective-permute-start.15 = (bf16[128,256]{1,0:T(8,128)(2,1)}, bf16[128,256]{1,0:T(8,128)(2,1)S(1)}, u32[]{:S(2)}, u32[]{:S(2)}) collective-permute-start(bf16[128,256]{1,0:T(8,128)(2,1)} %get-tuple-element.32), channel_id=1, source_target_pairs={{0,4},{2,6},{4,0},{6,2},{1,5},{3,7},{5,1},{7,3},{8,12},{10,14},{12... | collective-permute-start | bytes 196616 | tf_op jit(solution)/shard_map/ppermute | solution.py:33
  36.4 2.3 %copy-start.5 = (bf16[128,512]{1,0:T(8,128)(2,1)}, bf16[128,512]{1,0:T(8,128)(2,1)S(1)}, u32[]{:S(2)}) copy-start(bf16[128,512]{1,0:T(8,128)(2,1)S(1)} %collective-permute-done.8.refs_1_) | copy-start | bytes 393220
  36.4 6.3 %collective-permute-start.16 = (bf16[128,256]{1,0:T(8,128)(2,1)}, bf16[128,256]{1,0:T(8,128)(2,1)S(1)}, u32[]{:S(2)}, u32[]{:S(2)}) collective-permute-start(bf16[128,256]{1,0:T(8,128)(2,1)} %get-tuple-element.33), channel_id=1, source_target_pairs={{0,6},{2,4},{4,2},{6,0},{1,7},{3,5},{5,3},{7,1},{8,14},{10,12},{12... | collective-permute-start | bytes 196616 | tf_op jit(solution)/shard_map/ppermute | solution.py:33
  41.2 1.5 %copy-start.8 = (bf16[128,256]{1,0:T(8,128)(2,1)}, bf16[128,256]{1,0:T(8,128)(2,1)S(1)}, u32[]{:S(2)}) copy-start(bf16[128,256]{1,0:T(8,128)(2,1)S(1)} %collective-permute-done.14.refs_1_) | copy-start | bytes 196612
  42.0 0.8 %copy-start.9 = (bf16[128,256]{1,0:T(8,128)(2,1)}, bf16[128,256]{1,0:T(8,128)(2,1)S(1)}, u32[]{:S(2)}) copy-start(bf16[128,256]{1,0:T(8,128)(2,1)S(1)} %collective-permute-done.15.refs_2_) | copy-start | bytes 196612
  (4 other events, 2.7 us)

commit v2 on v1

v2 whole, which is shorter than its diff:
```python
import functools
import math

import jax
import jax.numpy as jnp
from jax import lax
from jax.experimental import pallas as pl
from jax.experimental.pallas import tpu as pltpu
from jax.sharding import Mesh
from jax.sharding import PartitionSpec as P

LOG2E = math.log2(math.e)
STATS = 8
VMEM_LIMIT = 32 * 1024 * 1024
SMALL_LIMIT = 8 * 1024 * 1024
BF16 = jnp.bfloat16
F32 = jnp.float32
VMEM = pl.BlockSpec(memory_space=pltpu.VMEM)


def peer(place, step, count):
    if count & (count - 1) == 0:
        return place ^ step
    return (place + count - step) % count


def fetch(value, axis, step):
    count = lax.axis_size(axis)
    return lax.ppermute(value, axis, [(peer(i, step, count), i) for i in range(count)])


def give_back(value, axis, step):
    count = lax.axis_size(axis)
    return lax.ppermute(value, axis, [(i, peer(i, step, count)) for i in range(count)])


def three_parts(value):
    high = value.astype(BF16).astype(F32)
    rest = value - high
    middle = rest.astype(BF16).astype(F32)
    return [high, middle, rest - middle]


def pack_kernel(heads, q_ref, g_ref, o_ref, lse_ref, start_ref, pack_ref):
    tok = q_ref.shape[0]
    width = q_ref.shape[1] // heads
    half = tok // 2
    lanes = heads * half
    rows = []
    lse = lse_ref[...]
    starts = start_ref[...]
    for late in range(2):
        here = slice(late * half, (late + 1) * half)
        products = []
        for h in range(heads):
            cols = slice(h * width, (h + 1) * width)
            q, g = q_ref[here, cols], g_ref[here, cols]
            first = late * lanes + h * half
            pack_ref[first : first + half, :] = q
            pack_ref[2 * lanes + first : 2 * lanes + first + half, :] = g
            products.append(g.astype(F32) * o_ref[here, cols].astype(F32))
        delta = jnp.sum(jnp.concatenate(products, axis=0).T, axis=0, keepdims=True)
        log_part = jnp.concatenate([lse[h : h + 1, here] for h in range(heads)], axis=1)
        start = jnp.concatenate([starts[:, here]] * heads, axis=1)
        stats = three_parts(log_part) + three_parts(delta)
        stats += [(start >> 8).astype(F32), (start & 255).astype(F32)]
        for value in stats:
            rows += [value[:, c : c + width] for c in range(0, lanes, width)]
    pack_ref[4 * lanes :, :] = jnp.concatenate(rows, axis=0).astype(BF16)


def pack(queries, d_out, outputs, lse, doc_start, heads):
    tok = queries.shape[0]
    width = queries.shape[1] // heads
    stat_rows = STATS * heads * tok // width
    return pl.pallas_call(
        functools.partial(pack_kernel, heads),
        out_shape=jax.ShapeDtypeStruct((2 * heads * tok + stat_rows, width), BF16),
        in_specs=[VMEM] * 5,
        out_specs=VMEM,
        compiler_params=pltpu.CompilerParams(vmem_limit_bytes=SMALL_LIMIT),
        name="pack",
    )(queries, d_out, outputs, lse.T, doc_start.reshape(1, tok))


def part_kernel(step, first, last, heads, sizes, *refs):
    inner, zed = sizes
    pack_ref, refs = refs[0], refs[1:]
    if first:
        blocks, refs = refs[: 2 * zed], refs[2 * zed :]
        dq_ref, acc_ref, k_ref, v_ref, kt_ref, dqt_ref = refs
    else:
        k_ref, v_ref, kt_ref, acc_in, dq_ref, acc_ref = refs[:6]
        dqt_ref = refs[-1]
    me = lax.axis_index("inner")
    z_me = lax.axis_index("z")
    core = lax.axis_index("core")
    outer = 2 * z_me + core
    tok, width = dq_ref.shape[0], dq_ref.shape[1] // heads
    half = tok // 2
    lanes = heads * half
    front = zed * tok
    band_len = inner * half
    bands = 4 * zed
    scale = width**-0.5
    nt = (((1,), (1,)), ((), ()))

    def rows_of(step, other):
        source = 2 * peer(z_me, step, zed) + (1 - core if other else core)
        return [pl.ds(pl.multiple_of(late * front + source * half, half), half) for late in range(2)]

    if first:
        for n, block in enumerate(blocks):
            for late, here in enumerate(rows_of(n % zed, n >= zed)):
                k_ref[here, :] = block[late * half : (late + 1) * half, :width]
                v_ref[here, :] = block[late * half : (late + 1) * half, width:]
        kt_ref[...] = k_ref[...].T

    per = lanes // width
    member = peer(me, step, inner)
    lane = lax.broadcasted_iota(jnp.int32, (1, lanes), 1) % half
    row = lax.broadcasted_iota(jnp.int32, (tok, 1), 0)
    rows = pack_ref[4 * lanes :, :].astype(F32)
    info = []
    for late in range(2):

        def stat(n):
            at = (late * STATS + n) * per
            return jnp.concatenate([rows[at + i : at + i + 1] for i in range(per)], axis=1)

        lse = (stat(0) + stat(1) + stat(2)) * LOG2E
        delta = stat(3) + stat(4) + stat(5)
        start = (stat(6) * 256.0 + stat(7)).astype(jnp.int32)
        band = bands - 1 - outer if late else outer
        info.append((lse, delta, start, band * band_len + member * half + lane))

    def pick(early, pair):
        return jnp.where(early, pair[0], pair[1])

    def tile(keys, values, q, g, lse, delta, mask):
        s = lax.dot_general(keys, q, nt, preferred_element_type=F32)
        dp = lax.dot_general(values, g, nt, preferred_element_type=F32)
        prob = jnp.where(mask, jnp.exp2(s * (scale * LOG2E) - lse), 0.0)
        dscore = prob * (dp - delta)
        return prob.astype(BF16), dscore.astype(BF16)

    lse, delta, start, _ = info[1]
    pos = jnp.concatenate(
        [(2 * j + row // half) * band_len + me * half + row % half for j in range(zed)], axis=0
    )
    q_late = pack_ref[lanes : 2 * lanes, :]
    g_late = pack_ref[3 * lanes : 4 * lanes, :]
    prob, dscore = tile(k_ref[:front, :], v_ref[:front, :], q_late, g_late, lse, delta, pos >= start)
    dk = jnp.dot(dscore, q_late, preferred_element_type=F32)
    dv = jnp.dot(prob, g_late, preferred_element_type=F32)
    dqt_ref[:, lanes:] = jnp.dot(kt_ref[:, :front], dscore, preferred_element_type=F32)
    dqt_ref[:, :lanes] = jnp.zeros((width, lanes), F32)
    if first:
        acc_ref[:front, :width] = dk
        acc_ref[:front, width:] = dv
        acc_ref[front:, :] = jnp.zeros((front, 2 * width), F32)
    else:
        acc_ref[:front, :width] = acc_in[:front, :width] + dk
        acc_ref[:front, width:] = acc_in[:front, width:] + dv
        acc_ref[front:, :] = acc_in[front:, :]

    done = []
    for t in range(zed + 1):
        early = t <= z_me
        j = jnp.where(early, t, t - 1)
        first_key = pl.multiple_of(jnp.where(early, 0, front) + j * tok, tok)
        first_query = pl.multiple_of(jnp.where(early, 0, lanes), lanes)
        source = 2 * j + row // half
        band = jnp.where(early, source, bands - 1 - source)
        pos = band * band_len + me * half + row % half
        lse, delta, start, q_pos = (pick(early, (a, b)) for a, b in zip(*info))
        keys = pl.ds(first_key, tok)
        q = pack_ref[pl.ds(first_query, lanes), :]
        g = pack_ref[pl.ds(pl.multiple_of(2 * lanes + first_query, lanes), lanes), :]
        mask = jnp.logical_and(pos <= q_pos, pos >= start)
        prob, dscore = tile(k_ref[keys, :], v_ref[keys, :], q, g, lse, delta, mask)
        done.append((keys, pl.ds(first_query, lanes), q, g, prob, dscore))
    parts = []
    for keys, here, q, g, prob, dscore in done:
        dk = jnp.dot(dscore, q, preferred_element_type=F32)
        dv = jnp.dot(prob, g, preferred_element_type=F32)
        dq = jnp.dot(kt_ref[:, keys], dscore, preferred_element_type=F32)
        parts.append((keys, here, dk, dv, dq))
    for keys, here, dk, dv, dq in parts:
        acc_ref[keys, :width] += dk
        acc_ref[keys, width:] += dv
        dqt_ref[:, here] += dq

    for late in range(2):
        turned = (dqt_ref[:, late * lanes : (late + 1) * lanes] * scale).T.astype(dq_ref.dtype)
        for h in range(heads):
            dq_ref[late * half : (late + 1) * half, h * width : (h + 1) * width] = turned[h * half : (h + 1) * half]

    if last:
        kept_ref, sent_ref = refs[6:8]
        for other, out in enumerate((kept_ref, sent_ref)):
            for s in range(zed):
                for late, here in enumerate(rows_of(s, other)):
                    to = slice(s * tok + late * half, s * tok + (late + 1) * half)
                    out[to, :width] = (acc_ref[here, :width] * scale).astype(out.dtype)
                    out[to, width:] = acc_ref[here, width:].astype(out.dtype)


def part(step, packed, state, last, heads, sizes, tok, width):
    zed = sizes[1]
    first = step == 0
    keys = 2 * zed * tok
    outs = [jax.ShapeDtypeStruct((tok, heads * width), F32 if first else BF16)]
    acc = jax.ShapeDtypeStruct((keys, 2 * width), F32)
    scratch = [pltpu.VMEM((width, heads * tok), F32)]
    if first:
        outs += [acc] + [jax.ShapeDtypeStruct(s, BF16) for s in ((keys, width), (keys, width), (width, keys))]
    else:
        outs += [acc]
    if last:
        outs += [jax.ShapeDtypeStruct((zed * tok, 2 * width), t) for t in (F32, BF16)]
    args = [packed] + list(state)
    elements = heads * tok * keys * 9 // 16
    return pl.pallas_call(
        functools.partial(part_kernel, step, first, last, heads, sizes),
        out_shape=outs,
        in_specs=[VMEM] * len(args),
        out_specs=[VMEM] * len(outs),
        scratch_shapes=scratch,
        compiler_params=pltpu.CompilerParams(vmem_limit_bytes=VMEM_LIMIT),
        cost_estimate=pl.CostEstimate(flops=elements * width * 10, bytes_accessed=1 << 20, transcendentals=elements),
        name="part",
    )(*args)


def join_kernel(kept_ref, other_ref, *outs):
    tok = outs[0].shape[0]
    for s, out in enumerate(outs):
        here = slice(s * tok, (s + 1) * tok)
        out[...] = (kept_ref[here, :] + other_ref[here, :].astype(F32)).astype(out.dtype)


def join(kept, other, zed):
    tok, two = kept.shape[0] // zed, kept.shape[1]
    outs = [jax.ShapeDtypeStruct((tok, two), F32 if s == 0 else BF16) for s in range(zed)]
    return pl.pallas_call(
        join_kernel, out_shape=outs, in_specs=[VMEM] * 2, out_specs=[VMEM] * zed, name="join",
        compiler_params=pltpu.CompilerParams(vmem_limit_bytes=SMALL_LIMIT),
    )(kept, other)


def total_kernel(*refs):
    out = refs[-1]
    total = refs[0][...]
    for ref in refs[1:-1]:
        total = total + ref[...].astype(F32)
    out[...] = total.astype(out.dtype)


def total(values):
    return pl.pallas_call(
        total_kernel,
        out_shape=jax.ShapeDtypeStruct(values[0].shape, BF16),
        in_specs=[VMEM] * len(values),
        out_specs=VMEM,
        compiler_params=pltpu.CompilerParams(vmem_limit_bytes=SMALL_LIMIT),
        name="total",
    )(*values)


def on_device(queries, keys_values, outputs, d_out, lse, doc_start):
    inner = lax.axis_size("inner")
    zed = lax.axis_size("z")
    heads = lse.shape[1]
    sizes = (inner, zed)
    own = pack(queries, d_out, outputs, lse, doc_start, heads)
    packs = [own] + [fetch(own, "inner", s) for s in range(1, inner)]
    mine = [keys_values] + [fetch(keys_values, "z", s) for s in range(1, zed)]
    others = [fetch(kv, "core", 1) for kv in mine]
    tok, width = keys_values.shape[0], keys_values.shape[1] // 2
    dqs = []
    state = mine + others
    for s in range(inner):
        out = part(s, packs[s], state, s == inner - 1, heads, sizes, tok, width)
        dqs.append(out[0])
        state = (list(out[2:5]) if s == 0 else state[:3]) + [out[1]]
    kept, sent = out[2:4]
    dq_home = [dqs[0]] + [give_back(dqs[s], "inner", s) for s in range(1, inner)]
    joined = join(kept, fetch(sent, "core", 1), zed)
    dkv_home = [joined[0]] + [give_back(joined[s], "z", s) for s in range(1, zed)]
    return (total(dq_home), total(dkv_home))


def solution(mesh):
    inner, outer = mesh.shape["inner"], mesh.shape["outer"]
    split = Mesh(mesh.devices.reshape(inner, outer // 2, 2), ("inner", "z", "core"))
    rows = P(("inner", "z", "core"), None)
    return jax.shard_map(
        on_device,
        mesh=split,
        in_specs=(rows, rows, rows, rows, rows, P(("inner", "z", "core"))),
        out_specs=(rows, rows),
        check_vma=False,
    )
```

time: 45.2 us -> 41.1 us (0.909)
  Pallas kernels: 13.9 us -> 7.57 us
  waiting for transfers between devices: 6.78 us -> 11.1 us
  local copies, waits for them, and re-layouts: 4.48 us -> 3.38 us
  starting transfers between devices: 19.1 us -> 18.1 us
    ppermute x6, waiting for transfers between devices: 1.55 us -> 5.29 us  [give_back(): lax.ppermute(value, axis, [(i, peer(i, step, count)) for i in range(count)])]
    pallas_call x2, Pallas kernels: 3.46 us -> 1.38 us  [total(): pl.pallas_call(total_kernel, out_shape=jax.ShapeDtypeStruct(values[0].sha...]
    pallas_call x1, Pallas kernels: 1.83 us -> 0.06 us  [join(): pl.pallas_call(join_kernel, out_shape=outs, in_specs=[VMEM] * 2, out_spec...]
    pallas_call x1, Pallas kernels: 1.94 us -> 0.17 us  [pack(): pl.pallas_call(functools.partial(pack_kernel, heads), out_shape=jax.Shape...]
    ppermute x6, starting transfers between devices: 7.88 us -> 6.37 us  [give_back(): lax.ppermute(value, axis, [(i, peer(i, step, count)) for i in range(count)])]
    unnamed x22 -> x12, local copies, waits for them, and re-layouts: 4.48 us -> 3.38 us
    pallas_call x4, Pallas kernels: 6.66 us -> 5.95 us  [part(): pl.pallas_call(functools.partial(part_kernel, step, first, last, heads, s...]
    ppermute x11, starting transfers between devices: 11.2 us -> 11.8 us  [fetch(): lax.ppermute(value, axis, [(peer(i, step, count), i) for i in range(count)])]
  transfers between devices with their start and end apart: 17 -> 17, of which waited for: 6 -> 11; matrix products, arithmetic and copies ran while one was open for 0% -> 0% of each run, Pallas kernels for 19% -> 11%
where the time goes in v2:
time: 41.1 us; the launch traced here: 40.9 us
  starting transfers between devices  18.1 us (44%)
  waiting for transfers between devices  11.1 us (27%)
  Pallas kernels  7.57 us (18%)
  local copies, waits for them, and re-layouts  3.38 us (8%)
  between operations  0.73 us (2%)
    ppermute x11, starting transfers between devices, fetch(): lax.ppermute(value, axis, [(peer(i, step, count), i) for i in range(count)])  11.8 us
    ppermute x6, starting transfers between devices, give_back(): lax.ppermute(value, axis, [(i, peer(i, step, count)) for i in range(count)])  6.37 us
    pallas_call x4, Pallas kernels, part(): pl.pallas_call(functools.partial(part_kernel, step, first, last, heads, s...  5.95 us
    ppermute x11, waiting for transfers between devices, fetch(): lax.ppermute(value, axis, [(peer(i, step, count), i) for i in range(count)])  5.77 us
    ppermute x6, waiting for transfers between devices, give_back(): lax.ppermute(value, axis, [(i, peer(i, step, count)) for i in range(count)])  5.29 us
    unnamed x12, local copies, waits for them, and re-layouts  3.38 us
    pallas_call x2, Pallas kernels, total(): pl.pallas_call(total_kernel, out_shape=jax.ShapeDtypeStruct(values[0].sha...  1.38 us
  transfers between devices with their start and end apart: 17, of which 11 were waited for; matrix products, arithmetic and copies ran while one was open for 0% of the time, Pallas kernels for 11%

profile of v2, /device:TPU:0, one launch (start us, length us, event | category | flops | bytes accessed | tf_op | source)
XLA Modules:
  0.0 40.9 jit_solution(9244064375611580481)
XLA Ops:
  1.3 0.9 %copy-done = bf16[128,512]{1,0:T(8,128)(2,1)S(1)} copy-done((bf16[128,512]{1,0:T(8,128)(2,1)S(1)}, bf16[128,512]{1,0:T(8,128)(2,1)}, u32[]{:S(2)}) %copy-start) | copy-done | bytes 131096
  2.2 0.9 %copy-done.1 = bf16[128,512]{1,0:T(8,128)(2,1)S(1)} copy-done((bf16[128,512]{1,0:T(8,128)(2,1)S(1)}, bf16[128,512]{1,0:T(8,128)(2,1)}, u32[]{:S(2)}) %copy-start.1) | copy-done | bytes 131096
  3.1 0.9 %copy-done.2 = bf16[128,512]{1,0:T(8,128)(2,1)S(1)} copy-done((bf16[128,512]{1,0:T(8,128)(2,1)S(1)}, bf16[128,512]{1,0:T(8,128)(2,1)}, u32[]{:S(2)}) %copy-start.2) | copy-done | bytes 131096
  4.2 3.0 %collective-permute-start.7 = (bf16[1056,128]{1,0:T(8,128)(2,1)S(1)}, bf16[1056,128]{1,0:T(8,128)(2,1)S(1)}, u32[]{:S(2)}, u32[]{:S(2)}) collective-permute-start(bf16[1056,128]{1,0:T(8,128)(2,1)S(1)} %pack.1.refs_0_), channel_id=1, source_target_pairs={{8,0},{0,8},{24,16},{16,24},{9,1},{1,9},{25,17},{17,25},{10,2},{2,... | collective-permute-start | bytes 811016 | tf_op jit(solution)/shard_map/ppermute | solution.py:29
  7.2 3.6 %collective-permute-start.2 = (bf16[128,256]{1,0:T(8,128)(2,1)S(1)}, bf16[128,256]{1,0:T(8,128)(2,1)S(1)}, u32[]{:S(2)}, u32[]{:S(2)}) collective-permute-start(bf16[128,256]{1,0:T(8,128)(2,1)S(1)} %copy-done.5), channel_id=1, source_target_pairs={{6,0},{4,2},{2,4},{0,6},{7,1},{5,3},{3,5},{1,7},{14,8},{12,10},{10... | collective-permute-start | bytes 196616 | tf_op jit(solution)/shard_map/ppermute | solution.py:29
  10.8 1.5 %collective-permute-start.9 = (bf16[1056,128]{1,0:T(8,128)(2,1)S(1)}, bf16[1056,128]{1,0:T(8,128)(2,1)S(1)}, u32[]{:S(2)}, u32[]{:S(2)}) collective-permute-start(bf16[1056,128]{1,0:T(8,128)(2,1)S(1)} %pack.1.refs_0_), channel_id=1, source_target_pairs={{16,0},{24,8},{0,16},{8,24},{17,1},{25,9},{1,17},{9,25},{18,2},{26... | collective-permute-start | bytes 811016 | tf_op jit(solution)/shard_map/ppermute | solution.py:29
  12.3 0.8 %collective-permute-start = (bf16[128,256]{1,0:T(8,128)(2,1)S(1)}, bf16[128,256]{1,0:T(8,128)(2,1)S(1)}, u32[]{:S(2)}, u32[]{:S(2)}) collective-permute-start(bf16[128,256]{1,0:T(8,128)(2,1)S(1)} %copy-done.5), channel_id=1, source_target_pairs={{2,0},{0,2},{6,4},{4,6},{3,1},{1,3},{7,5},{5,7},{10,8},{8,10},{14,... | collective-permute-start | bytes 196616 | tf_op jit(solution)/shard_map/ppermute | solution.py:29
  13.3 1.8 %collective-permute-start.11 = (bf16[1056,128]{1,0:T(8,128)(2,1)S(1)}, bf16[1056,128]{1,0:T(8,128)(2,1)S(1)}, u32[]{:S(2)}, u32[]{:S(2)}) collective-permute-start(bf16[1056,128]{1,0:T(8,128)(2,1)S(1)} %pack.1.refs_0_), channel_id=1, source_target_pairs={{24,0},{16,8},{8,16},{0,24},{25,1},{17,9},{9,17},{1,25},{26,2},{18... | collective-permute-start | bytes 811016 | tf_op jit(solution)/shard_map/ppermute | solution.py:29
  15.2 2.4 %collective-permute-done.1.refs_3_ = bf16[128,256]{1,0:T(8,128)(2,1)S(1)} collective-permute-done((bf16[128,256]{1,0:T(8,128)(2,1)S(1)}, bf16[128,256]{1,0:T(8,128)(2,1)S(1)}, u32[]{:S(2)}, u32[]{:S(2)}) %collective-permute-start.1) | collective-permute-done | bytes 65568 | tf_op jit(solution)/shard_map/ppermute | solution.py:29
  18.1 0.7 %collective-permute-done.3.refs_5_ = bf16[128,256]{1,0:T(8,128)(2,1)S(1)} collective-permute-done((bf16[128,256]{1,0:T(8,128)(2,1)S(1)}, bf16[128,256]{1,0:T(8,128)(2,1)S(1)}, u32[]{:S(2)}, u32[]{:S(2)}) %collective-permute-start.3) | collective-permute-done | bytes 65568 | tf_op jit(solution)/shard_map/ppermute | solution.py:29
  19.4 0.7 %collective-permute-done.5.refs_7_ = bf16[128,256]{1,0:T(8,128)(2,1)S(1)} collective-permute-done((bf16[128,256]{1,0:T(8,128)(2,1)S(1)}, bf16[128,256]{1,0:T(8,128)(2,1)S(1)}, u32[]{:S(2)}, u32[]{:S(2)}) %collective-permute-start.5) | collective-permute-done | bytes 65568 | tf_op jit(solution)/shard_map/ppermute | solution.py:29
  20.3 1.3 %part.4 = (f32[128,512]{1,0:T(8,128)S(1)}, f32[1024,256]{1,0:T(8,128)S(1)}, bf16[1024,128]{1,0:T(8,128)(2,1)S(1)}, bf16[1024,128]{1,0:T(8,128)(2,1)S(1)}, bf16[128,1024]{1,0:T(8,128)(2,1)S(1)}) custom-call(bf16[1056,128]{1,0:T(8,128)(2,1)S(1)} %pack.1.refs_0_, bf16[128,256]{1,0:T(8,128)(2,1)S(1)} %copy-done.5, ...), custom_call_target="tpu_custom_call" | custom-call | flops 377487360 | bytes 1048576 | tf_op jit(solution)/shard_map/part/pallas_call | solution.py:224
  21.6 1.2 %part.5 = (bf16[128,512]{1,0:T(8,128)(2,1)S(1)}, f32[1024,256]{1,0:T(8,128)S(1)}) custom-call(bf16[1056,128]{1,0:T(8,128)(2,1)S(1)} %collective-permute-done.7.refs_0_, bf16[1024,128]{1,0:T(8,128)(2,1)S(1)} %get-tuple-element.19.refs_1_, bf16[1024,128]{1,0:T(8,128)(2,1)S(1)} %get-tuple-element.20.refs_2_, bf16[128,1024]{1,0:T(8,128)(2,1)S(1)} %get-tuple-element.21.refs_3_, ...), custom_call_target="tpu_custom_call" | custom-call | flops 377487360 | bytes 1048576 | tf_op jit(solution)/shard_map/part/pallas_call | solution.py:224
  22.8 1.5 %collective-permute-done.9.refs_0_ = bf16[1056,128]{1,0:T(8,128)(2,1)S(1)} collective-permute-done((bf16[1056,128]{1,0:T(8,128)(2,1)S(1)}, bf16[1056,128]{1,0:T(8,128)(2,1)S(1)}, u32[]{:S(2)}, u32[]{:S(2)}) %collective-permute-start.9) | collective-permute-done | bytes 270368 | tf_op jit(solution)/shard_map/ppermute | solution.py:29
  24.3 1.2 %part.6 = (bf16[128,512]{1,0:T(8,128)(2,1)S(1)}, f32[1024,256]{1,0:T(8,128)S(1)}) custom-call(bf16[1056,128]{1,0:T(8,128)(2,1)S(1)} %collective-permute-done.9.refs_0_, bf16[1024,128]{1,0:T(8,128)(2,1)S(1)} %get-tuple-element.19.refs_1_, bf16[1024,128]{1,0:T(8,128)(2,1)S(1)} %get-tuple-element.20.refs_2_, bf16[128,1024]{1,0:T(8,128)(2,1)S(1)} %get-tuple-element.21.refs_3_, ...), custom_call_target="tpu_custom_call" | custom-call | flops 377487360 | bytes 1048576 | tf_op jit(solution)/shard_map/part/pallas_call | solution.py:224
  25.5 2.2 %part.7 = (bf16[128,512]{1,0:T(8,128)(2,1)S(1)}, f32[1024,256]{1,0:T(8,128)}, f32[512,256]{1,0:T(8,128)S(1)}, bf16[512,256]{1,0:T(8,128)(2,1)S(1)}) custom-call(bf16[1056,128]{1,0:T(8,128)(2,1)S(1)} %collective-permute-done.11.refs_0_, bf16[1024,128]{1,0:T(8,128)(2,1)S(1)} %get-tuple-element.19.refs_1_, bf16[1024,128]{1,0:T(8,128)(2,1)S(1)} %get-tuple-element.20.refs_2_, ...), custom_call_target="tpu_custom_call" | custom-call | flops 377487360 | bytes 1048576 | tf_op jit(solution)/shard_map/part/pallas_call | solution.py:224
  27.7 0.9 %collective-permute-start.8 = (bf16[128,512]{1,0:T(8,128)(2,1)S(1)}, bf16[128,512]{1,0:T(8,128)(2,1)S(1)}, u32[]{:S(2)}, u32[]{:S(2)}) collective-permute-start(bf16[128,512]{1,0:T(8,128)(2,1)S(1)} %get-tuple-element.23), channel_id=1, source_target_pairs={{0,8},{8,0},{16,24},{24,16},{1,9},{9,1},{17,25},{25,17},{2,10},{10... | collective-permute-start | bytes 393224 | tf_op jit(solution)/shard_map/ppermute | solution.py:34
  28.6 1.5 %collective-permute-start.10 = (bf16[128,512]{1,0:T(8,128)(2,1)S(1)}, bf16[128,512]{1,0:T(8,128)(2,1)S(1)}, u32[]{:S(2)}, u32[]{:S(2)}) collective-permute-start(bf16[128,512]{1,0:T(8,128)(2,1)S(1)} %get-tuple-element.25), channel_id=1, source_target_pairs={{0,16},{8,24},{16,0},{24,8},{1,17},{9,25},{17,1},{25,9},{2,18},{10... | collective-permute-start | bytes 393224 | tf_op jit(solution)/shard_map/ppermute | solution.py:34
  30.1 1.1 %collective-permute-start.12 = (bf16[128,512]{1,0:T(8,128)(2,1)S(1)}, bf16[128,512]{1,0:T(8,128)(2,1)S(1)}, u32[]{:S(2)}, u32[]{:S(2)}) collective-permute-start(bf16[128,512]{1,0:T(8,128)(2,1)S(1)} %get-tuple-element.27), channel_id=1, source_target_pairs={{0,24},{8,16},{16,8},{24,0},{1,25},{9,17},{17,9},{25,1},{2,26},{10... | collective-permute-start | bytes 393224 | tf_op jit(solution)/shard_map/ppermute | solution.py:34
  31.4 1.1 %collective-permute-start.15 = (bf16[128,256]{1,0:T(8,128)(2,1)S(1)}, bf16[128,256]{1,0:T(8,128)(2,1)S(1)}, u32[]{:S(2)}, u32[]{:S(2)}) collective-permute-start(bf16[128,256]{1,0:T(8,128)(2,1)S(1)} %get-tuple-element.32), channel_id=1, source_target_pairs={{0,4},{2,6},{4,0},{6,2},{1,5},{3,7},{5,1},{7,3},{8,12},{10,14},{12... | collective-permute-start | bytes 196616 | tf_op jit(solution)/shard_map/ppermute | solution.py:34
  32.5 1.6 %collective-permute-done.8.refs_1_ = bf16[128,512]{1,0:T(8,128)(2,1)S(1)} collective-permute-done((bf16[128,512]{1,0:T(8,128)(2,1)S(1)}, bf16[128,512]{1,0:T(8,128)(2,1)S(1)}, u32[]{:S(2)}, u32[]{:S(2)}) %collective-permute-start.8) | collective-permute-done | bytes 131104 | tf_op jit(solution)/shard_map/ppermute | solution.py:34
  34.0 1.7 %collective-permute-start.16 = (bf16[128,256]{1,0:T(8,128)(2,1)S(1)}, bf16[128,256]{1,0:T(8,128)(2,1)S(1)}, u32[]{:S(2)}, u32[]{:S(2)}) collective-permute-start(bf16[128,256]{1,0:T(8,128)(2,1)S(1)} %get-tuple-element.33), channel_id=1, source_target_pairs={{0,6},{2,4},{4,2},{6,0},{1,7},{3,5},{5,3},{7,1},{8,14},{10,12},{12... | collective-permute-start | bytes 196616 | tf_op jit(solution)/shard_map/ppermute | solution.py:34
  36.1 1.3 %collective-permute-done.12.refs_3_ = bf16[128,512]{1,0:T(8,128)(2,1)S(1)} collective-permute-done((bf16[128,512]{1,0:T(8,128)(2,1)S(1)}, bf16[128,512]{1,0:T(8,128)(2,1)S(1)}, u32[]{:S(2)}, u32[]{:S(2)}) %collective-permute-start.12) | collective-permute-done | bytes 131104 | tf_op jit(solution)/shard_map/ppermute | solution.py:34
  38.8 1.4 %collective-permute-done.16.refs_3_ = bf16[128,256]{1,0:T(8,128)(2,1)S(1)} collective-permute-done((bf16[128,256]{1,0:T(8,128)(2,1)S(1)}, bf16[128,256]{1,0:T(8,128)(2,1)S(1)}, u32[]{:S(2)}, u32[]{:S(2)}) %collective-permute-start.16) | collective-permute-done | bytes 65568 | tf_op jit(solution)/shard_map/ppermute | solution.py:34
  (30 shorter events, 4.8 us)
Async XLA Ops:
  0.6 0.7 %copy-start.3 = (f32[128,4]{0,1:T(4,128)S(1)}, f32[128,4]{0,1:T(4,128)}, u32[]{:S(2)}) copy-start(f32[128,4]{0,1:T(4,128)} %param.10) | copy-start | bytes 6148
  0.6 0.7 %copy-start.4 = (s32[128]{0:T(128)S(1)}, s32[128]{0:T(128)}, u32[]{:S(2)}) copy-start(s32[128]{0:T(128)} %param.11) | copy-start | bytes 1540
  1.3 0.9 %copy-start = (bf16[128,512]{1,0:T(8,128)(2,1)S(1)}, bf16[128,512]{1,0:T(8,128)(2,1)}, u32[]{:S(2)}) copy-start(bf16[128,512]{1,0:T(8,128)(2,1)} %q_ref.1) | copy-start | bytes 393220
  2.2 0.9 %copy-start.1 = (bf16[128,512]{1,0:T(8,128)(2,1)S(1)}, bf16[128,512]{1,0:T(8,128)(2,1)}, u32[]{:S(2)}) copy-start(bf16[128,512]{1,0:T(8,128)(2,1)} %g_ref.1) | copy-start | bytes 393220
  3.1 0.9 %copy-start.2 = (bf16[128,512]{1,0:T(8,128)(2,1)S(1)}, bf16[128,512]{1,0:T(8,128)(2,1)}, u32[]{:S(2)}) copy-start(bf16[128,512]{1,0:T(8,128)(2,1)} %o_ref.1) | copy-start | bytes 393220
  4.0 3.2 %copy-start.5 = (bf16[128,256]{1,0:T(8,128)(2,1)S(1)}, bf16[128,256]{1,0:T(8,128)(2,1)}, u32[]{:S(2)}) copy-start(bf16[128,256]{1,0:T(8,128)(2,1)} %refs_1_.1) | copy-start | bytes 196612
  4.2 17.4 %collective-permute-start.7 = (bf16[1056,128]{1,0:T(8,128)(2,1)S(1)}, bf16[1056,128]{1,0:T(8,128)(2,1)S(1)}, u32[]{:S(2)}, u32[]{:S(2)}) collective-permute-start(bf16[1056,128]{1,0:T(8,128)(2,1)S(1)} %pack.1.refs_0_), channel_id=1, source_target_pairs={{8,0},{0,8},{24,16},{16,24},{9,1},{1,9},{25,17},{17,25},{10,2},{2,... | collective-permute-start | bytes 811016 | tf_op jit(solution)/shard_map/ppermute | solution.py:29
  7.2 6.1 %collective-permute-start.2 = (bf16[128,256]{1,0:T(8,128)(2,1)S(1)}, bf16[128,256]{1,0:T(8,128)(2,1)S(1)}, u32[]{:S(2)}, u32[]{:S(2)}) collective-permute-start(bf16[128,256]{1,0:T(8,128)(2,1)S(1)} %copy-done.5), channel_id=1, source_target_pairs={{6,0},{4,2},{2,4},{0,6},{7,1},{5,3},{3,5},{1,7},{14,8},{12,10},{10... | collective-permute-start | bytes 196616 | tf_op jit(solution)/shard_map/ppermute | solution.py:29
  10.8 13.5 %collective-permute-start.9 = (bf16[1056,128]{1,0:T(8,128)(2,1)S(1)}, bf16[1056,128]{1,0:T(8,128)(2,1)S(1)}, u32[]{:S(2)}, u32[]{:S(2)}) collective-permute-start(bf16[1056,128]{1,0:T(8,128)(2,1)S(1)} %pack.1.refs_0_), channel_id=1, source_target_pairs={{16,0},{24,8},{0,16},{8,24},{17,1},{25,9},{1,17},{9,25},{18,2},{26... | collective-permute-start | bytes 811016 | tf_op jit(solution)/shard_map/ppermute | solution.py:29
  12.3 5.2 %collective-permute-start.1 = (bf16[128,256]{1,0:T(8,128)(2,1)S(1)}, bf16[128,256]{1,0:T(8,128)(2,1)S(1)}, u32[]{:S(2)}, u32[]{:S(2)}) collective-permute-start(bf16[128,256]{1,0:T(8,128)(2,1)S(1)} %copy-done.5), channel_id=1, source_target_pairs={{4,0},{6,2},{0,4},{2,6},{5,1},{7,3},{1,5},{3,7},{12,8},{14,10},{8,... | collective-permute-start | bytes 196616 | tf_op jit(solution)/shard_map/ppermute | solution.py:29
  12.3 5.3 %collective-permute-start = (bf16[128,256]{1,0:T(8,128)(2,1)S(1)}, bf16[128,256]{1,0:T(8,128)(2,1)S(1)}, u32[]{:S(2)}, u32[]{:S(2)}) collective-permute-start(bf16[128,256]{1,0:T(8,128)(2,1)S(1)} %copy-done.5), channel_id=1, source_target_pairs={{2,0},{0,2},{6,4},{4,6},{3,1},{1,3},{7,5},{5,7},{10,8},{8,10},{14,... | collective-permute-start | bytes 196616 | tf_op jit(solution)/shard_map/ppermute | solution.py:29
  13.3 12.1 %collective-permute-start.11 = (bf16[1056,128]{1,0:T(8,128)(2,1)S(1)}, bf16[1056,128]{1,0:T(8,128)(2,1)S(1)}, u32[]{:S(2)}, u32[]{:S(2)}) collective-permute-start(bf16[1056,128]{1,0:T(8,128)(2,1)S(1)} %pack.1.refs_0_), channel_id=1, source_target_pairs={{24,0},{16,8},{8,16},{0,24},{25,1},{17,9},{9,17},{1,25},{26,2},{18... | collective-permute-start | bytes 811016 | tf_op jit(solution)/shard_map/ppermute | solution.py:29
  17.6 1.3 %collective-permute-start.3 = (bf16[128,256]{1,0:T(8,128)(2,1)S(1)}, bf16[128,256]{1,0:T(8,128)(2,1)S(1)}, u32[]{:S(2)}, u32[]{:S(2)}) collective-permute-start(bf16[128,256]{1,0:T(8,128)(2,1)S(1)} %copy-done.5), channel_id=1, source_target_pairs={{1,0},{0,1},{3,2},{2,3},{5,4},{4,5},{7,6},{6,7},{9,8},{8,9},{11,10... | collective-permute-start | bytes 196616 | tf_op jit(solution)/shard_map/ppermute | solution.py:29
  17.6 1.4 %collective-permute-start.6 = (bf16[128,256]{1,0:T(8,128)(2,1)S(1)}, bf16[128,256]{1,0:T(8,128)(2,1)S(1)}, u32[]{:S(2)}, u32[]{:S(2)}) collective-permute-start(bf16[128,256]{1,0:T(8,128)(2,1)S(1)} %collective-permute-done.2.refs_4_), channel_id=1, source_target_pairs={{1,0},{0,1},{3,2},{2,3},{5,4},{4,5},{7,6},{6,7},{9,8},{8,9},{11,10... | collective-permute-start | bytes 196616 | tf_op jit(solution)/shard_map/ppermute | solution.py:29
  18.8 1.3 %collective-permute-start.5 = (bf16[128,256]{1,0:T(8,128)(2,1)S(1)}, bf16[128,256]{1,0:T(8,128)(2,1)S(1)}, u32[]{:S(2)}, u32[]{:S(2)}) collective-permute-start(bf16[128,256]{1,0:T(8,128)(2,1)S(1)} %collective-permute-done.1.refs_3_), channel_id=1, source_target_pairs={{1,0},{0,1},{3,2},{2,3},{5,4},{4,5},{7,6},{6,7},{9,8},{8,9},{11,10... | collective-permute-start | bytes 196616 | tf_op jit(solution)/shard_map/ppermute | solution.py:29
  19.0 1.3 %collective-permute-start.4 = (bf16[128,256]{1,0:T(8,128)(2,1)S(1)}, bf16[128,256]{1,0:T(8,128)(2,1)S(1)}, u32[]{:S(2)}, u32[]{:S(2)}) collective-permute-start(bf16[128,256]{1,0:T(8,128)(2,1)S(1)} %collective-permute-done.refs_2_), channel_id=1, source_target_pairs={{1,0},{0,1},{3,2},{2,3},{5,4},{4,5},{7,6},{6,7},{9,8},{8,9},{11,10... | collective-permute-start | bytes 196616 | tf_op jit(solution)/shard_map/ppermute | solution.py:29
  27.7 3.5 %collective-permute-start.13 = (bf16[512,256]{1,0:T(8,128)(2,1)S(1)}, bf16[512,256]{1,0:T(8,128)(2,1)S(1)}, u32[]{:S(2)}, u32[]{:S(2)}) collective-permute-start(bf16[512,256]{1,0:T(8,128)(2,1)S(1)} %get-tuple-element.29), channel_id=1, source_target_pairs={{1,0},{0,1},{3,2},{2,3},{5,4},{4,5},{7,6},{6,7},{9,8},{8,9},{11,10... | collective-permute-start | bytes 786440 | tf_op jit(solution)/shard_map/ppermute | solution.py:29
  27.7 6.3 %collective-permute-start.8 = (bf16[128,512]{1,0:T(8,128)(2,1)S(1)}, bf16[128,512]{1,0:T(8,128)(2,1)S(1)}, u32[]{:S(2)}, u32[]{:S(2)}) collective-permute-start(bf16[128,512]{1,0:T(8,128)(2,1)S(1)} %get-tuple-element.23), channel_id=1, source_target_pairs={{0,8},{8,0},{16,24},{24,16},{1,9},{9,1},{17,25},{25,17},{2,10},{10... | collective-permute-start | bytes 393224 | tf_op jit(solution)/shard_map/ppermute | solution.py:34
  28.6 7.5 %collective-permute-start.10 = (bf16[128,512]{1,0:T(8,128)(2,1)S(1)}, bf16[128,512]{1,0:T(8,128)(2,1)S(1)}, u32[]{:S(2)}, u32[]{:S(2)}) collective-permute-start(bf16[128,512]{1,0:T(8,128)(2,1)S(1)} %get-tuple-element.25), channel_id=1, source_target_pairs={{0,16},{8,24},{16,0},{24,8},{1,17},{9,25},{17,1},{25,9},{2,18},{10... | collective-permute-start | bytes 393224 | tf_op jit(solution)/shard_map/ppermute | solution.py:34
  30.1 7.3 %collective-permute-start.12 = (bf16[128,512]{1,0:T(8,128)(2,1)S(1)}, bf16[128,512]{1,0:T(8,128)(2,1)S(1)}, u32[]{:S(2)}, u32[]{:S(2)}) collective-permute-start(bf16[128,512]{1,0:T(8,128)(2,1)S(1)} %get-tuple-element.27), channel_id=1, source_target_pairs={{0,24},{8,16},{16,8},{24,0},{1,25},{9,17},{17,9},{25,1},{2,26},{10... | collective-permute-start | bytes 393224 | tf_op jit(solution)/shard_map/ppermute | solution.py:34
  31.3 6.8 %collective-permute-start.14 = (bf16[128,256]{1,0:T(8,128)(2,1)S(1)}, bf16[128,256]{1,0:T(8,128)(2,1)S(1)}, u32[]{:S(2)}, u32[]{:S(2)}) collective-permute-start(bf16[128,256]{1,0:T(8,128)(2,1)S(1)} %get-tuple-element.31), channel_id=1, source_target_pairs={{0,2},{2,0},{4,6},{6,4},{1,3},{3,1},{5,7},{7,5},{8,10},{10,8},{12,... | collective-permute-start | bytes 196616 | tf_op jit(solution)/shard_map/ppermute | solution.py:34
  31.4 7.4 %collective-permute-start.15 = (bf16[128,256]{1,0:T(8,128)(2,1)S(1)}, bf16[128,256]{1,0:T(8,128)(2,1)S(1)}, u32[]{:S(2)}, u32[]{:S(2)}) collective-permute-start(bf16[128,256]{1,0:T(8,128)(2,1)S(1)} %get-tuple-element.32), channel_id=1, source_target_pairs={{0,4},{2,6},{4,0},{6,2},{1,5},{3,7},{5,1},{7,3},{8,12},{10,14},{12... | collective-permute-start | bytes 196616 | tf_op jit(solution)/shard_map/ppermute | solution.py:34
  34.0 6.2 %collective-permute-start.16 = (bf16[128,256]{1,0:T(8,128)(2,1)S(1)}, bf16[128,256]{1,0:T(8,128)(2,1)S(1)}, u32[]{:S(2)}, u32[]{:S(2)}) collective-permute-start(bf16[128,256]{1,0:T(8,128)(2,1)S(1)} %get-tuple-element.33), channel_id=1, source_target_pairs={{0,6},{2,4},{4,2},{6,0},{1,7},{3,5},{5,3},{7,1},{8,14},{10,12},{12... | collective-permute-start | bytes 196616 | tf_op jit(solution)/shard_map/ppermute | solution.py:34

commit v3 on v2

v3 whole, which is shorter than its diff:
```python
import functools
import math

import jax
import jax.numpy as jnp
from jax import lax
from jax.experimental import pallas as pl
from jax.experimental.pallas import tpu as pltpu
from jax.sharding import Mesh
from jax.sharding import PartitionSpec as P

LOG2E = math.log2(math.e)
STATS = 8
PIECES = 4
PART_COST = 200000000
VMEM_LIMIT = 32 * 1024 * 1024
SMALL_LIMIT = 8 * 1024 * 1024
BF16 = jnp.bfloat16
F32 = jnp.float32
VMEM = pl.BlockSpec(memory_space=pltpu.VMEM)


def power_of_two(count):
    return count & (count - 1) == 0


def peer(place, step, count):
    if power_of_two(count):
        return place ^ step
    return (place + count - step) % count


def query_rounds(inner):
    steps = list(range(1, inner))
    return [tuple(steps[n : n + 2]) for n in range(0, inner - 1, 2)]


def inner_pairs(steps, count):
    return [(2 * peer(i, steps[min(c, len(steps) - 1)], count) + c, 2 * i + c) for i in range(count) for c in range(2)]


def fetch(value, steps):
    return lax.ppermute(value, ("inner", "core"), inner_pairs(steps, lax.axis_size("inner")))


def give_back(value, steps):
    pairs = inner_pairs(steps, lax.axis_size("inner"))
    return lax.ppermute(value, ("inner", "core"), [(b, a) for a, b in pairs])


def fetch_z(value, step):
    count = lax.axis_size("z")
    return lax.ppermute(value, "z", [(peer(z, step, count), z) for z in range(count)])


def give_back_z(value, step):
    count = lax.axis_size("z")
    return lax.ppermute(value, "z", [(z, peer(z, step, count)) for z in range(count)])


def swap_cores(value):
    return lax.ppermute(value, "core", [(0, 1), (1, 0)])


def three_parts(value):
    high = value.astype(BF16).astype(F32)
    rest = value - high
    middle = rest.astype(BF16).astype(F32)
    return [high, middle, rest - middle]


def pack_kernel(heads, *refs):
    sources, pack_ref, places, arrived = refs[:5], refs[5], refs[6:11], refs[11]
    copies = [pltpu.make_async_copy(a, b, arrived.at[i]) for i, (a, b) in enumerate(zip(sources, places))]
    for copy in copies:
        copy.start()
    for copy in copies:
        copy.wait()
    q_ref, g_ref, o_ref, lse_ref, start_ref = places
    tok = q_ref.shape[0]
    width = q_ref.shape[1] // heads
    half = tok // 2
    lanes = heads * half
    rows = []
    lse = lse_ref[...]
    starts = start_ref[...]
    for late in range(2):
        here = slice(late * half, (late + 1) * half)
        products = []
        for h in range(heads):
            cols = slice(h * width, (h + 1) * width)
            q, g = q_ref[here, cols], g_ref[here, cols]
            first = late * lanes + h * half
            pack_ref[first : first + half, :] = q
            pack_ref[2 * lanes + first : 2 * lanes + first + half, :] = g
            products.append(g.astype(F32) * o_ref[here, cols].astype(F32))
        delta = jnp.sum(jnp.concatenate(products, axis=0).T, axis=0, keepdims=True)
        log_part = jnp.concatenate([lse[h : h + 1, here] for h in range(heads)], axis=1)
        start = jnp.concatenate([starts[:, here]] * heads, axis=1)
        stats = three_parts(log_part) + three_parts(delta)
        stats += [(start >> 8).astype(F32), (start & 255).astype(F32)]
        for value in stats:
            rows += [value[:, c : c + width] for c in range(0, lanes, width)]
    pack_ref[4 * lanes :, :] = jnp.concatenate(rows, axis=0).astype(BF16)


def pack(queries, d_out, outputs, lse, doc_start, heads):
    tok = queries.shape[0]
    width = queries.shape[1] // heads
    stat_rows = STATS * heads * tok // width
    args = (queries, d_out, outputs, lse.T, doc_start.reshape(1, tok))
    args = [pltpu.with_memory_space_constraint(a, pltpu.HBM) for a in args]
    return pl.pallas_call(
        functools.partial(pack_kernel, heads),
        out_shape=jax.ShapeDtypeStruct((2 * heads * tok + stat_rows, width), BF16),
        in_specs=[pl.BlockSpec(memory_space=pltpu.HBM)] * 5,
        out_specs=VMEM,
        scratch_shapes=[pltpu.VMEM(a.shape, a.dtype) for a in args] + [pltpu.SemaphoreType.DMA((5,))],
        compiler_params=pltpu.CompilerParams(vmem_limit_bytes=SMALL_LIMIT),
        name="pack",
    )(*args)


def stack_kernel(*refs):
    out = refs[-1]
    rows = refs[0].shape[0]
    for n, ref in enumerate(refs[:-1]):
        out[n * rows : (n + 1) * rows, :] = ref[...]


def stack(*values):
    rows, columns = values[0].shape
    return pl.pallas_call(
        stack_kernel,
        out_shape=jax.ShapeDtypeStruct((len(values) * rows, columns), values[0].dtype),
        in_specs=[VMEM] * len(values),
        out_specs=VMEM,
        compiler_params=pltpu.CompilerParams(vmem_limit_bytes=SMALL_LIMIT),
        name="stack",
    )(*values)


def part_kernel(steps, first, last, heads, sizes, *refs):
    inner, zed = sizes
    pack_ref, refs = refs[0], refs[1:]
    if first:
        blocks, refs = refs[:4], refs[4:]
        dq_ref, acc_ref, k_ref, v_ref, kt_ref, dqt_ref = refs
    elif last:
        k_ref, v_ref, kt_ref, acc_in, dq_ref, kept_ref, sent_ref, dqt_ref, acc_ref = refs
    else:
        k_ref, v_ref, kt_ref, acc_in, dq_ref, acc_ref, dqt_ref = refs
    me = lax.axis_index("inner")
    z_me = lax.axis_index("z")
    core = lax.axis_index("core")
    width = dq_ref.shape[1] // heads
    tok = k_ref.shape[0] // (2 * zed)
    half = tok // 2
    lanes = heads * half
    front = zed * tok
    band_len = inner * half
    bands = 4 * zed
    scale = width**-0.5
    nt = (((1,), (1,)), ((), ()))
    per = lanes // width
    rows_each = 4 * lanes + STATS * 2 * per
    jobs = pack_ref.shape[0] // rows_each
    lane = lax.broadcasted_iota(jnp.int32, (1, lanes), 1) % half
    row = lax.broadcasted_iota(jnp.int32, (tok, 1), 0)

    if first:
        for n, block in enumerate(blocks):
            steps_here = [0] if n < 2 else range(zed - 1, 0, -1)
            for m, s in enumerate(steps_here):
                source = 2 * peer(z_me, s, zed) + (1 - core if n % 2 else core)
                for late in range(2):
                    here = pl.ds(pl.multiple_of(late * front + source * half, half), half)
                    rows = slice(m * tok + late * half, m * tok + (late + 1) * half)
                    k_ref[here, :] = block[rows, :width]
                    v_ref[here, :] = block[rows, width:]
        kt_ref[...] = k_ref[...].T

    member = peer(me, jnp.where(core == 0, steps[0], steps[-1]), inner) if steps else me

    def tile(keys, values, q, g, lse, delta, mask):
        s = lax.dot_general(keys, q, nt, preferred_element_type=F32)
        dp = lax.dot_general(values, g, nt, preferred_element_type=F32)
        prob = jnp.where(mask, jnp.exp2(s * (scale * LOG2E) - lse), 0.0)
        dscore = prob * (dp - delta)
        return prob.astype(BF16), dscore.astype(BF16)

    def pick(early, pair):
        return jnp.where(early, pair[0], pair[1])

    for job in range(jobs):
        base = job * rows_each
        outer = 2 * z_me + (core if job == 0 else 1 - core)
        rows = pack_ref[base + 4 * lanes : base + rows_each, :].astype(F32)
        info = []
        for late in range(2):

            def stat(n):
                at = (late * STATS + n) * per
                return jnp.concatenate([rows[at + i : at + i + 1] for i in range(per)], axis=1)

            lse = (stat(0) + stat(1) + stat(2)) * LOG2E
            delta = stat(3) + stat(4) + stat(5)
            start = (stat(6) * 256.0 + stat(7)).astype(jnp.int32)
            band = bands - 1 - outer if late else outer
            info.append((lse, delta, start, band * band_len + member * half + lane))

        lse, delta, start, _ = info[1]
        pos = jnp.concatenate(
            [(2 * j + row // half) * band_len + me * half + row % half for j in range(zed)], axis=0
        )
        q_late = pack_ref[base + lanes : base + 2 * lanes, :]
        g_late = pack_ref[base + 3 * lanes : base + 4 * lanes, :]
        prob, dscore = tile(k_ref[:front, :], v_ref[:front, :], q_late, g_late, lse, delta, pos >= start)
        dk = jnp.dot(dscore, q_late, preferred_element_type=F32)
        dv = jnp.dot(prob, g_late, preferred_element_type=F32)
        dqt_ref[:, lanes:] = jnp.dot(kt_ref[:, :front], dscore, preferred_element_type=F32)
        dqt_ref[:, :lanes] = jnp.zeros((width, lanes), F32)
        if first:
            acc_ref[:front, :width] = dk
            acc_ref[:front, width:] = dv
            acc_ref[front:, :] = jnp.zeros((front, 2 * width), F32)
        else:
            before = acc_in if job == 0 else acc_ref
            acc_ref[:front, :width] = before[:front, :width] + dk
            acc_ref[:front, width:] = before[:front, width:] + dv
            if job == 0:
                acc_ref[front:, :] = acc_in[front:, :]

        done = []
        for t in range(zed + 1):
            early = t <= z_me
            j = jnp.where(early, t, t - 1)
            first_key = pl.multiple_of(jnp.where(early, 0, front) + j * tok, tok)
            first_query = pl.multiple_of(jnp.where(early, 0, lanes), lanes)
            source = 2 * j + row // half
            band = jnp.where(early, source, bands - 1 - source)
            pos = band * band_len + me * half + row % half
            lse, delta, start, q_pos = (pick(early, (a, b)) for a, b in zip(*info))
            keys = pl.ds(first_key, tok)
            q = pack_ref[pl.ds(pl.multiple_of(base + first_query, 16), lanes), :]
            g = pack_ref[pl.ds(pl.multiple_of(base + 2 * lanes + first_query, 16), lanes), :]
            mask = jnp.logical_and(pos <= q_pos, pos >= start)
            prob, dscore = tile(k_ref[keys, :], v_ref[keys, :], q, g, lse, delta, mask)
            done.append((keys, pl.ds(first_query, lanes), q, g, prob, dscore))
        parts = []
        for keys, here, q, g, prob, dscore in done:
            dk = jnp.dot(dscore, q, preferred_element_type=F32)
            dv = jnp.dot(prob, g, preferred_element_type=F32)
            dq = jnp.dot(kt_ref[:, keys], dscore, preferred_element_type=F32)
            parts.append((keys, here, dk, dv, dq))
        for keys, here, dk, dv, dq in parts:
            acc_ref[keys, :width] += dk
            acc_ref[keys, width:] += dv
            dqt_ref[:, here] += dq

        for late in range(2):
            turned = (dqt_ref[:, late * lanes : (late + 1) * lanes] * scale).T.astype(dq_ref.dtype)
            to = slice(job * tok + late * half, job * tok + (late + 1) * half)
            for h in range(heads):
                dq_ref[to, h * width : (h + 1) * width] = turned[h * half : (h + 1) * half]

    if last:
        low = core == 0
        for n in range(2 * zed):
            to = slice(n * half, (n + 1) * half)
            for columns, factor in ((slice(0, width), scale), (slice(width, 2 * width), 1.0)):
                one = acc_ref[n * tok : n * tok + half, columns] * factor
                two = acc_ref[n * tok + half : (n + 1) * tok, columns] * factor
                kept_ref[to, columns] = jnp.where(low, one, two)
                sent_ref[to, columns] = jnp.where(low, two, one).astype(sent_ref.dtype)


def part(steps, packed, state, last, heads, sizes, tok, width):
    zed = sizes[1]
    first = not steps
    jobs = max(1, len(steps))
    keys = 2 * zed * tok
    outs = [jax.ShapeDtypeStruct((jobs * tok, heads * width), F32 if first else BF16)]
    acc = ((keys, 2 * width), F32)
    scratch = [pltpu.VMEM((width, heads * tok), F32)]
    if last:
        outs += [jax.ShapeDtypeStruct((zed * tok, 2 * width), t) for t in (F32, BF16)]
        scratch.append(pltpu.VMEM(*acc))
    else:
        outs.append(jax.ShapeDtypeStruct(*acc))
    if first:
        outs += [jax.ShapeDtypeStruct(s, BF16) for s in ((keys, width), (keys, width), (width, keys))]
    args = [packed] + list(state)
    return pl.pallas_call(
        functools.partial(part_kernel, steps, first, last, heads, sizes),
        out_shape=outs,
        in_specs=[VMEM] * len(args),
        out_specs=[VMEM] * len(outs),
        scratch_shapes=scratch,
        compiler_params=pltpu.CompilerParams(vmem_limit_bytes=VMEM_LIMIT),
        cost_estimate=pl.CostEstimate(flops=jobs * PART_COST, bytes_accessed=1000, transcendentals=0),
        name="part",
    )(*args)


def join_kernel(zed, kept_ref, other_ref, *outs):
    z_me = lax.axis_index("z")
    tok = outs[0].shape[0]
    half = tok // 2
    for s, out in enumerate(outs):
        for late in range(2):
            here = pl.ds(pl.multiple_of((late * zed + peer(z_me, s, zed)) * half, half), half)
            both = kept_ref[here, :] + other_ref[here, :].astype(F32)
            out[late * half : (late + 1) * half, :] = both.astype(out.dtype)


def join(kept, other, zed):
    tok, two = kept.shape[0] // zed, kept.shape[1]
    outs = [jax.ShapeDtypeStruct((tok, two), F32 if s == 0 else BF16) for s in range(zed)]
    return pl.pallas_call(
        functools.partial(join_kernel, zed), out_shape=outs, in_specs=[VMEM] * 2, out_specs=[VMEM] * zed, name="join",
        compiler_params=pltpu.CompilerParams(vmem_limit_bytes=SMALL_LIMIT),
    )(kept, other)


def split_kernel(ref, *outs):
    rows = outs[0].shape[0]
    first = ref.shape[0] - rows * len(outs)
    for n, out in enumerate(outs):
        out[...] = ref[first + n * rows : first + (n + 1) * rows, :]


def split(value, pieces):
    rows, columns = value.shape
    one = jax.ShapeDtypeStruct((rows // 2 // pieces, columns), value.dtype)
    return pl.pallas_call(
        split_kernel,
        out_shape=[one] * pieces,
        in_specs=[VMEM],
        out_specs=[VMEM] * pieces,
        compiler_params=pltpu.CompilerParams(vmem_limit_bytes=SMALL_LIMIT),
        name="split",
    )(value)


def total_kernel(*refs):
    out = refs[-1]
    rows = out.shape[0]
    whole = [ref for ref in refs[:-1] if ref.shape[0] >= rows]
    pieces = [ref for ref in refs[:-1] if ref.shape[0] < rows]
    step = pieces[0].shape[0] if pieces else rows
    for at in range(0, rows, step):
        value = whole[0][at : at + step, :].astype(F32)
        for ref in whole[1:]:
            value = value + ref[at : at + step, :].astype(F32)
        for n, ref in enumerate(pieces):
            if n * step % rows == at:
                value = value + ref[...].astype(F32)
        out[at : at + step, :] = value.astype(out.dtype)


def total(values, rows):
    return pl.pallas_call(
        total_kernel,
        out_shape=jax.ShapeDtypeStruct((rows, values[0].shape[1]), BF16),
        in_specs=[VMEM] * len(values),
        out_specs=VMEM,
        compiler_params=pltpu.CompilerParams(vmem_limit_bytes=SMALL_LIMIT),
        name="total",
    )(*values)


def on_device(queries, keys_values, outputs, d_out, lse, doc_start):
    inner = lax.axis_size("inner")
    zed = lax.axis_size("z")
    heads = lse.shape[1]
    sizes = (inner, zed)
    tok, width = keys_values.shape[0], keys_values.shape[1] // 2
    rounds = query_rounds(inner)
    own = pack(queries, d_out, outputs, lse, doc_start, heads)
    swapped = swap_cores(keys_values)
    own, swapped = lax.optimization_barrier((own, swapped))
    chip = stack(own, swap_cores(own)) if any(len(steps) == 2 for steps in rounds) else None
    packs = [fetch(chip if len(steps) == 2 else own, steps) for steps in rounds]
    mine = [keys_values] + [fetch_z(keys_values, s) for s in range(1, zed)]
    far = list(range(zed - 1, 0, -1))
    arrived = stack(*[mine[s] for s in far])
    out = part((), own, [keys_values, swapped, arrived, swap_cores(arrived)], False, heads, sizes, tok, width)
    dq_parts = [out[0]]
    acc, state = out[1], list(out[2:])
    returned = []
    for steps, packed in zip(rounds, packs):
        last = steps == rounds[-1]
        out = part(steps, packed, state + [acc], last, heads, sizes, tok, width)
        returned.append(give_back(out[0], steps))
        acc = out[1]
    kept, sent = out[1:]
    joined = join(kept, swap_cores(sent), zed)
    dkv_parts = [joined[0]] + [give_back_z(joined[s], s) for s in range(zed - 1, 0, -1)]
    for steps, back in zip(rounds, returned):
        dq_parts.append(back)
        if len(steps) == 2:
            back, dkv_parts[2] = lax.optimization_barrier((back, dkv_parts[2]))
            dq_parts += [swap_cores(piece) for piece in split(back, PIECES)]
    d_queries = total(dq_parts, tok)
    return (d_queries, total(dkv_parts, tok))


def solution(mesh):
    inner, outer = mesh.shape["inner"], mesh.shape["outer"]
    split = Mesh(mesh.devices.reshape(inner, outer // 2, 2), ("inner", "z", "core"))
    rows = P(("inner", "z", "core"), None)
    return jax.shard_map(
        on_device,
        mesh=split,
        in_specs=(rows, rows, rows, rows, rows, P(("inner", "z", "core"))),
        out_specs=(rows, rows),
        check_vma=False,
    )
```

time: 41.1 us -> 36.9 us (0.90)
  local copies, waits for them, and re-layouts: 3.38 us -> 0.01 us
  starting transfers between devices: 18.1 us -> 16 us
  waiting for transfers between devices: 11.1 us -> 12.5 us
    unnamed x12 -> x2, local copies, waits for them, and re-layouts: 3.38 us -> 0.01 us
    ppermute x17 -> x18, starting transfers between devices: 18.1 us -> 16 us  [the longest x2 4.18 us: fetch(): lax.ppermute(value, ('inner', 'core'), inner_pairs(steps, lax.axis_size('...]
    ppermute x17 -> x18, waiting for transfers between devices: 11.1 us -> 12.5 us  [the longest x3 3.68 us: give_back_z(): lax.ppermute(value, 'z', [(z, peer(z, step, count)) for z in range(count)])]
    pallas_call x7 -> x9, Pallas kernels: 7.4 us -> 6.22 us  [the longest x3 4.71 us: part(): pl.pallas_call(functools.partial(part_kernel, steps, first, last, heads,...]
    pallas_call x1, Pallas kernels: 0.17 us -> 1.27 us  [pack(): pl.pallas_call(functools.partial(pack_kernel, heads), out_shape=jax.Shape...]
  transfers between devices with their start and end apart: 17 -> 18, of which waited for: 11 -> 11; matrix products, arithmetic and copies ran while one was open for 0% -> 0% of each run, Pallas kernels for 11% -> 15%
where the time goes in v3:
time: 36.9 us; the launch traced here: 36.8 us
  starting transfers between devices  16 us (43%)
  waiting for transfers between devices  12.5 us (34%)
  Pallas kernels  7.49 us (20%)
  between operations  0.75 us (2%)
    pallas_call x3, Pallas kernels, part(): pl.pallas_call(functools.partial(part_kernel, steps, first, last, heads,...  4.71 us
    ppermute x2, starting transfers between devices, fetch(): lax.ppermute(value, ('inner', 'core'), inner_pairs(steps, lax.axis_size('...  4.18 us
    ppermute x3, starting transfers between devices, fetch_z(): lax.ppermute(value, 'z', [(peer(z, step, count), z) for z in range(count)])  4.17 us
    ppermute x3, starting transfers between devices, give_back_z(): lax.ppermute(value, 'z', [(z, peer(z, step, count)) for z in range(count)])  3.85 us
    ppermute x3, waiting for transfers between devices, give_back_z(): lax.ppermute(value, 'z', [(z, peer(z, step, count)) for z in range(count)])  3.68 us
    ppermute x3, waiting for transfers between devices, fetch_z(): lax.ppermute(value, 'z', [(peer(z, step, count), z) for z in range(count)])  3.63 us
    ppermute x8, waiting for transfers between devices, swap_cores(): return lax.ppermute(value, 'core', [(0, 1), (1, 0)])  3.41 us
    ppermute x2, starting transfers between devices, give_back(): return lax.ppermute(value, ('inner', 'core'), [(b, a) for a, b in pairs])  2.42 us
  transfers between devices with their start and end apart: 18, of which 11 were waited for; matrix products, arithmetic and copies ran while one was open for 0% of the time, Pallas kernels for 15%

profile of v3, /device:TPU:0, one launch (start us, length us, event | category | flops | bytes accessed | tf_op | source)
XLA Modules:
  0.0 36.8 jit_solution(2808994736261502860)
XLA Ops:
  0.6 0.5 %collective-permute-start = (bf16[128,256]{1,0:T(8,128)(2,1)}, bf16[128,256]{1,0:T(8,128)(2,1)S(1)}, u32[]{:S(2)}, u32[]{:S(2)}) collective-permute-start(bf16[128,256]{1,0:T(8,128)(2,1)} %refs_1_.3), channel_id=1, source_target_pairs={{0,1},{1,0},{2,3},{3,2},{4,5},{5,4},{6,7},{7,6},{8,9},{9,8},{10,11... | collective-permute-start | bytes 196616 | tf_op jit(solution)/shard_map/ppermute | solution.py:62
  1.1 1.3 %pack.1.refs_0_ = bf16[1056,128]{1,0:T(8,128)(2,1)S(1)} custom-call(bf16[128,512]{1,0:T(8,128)(2,1)} %refs_0_.1, bf16[128,512]{1,0:T(8,128)(2,1)} %refs_1_.2, bf16[128,512]{1,0:T(8,128)(2,1)} %refs_2_.1, f32[4,128]{1,0:T(4,128)} %bitcast.2, s32[1,128]{1,0:T(1,128)} %bitcast.3), custom_call_target="tpu_custom_call" | custom-call | tf_op jit(solution)/shard_map/pack/pallas_call | solution.py:113
  2.6 1.5 %collective-permute-done.5.refs_1_ = bf16[1056,128]{1,0:T(8,128)(2,1)S(1)} collective-permute-done((bf16[1056,128]{1,0:T(8,128)(2,1)S(1)}, bf16[1056,128]{1,0:T(8,128)(2,1)S(1)}, u32[]{:S(2)}, u32[]{:S(2)}) %collective-permute-start.5) | collective-permute-done | bytes 270368 | tf_op jit(solution)/shard_map/ppermute | solution.py:62
  4.1 2.7 %collective-permute-start.6 = (bf16[2112,128]{1,0:T(8,128)(2,1)S(1)}, bf16[2112,128]{1,0:T(8,128)(2,1)S(1)}, u32[]{:S(2)}, u32[]{:S(2)}) collective-permute-start(bf16[2112,128]{1,0:T(8,128)(2,1)S(1)} %stack.3), channel_id=1, source_target_pairs={{8,0},{17,1},{0,8},{25,9},{24,16},{1,17},{16,24},{9,25},{10,2},{19... | collective-permute-start | bytes 1622024 | tf_op jit(solution)/shard_map/ppermute | solution.py:43
  6.8 2.6 %collective-permute-start.2 = (bf16[128,256]{1,0:T(8,128)(2,1)S(1)}, bf16[128,256]{1,0:T(8,128)(2,1)S(1)}, u32[]{:S(2)}, u32[]{:S(2)}) collective-permute-start(bf16[128,256]{1,0:T(8,128)(2,1)S(1)} %copy-done), channel_id=1, source_target_pairs={{4,0},{6,2},{0,4},{2,6},{5,1},{7,3},{1,5},{3,7},{12,8},{14,10},{8,... | collective-permute-start | bytes 196616 | tf_op jit(solution)/shard_map/ppermute | solution.py:53
  9.4 1.3 %collective-permute-start.1 = (bf16[128,256]{1,0:T(8,128)(2,1)S(1)}, bf16[128,256]{1,0:T(8,128)(2,1)S(1)}, u32[]{:S(2)}, u32[]{:S(2)}) collective-permute-start(bf16[128,256]{1,0:T(8,128)(2,1)S(1)} %copy-done), channel_id=1, source_target_pairs={{6,0},{4,2},{2,4},{0,6},{7,1},{5,3},{3,5},{1,7},{14,8},{12,10},{10... | collective-permute-start | bytes 196616 | tf_op jit(solution)/shard_map/ppermute | solution.py:53
  11.0 1.5 %collective-permute-start.8 = (bf16[1056,128]{1,0:T(8,128)(2,1)S(1)}, bf16[1056,128]{1,0:T(8,128)(2,1)S(1)}, u32[]{:S(2)}, u32[]{:S(2)}) collective-permute-start(bf16[1056,128]{1,0:T(8,128)(2,1)S(1)} %pack.1.refs_0_), channel_id=1, source_target_pairs={{24,0},{25,1},{16,8},{17,9},{8,16},{9,17},{0,24},{1,25},{26,2},{27... | collective-permute-start | bytes 811016 | tf_op jit(solution)/shard_map/ppermute | solution.py:43
  12.5 2.0 %collective-permute-done.2.refs_1_ = bf16[128,256]{1,0:T(8,128)(2,1)S(1)} collective-permute-done((bf16[128,256]{1,0:T(8,128)(2,1)S(1)}, bf16[128,256]{1,0:T(8,128)(2,1)S(1)}, u32[]{:S(2)}, u32[]{:S(2)}) %collective-permute-start.2) | collective-permute-done | bytes 65568 | tf_op jit(solution)/shard_map/ppermute | solution.py:53
  14.5 1.3 %collective-permute-done.1.refs_0_ = bf16[128,256]{1,0:T(8,128)(2,1)S(1)} collective-permute-done((bf16[128,256]{1,0:T(8,128)(2,1)S(1)}, bf16[128,256]{1,0:T(8,128)(2,1)S(1)}, u32[]{:S(2)}, u32[]{:S(2)}) %collective-permute-start.1) | collective-permute-done | bytes 65568 | tf_op jit(solution)/shard_map/ppermute | solution.py:53
  16.2 1.4 %collective-permute-done.4.refs_4_ = bf16[384,256]{1,0:T(8,128)(2,1)S(1)} collective-permute-done((bf16[384,256]{1,0:T(8,128)(2,1)S(1)}, bf16[384,256]{1,0:T(8,128)(2,1)S(1)}, u32[]{:S(2)}, u32[]{:S(2)}) %collective-permute-start.4) | collective-permute-done | bytes 196640 | tf_op jit(solution)/shard_map/ppermute | solution.py:62
  17.6 1.3 %part.3 = (f32[128,512]{1,0:T(8,128)S(1)}, f32[1024,256]{1,0:T(8,128)S(1)}, bf16[1024,128]{1,0:T(8,128)(2,1)S(1)}, bf16[1024,128]{1,0:T(8,128)(2,1)S(1)}, bf16[128,1024]{1,0:T(8,128)(2,1)S(1)}) custom-call(bf16[1056,128]{1,0:T(8,128)(2,1)S(1)} %pack.1.refs_0_, bf16[128,256]{1,0:T(8,128)(2,1)S(1)} %copy-done, ...), custom_call_target="tpu_custom_call" | custom-call | flops 200000000 | bytes 1000 | tf_op jit(solution)/shard_map/part/pallas_call | solution.py:294
  18.9 2.1 %part.4 = (bf16[256,512]{1,0:T(8,128)(2,1)S(1)}, f32[1024,256]{1,0:T(8,128)S(1)}) custom-call(bf16[2112,128]{1,0:T(8,128)(2,1)S(1)} %collective-permute-done.6.refs_0_, bf16[1024,128]{1,0:T(8,128)(2,1)S(1)} %get-tuple-element.27.refs_1_, bf16[1024,128]{1,0:T(8,128)(2,1)S(1)} %get-tuple-element.28.refs_2_, bf16[128,1024]{1,0:T(8,128)(2,1)S(1)} %get-tuple-element.29.refs_3_, ...), custom_call_target="tpu_custom_call" | custom-call | flops 400000000 | bytes 1000 | tf_op jit(solution)/shard_map/part/pallas_call | solution.py:294
  21.4 1.3 %part.5 = (bf16[128,512]{1,0:T(8,128)(2,1)S(1)}, f32[512,256]{1,0:T(8,128)S(1)}, bf16[512,256]{1,0:T(8,128)(2,1)S(1)}) custom-call(bf16[1056,128]{1,0:T(8,128)(2,1)S(1)} %collective-permute-done.8.refs_0_, bf16[1024,128]{1,0:T(8,128)(2,1)S(1)} %get-tuple-element.27.refs_1_, bf16[1024,128]{1,0:T(8,128)(2,1)S(1)} %get-tuple-element.28.refs_2_, ...), custom_call_target="tpu_custom_call" | custom-call | flops 200000000 | bytes 1000 | tf_op jit(solution)/shard_map/part/pallas_call | solution.py:294
  22.8 1.6 %collective-permute-start.7 = (bf16[256,512]{1,0:T(8,128)(2,1)S(1)}, bf16[256,512]{1,0:T(8,128)(2,1)S(1)}, u32[]{:S(2)}, u32[]{:S(2)}) collective-permute-start(bf16[256,512]{1,0:T(8,128)(2,1)S(1)} %get-tuple-element.31), channel_id=1, source_target_pairs={{0,8},{1,17},{8,0},{9,25},{16,24},{17,1},{24,16},{25,9},{2,10},{3,... | collective-permute-start | bytes 786440 | tf_op jit(solution)/shard_map/ppermute | solution.py:48
  24.3 0.9 %collective-permute-start.15 = (bf16[128,512]{1,0:T(8,128)(2,1)S(1)}, bf16[128,512]{1,0:T(8,128)(2,1)S(1)}, u32[]{:S(2)}, u32[]{:S(2)}) collective-permute-start(bf16[128,512]{1,0:T(8,128)(2,1)S(1)} %get-tuple-element.41), channel_id=1, source_target_pairs={{0,24},{1,25},{8,16},{9,17},{16,8},{17,9},{24,0},{25,1},{2,26},{3,... | collective-permute-start | bytes 393224 | tf_op jit(solution)/shard_map/ppermute | solution.py:48
  25.2 2.3 %collective-permute-start.10 = (bf16[128,256]{1,0:T(8,128)(2,1)S(1)}, bf16[128,256]{1,0:T(8,128)(2,1)S(1)}, u32[]{:S(2)}, u32[]{:S(2)}) collective-permute-start(bf16[128,256]{1,0:T(8,128)(2,1)S(1)} %get-tuple-element.35), channel_id=1, source_target_pairs={{0,4},{2,6},{4,0},{6,2},{1,5},{3,7},{5,1},{7,3},{8,12},{10,14},{12... | collective-permute-start | bytes 196616 | tf_op jit(solution)/shard_map/ppermute | solution.py:58
  27.5 1.4 %collective-permute-start.16 = (bf16[128,256]{1,0:T(8,128)(2,1)S(1)}, bf16[128,256]{1,0:T(8,128)(2,1)S(1)}, u32[]{:S(2)}, u32[]{:S(2)}) collective-permute-start(bf16[128,256]{1,0:T(8,128)(2,1)S(1)} %get-tuple-element.43), channel_id=1, source_target_pairs={{0,6},{2,4},{4,2},{6,0},{1,7},{3,5},{5,3},{7,1},{8,14},{10,12},{12... | collective-permute-start | bytes 196616 | tf_op jit(solution)/shard_map/ppermute | solution.py:58
  29.1 1.5 %collective-permute-done.7.ref.refs_1_ = bf16[256,512]{1,0:T(8,128)(2,1)S(1)} collective-permute-done((bf16[256,512]{1,0:T(8,128)(2,1)S(1)}, bf16[256,512]{1,0:T(8,128)(2,1)S(1)}, u32[]{:S(2)}, u32[]{:S(2)}) %collective-permute-start.7) | collective-permute-done | bytes 262176 | tf_op jit(solution)/shard_map/ppermute | solution.py:48
  30.6 1.7 %collective-permute-done.10.refs_2_ = bf16[128,256]{1,0:T(8,128)(2,1)S(1)} collective-permute-done((bf16[128,256]{1,0:T(8,128)(2,1)S(1)}, bf16[128,256]{1,0:T(8,128)(2,1)S(1)}, u32[]{:S(2)}, u32[]{:S(2)}) %collective-permute-start.10) | collective-permute-done | bytes 65568 | tf_op jit(solution)/shard_map/ppermute | solution.py:58
  32.9 1.3 %collective-permute-done.16.refs_1_ = bf16[128,256]{1,0:T(8,128)(2,1)S(1)} collective-permute-done((bf16[128,256]{1,0:T(8,128)(2,1)S(1)}, bf16[128,256]{1,0:T(8,128)(2,1)S(1)}, u32[]{:S(2)}, u32[]{:S(2)}) %collective-permute-start.16) | collective-permute-done | bytes 65568 | tf_op jit(solution)/shard_map/ppermute | solution.py:58
  34.2 0.6 %collective-permute-done.17.refs_3_ = bf16[128,256]{1,0:T(8,128)(2,1)S(1)} collective-permute-done((bf16[128,256]{1,0:T(8,128)(2,1)S(1)}, bf16[128,256]{1,0:T(8,128)(2,1)S(1)}, u32[]{:S(2)}, u32[]{:S(2)}) %collective-permute-start.17) | collective-permute-done | bytes 65568 | tf_op jit(solution)/shard_map/ppermute | solution.py:58
  34.9 0.7 %total.3 = bf16[128,256]{1,0:T(8,128)(2,1)} custom-call(f32[128,256]{1,0:T(8,128)S(1)} %get-tuple-element.42.refs_0_, bf16[128,256]{1,0:T(8,128)(2,1)S(1)} %collective-permute-done.16.refs_1_, bf16[128,256]{1,0:T(8,128)(2,1)S(1)} %collective-permute-done.10.refs_2_, bf16[128,256]{1,0:T(8,128)(2,1)S(1)} %collective-permute-done.17.refs_3_), custom_call_target="tpu_custom_call" | custom-call | tf_op jit(solution)/shard_map/total/pallas_call | solution.py:363
  35.6 0.5 %collective-permute-done.14.refs_5_ = bf16[32,512]{1,0:T(8,128)(2,1)S(1)} collective-permute-done((bf16[32,512]{1,0:T(8,128)(2,1)S(1)}, bf16[32,512]{1,0:T(8,128)(2,1)S(1)}, u32[]{:S(2)}, u32[]{:S(2)}) %collective-permute-start.14) | collective-permute-done | bytes 32800 | tf_op jit(solution)/shard_map/ppermute | solution.py:62
  36.1 0.7 %total.2 = bf16[128,512]{1,0:T(8,128)(2,1)} custom-call(f32[128,512]{1,0:T(8,128)S(1)} %get-tuple-element.26.refs_0_, bf16[256,512]{1,0:T(8,128)(2,1)S(1)} %collective-permute-done.7.ref.refs_1_, bf16[32,512]{1,0:T(8,128)(2,1)S(1)} %collective-permute-done.11.refs_2_, bf16[32,512]{1,0:T(8,128)(2,1)S(1)} %collective-permute-done.12.refs_3_, ...), custom_call_target="tpu_custom_call" | custom-call | tf_op jit(solution)/shard_map/total/pallas_call | solution.py:363
  (24 shorter events, 2.1 us)
Async XLA Ops:
  0.6 1.8 %collective-permute-start = (bf16[128,256]{1,0:T(8,128)(2,1)}, bf16[128,256]{1,0:T(8,128)(2,1)S(1)}, u32[]{:S(2)}, u32[]{:S(2)}) collective-permute-start(bf16[128,256]{1,0:T(8,128)(2,1)} %refs_1_.3), channel_id=1, source_target_pairs={{0,1},{1,0},{2,3},{3,2},{4,5},{5,4},{6,7},{7,6},{8,9},{9,8},{10,11... | collective-permute-start | bytes 196616 | tf_op jit(solution)/shard_map/ppermute | solution.py:62
  2.4 4.4 %copy-start = (bf16[128,256]{1,0:T(8,128)(2,1)S(1)}, bf16[128,256]{1,0:T(8,128)(2,1)}, u32[]{:S(2)}) copy-start(bf16[128,256]{1,0:T(8,128)(2,1)} %refs_1_.3) | copy-start | bytes 196612
  2.5 1.6 %collective-permute-start.5 = (bf16[1056,128]{1,0:T(8,128)(2,1)S(1)}, bf16[1056,128]{1,0:T(8,128)(2,1)S(1)}, u32[]{:S(2)}, u32[]{:S(2)}) collective-permute-start(bf16[1056,128]{1,0:T(8,128)(2,1)S(1)} %pack.1.refs_0_), channel_id=1, source_target_pairs={{0,1},{1,0},{2,3},{3,2},{4,5},{5,4},{6,7},{7,6},{8,9},{9,8},{10,11... | collective-permute-start | bytes 811016 | tf_op jit(solution)/shard_map/ppermute | solution.py:62
  4.1 14.8 %collective-permute-start.6 = (bf16[2112,128]{1,0:T(8,128)(2,1)S(1)}, bf16[2112,128]{1,0:T(8,128)(2,1)S(1)}, u32[]{:S(2)}, u32[]{:S(2)}) collective-permute-start(bf16[2112,128]{1,0:T(8,128)(2,1)S(1)} %stack.3), channel_id=1, source_target_pairs={{8,0},{17,1},{0,8},{25,9},{24,16},{1,17},{16,24},{9,25},{10,2},{19... | collective-permute-start | bytes 1622024 | tf_op jit(solution)/shard_map/ppermute | solution.py:43
  6.8 7.7 %collective-permute-start.2 = (bf16[128,256]{1,0:T(8,128)(2,1)S(1)}, bf16[128,256]{1,0:T(8,128)(2,1)S(1)}, u32[]{:S(2)}, u32[]{:S(2)}) collective-permute-start(bf16[128,256]{1,0:T(8,128)(2,1)S(1)} %copy-done), channel_id=1, source_target_pairs={{4,0},{6,2},{0,4},{2,6},{5,1},{7,3},{1,5},{3,7},{12,8},{14,10},{8,... | collective-permute-start | bytes 196616 | tf_op jit(solution)/shard_map/ppermute | solution.py:53
  9.4 6.4 %collective-permute-start.1 = (bf16[128,256]{1,0:T(8,128)(2,1)S(1)}, bf16[128,256]{1,0:T(8,128)(2,1)S(1)}, u32[]{:S(2)}, u32[]{:S(2)}) collective-permute-start(bf16[128,256]{1,0:T(8,128)(2,1)S(1)} %copy-done), channel_id=1, source_target_pairs={{6,0},{4,2},{2,4},{0,6},{7,1},{5,3},{3,5},{1,7},{14,8},{12,10},{10... | collective-permute-start | bytes 196616 | tf_op jit(solution)/shard_map/ppermute | solution.py:53
  10.7 5.4 %collective-permute-start.3 = (bf16[128,256]{1,0:T(8,128)(2,1)S(1)}, bf16[128,256]{1,0:T(8,128)(2,1)S(1)}, u32[]{:S(2)}, u32[]{:S(2)}) collective-permute-start(bf16[128,256]{1,0:T(8,128)(2,1)S(1)} %copy-done), channel_id=1, source_target_pairs={{2,0},{0,2},{6,4},{4,6},{3,1},{1,3},{7,5},{5,7},{10,8},{8,10},{14,... | collective-permute-start | bytes 196616 | tf_op jit(solution)/shard_map/ppermute | solution.py:53
  11.0 10.4 %collective-permute-start.8 = (bf16[1056,128]{1,0:T(8,128)(2,1)S(1)}, bf16[1056,128]{1,0:T(8,128)(2,1)S(1)}, u32[]{:S(2)}, u32[]{:S(2)}) collective-permute-start(bf16[1056,128]{1,0:T(8,128)(2,1)S(1)} %pack.1.refs_0_), channel_id=1, source_target_pairs={{24,0},{25,1},{16,8},{17,9},{8,16},{9,17},{0,24},{1,25},{26,2},{27... | collective-permute-start | bytes 811016 | tf_op jit(solution)/shard_map/ppermute | solution.py:43
  16.1 1.5 %collective-permute-start.4 = (bf16[384,256]{1,0:T(8,128)(2,1)S(1)}, bf16[384,256]{1,0:T(8,128)(2,1)S(1)}, u32[]{:S(2)}, u32[]{:S(2)}) collective-permute-start(bf16[384,256]{1,0:T(8,128)(2,1)S(1)} %stack.2.refs_3_), channel_id=1, source_target_pairs={{0,1},{1,0},{2,3},{3,2},{4,5},{5,4},{6,7},{7,6},{8,9},{9,8},{10,11... | collective-permute-start | bytes 589832 | tf_op jit(solution)/shard_map/ppermute | solution.py:62
  22.7 2.5 %collective-permute-start.9 = (bf16[512,256]{1,0:T(8,128)(2,1)S(1)}, bf16[512,256]{1,0:T(8,128)(2,1)S(1)}, u32[]{:S(2)}, u32[]{:S(2)}) collective-permute-start(bf16[512,256]{1,0:T(8,128)(2,1)S(1)} %get-tuple-element.34), channel_id=1, source_target_pairs={{0,1},{1,0},{2,3},{3,2},{4,5},{5,4},{6,7},{7,6},{8,9},{9,8},{10,11... | collective-permute-start | bytes 786440 | tf_op jit(solution)/shard_map/ppermute | solution.py:62
  22.8 7.8 %collective-permute-start.7 = (bf16[256,512]{1,0:T(8,128)(2,1)S(1)}, bf16[256,512]{1,0:T(8,128)(2,1)S(1)}, u32[]{:S(2)}, u32[]{:S(2)}) collective-permute-start(bf16[256,512]{1,0:T(8,128)(2,1)S(1)} %get-tuple-element.31), channel_id=1, source_target_pairs={{0,8},{1,17},{8,0},{9,25},{16,24},{17,1},{24,16},{25,9},{2,10},{3,... | collective-permute-start | bytes 786440 | tf_op jit(solution)/shard_map/ppermute | solution.py:48
  24.3 11.2 %collective-permute-start.15 = (bf16[128,512]{1,0:T(8,128)(2,1)S(1)}, bf16[128,512]{1,0:T(8,128)(2,1)S(1)}, u32[]{:S(2)}, u32[]{:S(2)}) collective-permute-start(bf16[128,512]{1,0:T(8,128)(2,1)S(1)} %get-tuple-element.41), channel_id=1, source_target_pairs={{0,24},{1,25},{8,16},{9,17},{16,8},{17,9},{24,0},{25,1},{2,26},{3,... | collective-permute-start | bytes 393224 | tf_op jit(solution)/shard_map/ppermute | solution.py:48
  25.2 7.1 %collective-permute-start.10 = (bf16[128,256]{1,0:T(8,128)(2,1)S(1)}, bf16[128,256]{1,0:T(8,128)(2,1)S(1)}, u32[]{:S(2)}, u32[]{:S(2)}) collective-permute-start(bf16[128,256]{1,0:T(8,128)(2,1)S(1)} %get-tuple-element.35), channel_id=1, source_target_pairs={{0,4},{2,6},{4,0},{6,2},{1,5},{3,7},{5,1},{7,3},{8,12},{10,14},{12... | collective-permute-start | bytes 196616 | tf_op jit(solution)/shard_map/ppermute | solution.py:58
  27.5 6.7 %collective-permute-start.16 = (bf16[128,256]{1,0:T(8,128)(2,1)S(1)}, bf16[128,256]{1,0:T(8,128)(2,1)S(1)}, u32[]{:S(2)}, u32[]{:S(2)}) collective-permute-start(bf16[128,256]{1,0:T(8,128)(2,1)S(1)} %get-tuple-element.43), channel_id=1, source_target_pairs={{0,6},{2,4},{4,2},{6,0},{1,7},{3,5},{5,3},{7,1},{8,14},{10,12},{12... | collective-permute-start | bytes 196616 | tf_op jit(solution)/shard_map/ppermute | solution.py:58
  28.9 6.0 %collective-permute-start.17 = (bf16[128,256]{1,0:T(8,128)(2,1)S(1)}, bf16[128,256]{1,0:T(8,128)(2,1)S(1)}, u32[]{:S(2)}, u32[]{:S(2)}) collective-permute-start(bf16[128,256]{1,0:T(8,128)(2,1)S(1)} %get-tuple-element.45), channel_id=1, source_target_pairs={{0,2},{2,0},{4,6},{6,4},{1,3},{3,1},{5,7},{7,5},{8,10},{10,8},{12,... | collective-permute-start | bytes 196616 | tf_op jit(solution)/shard_map/ppermute | solution.py:58
  32.3 3.2 %collective-permute-start.11 = (bf16[32,512]{1,0:T(8,128)(2,1)S(1)}, bf16[32,512]{1,0:T(8,128)(2,1)S(1)}, u32[]{:S(2)}, u32[]{:S(2)}) collective-permute-start(bf16[32,512]{1,0:T(8,128)(2,1)S(1)} %get-tuple-element.37), channel_id=1, source_target_pairs={{0,1},{1,0},{2,3},{3,2},{4,5},{5,4},{6,7},{7,6},{8,9},{9,8},{10,11... | collective-permute-start | bytes 98312 | tf_op jit(solution)/shard_map/ppermute | solution.py:62
  32.4 3.1 %collective-permute-start.12 = (bf16[32,512]{1,0:T(8,128)(2,1)S(1)}, bf16[32,512]{1,0:T(8,128)(2,1)S(1)}, u32[]{:S(2)}, u32[]{:S(2)}) collective-permute-start(bf16[32,512]{1,0:T(8,128)(2,1)S(1)} %get-tuple-element.38), channel_id=1, source_target_pairs={{0,1},{1,0},{2,3},{3,2},{4,5},{5,4},{6,7},{7,6},{8,9},{9,8},{10,11... | collective-permute-start | bytes 98312 | tf_op jit(solution)/shard_map/ppermute | solution.py:62
  34.2 1.3 %collective-permute-start.13 = (bf16[32,512]{1,0:T(8,128)(2,1)S(1)}, bf16[32,512]{1,0:T(8,128)(2,1)S(1)}, u32[]{:S(2)}, u32[]{:S(2)}) collective-permute-start(bf16[32,512]{1,0:T(8,128)(2,1)S(1)} %get-tuple-element.39), channel_id=1, source_target_pairs={{0,1},{1,0},{2,3},{3,2},{4,5},{5,4},{6,7},{7,6},{8,9},{9,8},{10,11... | collective-permute-start | bytes 98312 | tf_op jit(solution)/shard_map/ppermute | solution.py:62
  34.9 1.2 %collective-permute-start.14 = (bf16[32,512]{1,0:T(8,128)(2,1)S(1)}, bf16[32,512]{1,0:T(8,128)(2,1)S(1)}, u32[]{:S(2)}, u32[]{:S(2)}) collective-permute-start(bf16[32,512]{1,0:T(8,128)(2,1)S(1)} %get-tuple-element.40), channel_id=1, source_target_pairs={{0,1},{1,0},{2,3},{3,2},{4,5},{5,4},{6,7},{7,6},{8,9},{9,8},{10,11... | collective-permute-start | bytes 98312 | tf_op jit(solution)/shard_map/ppermute | solution.py:62

commit v4 on v3

--- a/solution.py
+++ b/solution.py
@@ -12,7 +12,7 @@
 LOG2E = math.log2(math.e)
 STATS = 8
 PIECES = 4
-PART_COST = 200000000
+PART_COST = 1000
 VMEM_LIMIT = 32 * 1024 * 1024
 SMALL_LIMIT = 8 * 1024 * 1024
 BF16 = jnp.bfloat16
@@ -69,14 +69,7 @@
     return [high, middle, rest - middle]
 
 
-def pack_kernel(heads, *refs):
-    sources, pack_ref, places, arrived = refs[:5], refs[5], refs[6:11], refs[11]
-    copies = [pltpu.make_async_copy(a, b, arrived.at[i]) for i, (a, b) in enumerate(zip(sources, places))]
-    for copy in copies:
-        copy.start()
-    for copy in copies:
-        copy.wait()
-    q_ref, g_ref, o_ref, lse_ref, start_ref = places
+def pack_rows(heads, q_ref, g_ref, o_ref, lse_ref, start_ref, pack_ref, base):
     tok = q_ref.shape[0]
     width = q_ref.shape[1] // heads
     half = tok // 2
@@ -90,7 +83,7 @@
         for h in range(heads):
             cols = slice(h * width, (h + 1) * width)
             q, g = q_ref[here, cols], g_ref[here, cols]
-            first = late * lanes + h * half
+            first = base + late * lanes + h * half
             pack_ref[first : first + half, :] = q
             pack_ref[2 * lanes + first : 2 * lanes + first + half, :] = g
             products.append(g.astype(F32) * o_ref[here, cols].astype(F32))
@@ -101,24 +94,54 @@
         stats += [(start >> 8).astype(F32), (start & 255).astype(F32)]
         for value in stats:
             rows += [value[:, c : c + width] for c in range(0, lanes, width)]
-    pack_ref[4 * lanes :, :] = jnp.concatenate(rows, axis=0).astype(BF16)
-
-
-def pack(queries, d_out, outputs, lse, doc_start, heads):
-    tok = queries.shape[0]
-    width = queries.shape[1] // heads
-    stat_rows = STATS * heads * tok // width
-    args = (queries, d_out, outputs, lse.T, doc_start.reshape(1, tok))
+    first = base + 4 * lanes
+    pack_ref[first : first + len(rows), :] = jnp.concatenate(rows, axis=0).astype(BF16)
+
+
+def pack_kernel(heads, *refs):
+    sources, pack_ref, places, arrived = refs[:5], refs[5], refs[6:11], refs[11]
+    copies = [pltpu.make_async_copy(a, b, arrived.at[i]) for i, (a, b) in enumerate(zip(sources, places))]
+    for copy in copies:
+        copy.start()
+    for copy in copies:
+        copy.wait()
+    pack_rows(heads, *places, pack_ref, 0)
+
+
+def rows_packed(heads, queries):
+    tok, columns = queries.shape
+    return 2 * heads * tok + STATS * heads * tok // (columns // heads)
+
+
+def pack(heads, args):
     args = [pltpu.with_memory_space_constraint(a, pltpu.HBM) for a in args]
     return pl.pallas_call(
         functools.partial(pack_kernel, heads),
-        out_shape=jax.ShapeDtypeStruct((2 * heads * tok + stat_rows, width), BF16),
+        out_shape=jax.ShapeDtypeStruct((rows_packed(heads, args[0]), args[0].shape[1] // heads), BF16),
         in_specs=[pl.BlockSpec(memory_space=pltpu.HBM)] * 5,
         out_specs=VMEM,
         scratch_shapes=[pltpu.VMEM(a.shape, a.dtype) for a in args] + [pltpu.SemaphoreType.DMA((5,))],
         compiler_params=pltpu.CompilerParams(vmem_limit_bytes=SMALL_LIMIT),
         name="pack",
     )(*args)
+
+
+def pack_chip_kernel(heads, *refs):
+    own_ref, pack_ref = refs[0], refs[-1]
+    rows = own_ref.shape[0]
+    pack_ref[:rows, :] = own_ref[...]
+    pack_rows(heads, *refs[1:6], pack_ref, rows)
+
+
+def pack_chip(heads, own, args):
+    return pl.pallas_call(
+        functools.partial(pack_chip_kernel, heads),
+        out_shape=jax.ShapeDtypeStruct((2 * own.shape[0], own.shape[1]), BF16),
+        in_specs=[VMEM] * 6,
+        out_specs=VMEM,
+        compiler_params=pltpu.CompilerParams(vmem_limit_bytes=SMALL_LIMIT),
+        name="pack_chip",
+    )(own, *args)
 
 
 def stack_kernel(*refs):
@@ -144,7 +167,7 @@
     inner, zed = sizes
     pack_ref, refs = refs[0], refs[1:]
     if first:
-        blocks, refs = refs[:4], refs[4:]
+        blocks, refs = refs[:2], refs[2:]
         dq_ref, acc_ref, k_ref, v_ref, kt_ref, dqt_ref = refs
     elif last:
         k_ref, v_ref, kt_ref, acc_in, dq_ref, kept_ref, sent_ref, dqt_ref, acc_ref = refs
@@ -170,9 +193,8 @@
 
     if first:
         for n, block in enumerate(blocks):
-            steps_here = [0] if n < 2 else range(zed - 1, 0, -1)
-            for m, s in enumerate(steps_here):
-                source = 2 * peer(z_me, s, zed) + (1 - core if n % 2 else core)
+            for m, s in enumerate(range(zed - 1, -1, -1)):
+                source = 2 * peer(z_me, s, zed) + (1 - core if n else core)
                 for late in range(2):
                     here = pl.ds(pl.multiple_of(late * front + source * half, half), half)
                     rows = slice(m * tok + late * half, m * tok + (late + 1) * half)
@@ -343,11 +365,10 @@
     )(value)
 
 
-def total_kernel(*refs):
-    out = refs[-1]
+def add_up(out, refs):
     rows = out.shape[0]
-    whole = [ref for ref in refs[:-1] if ref.shape[0] >= rows]
-    pieces = [ref for ref in refs[:-1] if ref.shape[0] < rows]
+    whole = [ref for ref in refs if ref.shape[0] >= rows]
+    pieces = [ref for ref in refs if ref.shape[0] < rows]
     step = pieces[0].shape[0] if pieces else rows
     for at in range(0, rows, step):
         value = whole[0][at : at + step, :].astype(F32)
@@ -359,15 +380,23 @@
         out[at : at + step, :] = value.astype(out.dtype)
 
 
-def total(values, rows):
-    return pl.pallas_call(
-        total_kernel,
-        out_shape=jax.ShapeDtypeStruct((rows, values[0].shape[1]), BF16),
-        in_specs=[VMEM] * len(values),
-        out_specs=VMEM,
-        compiler_params=pltpu.CompilerParams(vmem_limit_bytes=SMALL_LIMIT),
-        name="total",
-    )(*values)
+def totals_kernel(counts, *refs):
+    first = 0
+    for count, out in zip(counts, refs[sum(counts) :]):
+        add_up(out, refs[first : first + count])
+        first += count
+
+
+def totals(groups, rows):
+    args = [value for values in groups for value in values]
+    return pl.pallas_call(
+        functools.partial(totals_kernel, [len(values) for values in groups]),
+        out_shape=[jax.ShapeDtypeStruct((rows, values[0].shape[1]), BF16) for values in groups],
+        in_specs=[VMEM] * len(args),
+        out_specs=[VMEM] * len(groups),
+        compiler_params=pltpu.CompilerParams(vmem_limit_bytes=SMALL_LIMIT),
+        name="totals",
+    )(*args)
 
 
 def on_device(queries, keys_values, outputs, d_out, lse, doc_start):
@@ -377,15 +406,16 @@
     sizes = (inner, zed)
     tok, width = keys_values.shape[0], keys_values.shape[1] // 2
     rounds = query_rounds(inner)
-    own = pack(queries, d_out, outputs, lse, doc_start, heads)
-    swapped = swap_cores(keys_values)
-    own, swapped = lax.optimization_barrier((own, swapped))
-    chip = stack(own, swap_cores(own)) if any(len(steps) == 2 for steps in rounds) else None
+    inputs = (queries, d_out, outputs, lse.T, doc_start.reshape(1, tok))
+    own = pack(heads, inputs)
+    chip = None
+    if any(len(steps) == 2 for steps in rounds):
+        chip = pack_chip(heads, own, [swap_cores(value) for value in inputs])
     packs = [fetch(chip if len(steps) == 2 else own, steps) for steps in rounds]
     mine = [keys_values] + [fetch_z(keys_values, s) for s in range(1, zed)]
-    far = list(range(zed - 1, 0, -1))
+    far = list(range(zed - 1, -1, -1))
     arrived = stack(*[mine[s] for s in far])
-    out = part((), own, [keys_values, swapped, arrived, swap_cores(arrived)], False, heads, sizes, tok, width)
+    out = part((), own, [arrived, swap_cores(arrived)], False, heads, sizes, tok, width)
     dq_parts = [out[0]]
     acc, state = out[1], list(out[2:])
     returned = []
@@ -402,8 +432,7 @@
         if len(steps) == 2:
             back, dkv_parts[2] = lax.optimization_barrier((back, dkv_parts[2]))
             dq_parts += [swap_cores(piece) for piece in split(back, PIECES)]
-    d_queries = total(dq_parts, tok)
-    return (d_queries, total(dkv_parts, tok))
+    return tuple(totals([dq_parts, dkv_parts], tok))
 
 
 def solution(mesh):

time: 36.9 us -> 36.5 us (0.989)
  waiting for transfers between devices: 12.5 us -> 11 us
  starting transfers between devices: 16 us -> 16.9 us
  local copies, waits for them, and re-layouts: 0.01 us -> 0.58 us
  Pallas kernels: 7.49 us -> 7.03 us
    ppermute x8 -> x11, waiting for transfers between devices: 3.41 us -> 2.1 us  [swap_cores(): return lax.ppermute(value, 'core', [(0, 1), (1, 0)])]
    ppermute x8 -> x11, starting transfers between devices: 1.39 us -> 1.98 us  [swap_cores(): return lax.ppermute(value, 'core', [(0, 1), (1, 0)])]
    unnamed x2 -> x4, local copies, waits for them, and re-layouts: 0.01 us -> 0.58 us
    pallas_call x2, Pallas kernels: 1.38 us -> 0.92 us  [the longest x1 0.74 us: totals(): pl.pallas_call(functools.partial(totals_kernel, [len(values) for values i...]
    ppermute x3, waiting for transfers between devices: 3.63 us -> 3.24 us  [fetch_z(): lax.ppermute(value, 'z', [(peer(z, step, count), z) for z in range(count)])]
  transfers between devices with their start and end apart: 18 -> 21, of which waited for: 11 -> 10; matrix products, arithmetic and copies ran while one was open for 0% -> 0% of each run, Pallas kernels for 15% -> 13%
where the time goes in v4:
time: 36.5 us; the launch traced here: 36.3 us
  starting transfers between devices  16.9 us (46%)
  waiting for transfers between devices  11 us (30%)
  Pallas kernels  7.03 us (19%)
  between operations  0.78 us (2%)
  local copies, waits for them, and re-layouts  0.58 us (2%)
    pallas_call x3, Pallas kernels, part(): pl.pallas_call(functools.partial(part_kernel, steps, first, last, heads,...  4.74 us
    ppermute x2, starting transfers between devices, fetch(): lax.ppermute(value, ('inner', 'core'), inner_pairs(steps, lax.axis_size('...  4.47 us
    ppermute x3, starting transfers between devices, fetch_z(): lax.ppermute(value, 'z', [(peer(z, step, count), z) for z in range(count)])  4.17 us
    ppermute x3, starting transfers between devices, give_back_z(): lax.ppermute(value, 'z', [(z, peer(z, step, count)) for z in range(count)])  3.73 us
    ppermute x3, waiting for transfers between devices, give_back_z(): lax.ppermute(value, 'z', [(z, peer(z, step, count)) for z in range(count)])  3.59 us
    ppermute x3, waiting for transfers between devices, fetch_z(): lax.ppermute(value, 'z', [(peer(z, step, count), z) for z in range(count)])  3.24 us
    ppermute x2, starting transfers between devices, give_back(): return lax.ppermute(value, ('inner', 'core'), [(b, a) for a, b in pairs])  2.53 us
    ppermute x11, waiting for transfers between devices, swap_cores(): return lax.ppermute(value, 'core', [(0, 1), (1, 0)])  2.1 us
  transfers between devices with their start and end apart: 21, of which 10 were waited for; matrix products, arithmetic and copies ran while one was open for 0% of the time, Pallas kernels for 13%

profile of v4, /device:TPU:0, one launch (start us, length us, event | category | flops | bytes accessed | tf_op | source)
XLA Modules:
  0.0 36.3 jit_solution(6813488395043125535)
XLA Ops:
  0.6 0.5 %collective-permute-start.4 = (bf16[128,512]{1,0:T(8,128)(2,1)}, bf16[128,512]{1,0:T(8,128)(2,1)S(1)}, u32[]{:S(2)}, u32[]{:S(2)}) collective-permute-start(bf16[128,512]{1,0:T(8,128)(2,1)} %refs_0_.1), channel_id=1, source_target_pairs={{0,1},{1,0},{2,3},{3,2},{4,5},{5,4},{6,7},{7,6},{8,9},{9,8},{10,11... | collective-permute-start | bytes 393224 | tf_op jit(solution)/shard_map/ppermute | solution.py:62
  1.7 0.6 %copy-done.1 = s32[128]{0:T(128)S(1)} copy-done((s32[128]{0:T(128)S(1)}, s32[128]{0:T(128)}, u32[]{:S(2)}) %copy-start.1) | copy-done | bytes 536
  2.4 1.3 %pack.1.refs_0_ = bf16[1056,128]{1,0:T(8,128)(2,1)S(1)} custom-call(bf16[128,512]{1,0:T(8,128)(2,1)} %refs_0_.1, bf16[128,512]{1,0:T(8,128)(2,1)} %refs_1_.1, bf16[128,512]{1,0:T(8,128)(2,1)} %refs_2_.1, f32[4,128]{1,0:T(4,128)} %bitcast.3, s32[1,128]{1,0:T(1,128)} %bitcast.4), custom_call_target="tpu_custom_call" | custom-call | tf_op jit(solution)/shard_map/pack/pallas_call | solution.py:118
  3.9 3.0 %collective-permute-start.9 = (bf16[2112,128]{1,0:T(8,128)(2,1)S(1)}, bf16[2112,128]{1,0:T(8,128)(2,1)S(1)}, u32[]{:S(2)}, u32[]{:S(2)}) collective-permute-start(bf16[2112,128]{1,0:T(8,128)(2,1)S(1)} %pack_chip.1), channel_id=1, source_target_pairs={{8,0},{17,1},{0,8},{25,9},{24,16},{1,17},{16,24},{9,25},{10,2},{19... | collective-permute-start | bytes 1622024 | tf_op jit(solution)/shard_map/ppermute | solution.py:43
  6.9 2.6 %collective-permute-start.1 = (bf16[128,256]{1,0:T(8,128)(2,1)S(1)}, bf16[128,256]{1,0:T(8,128)(2,1)S(1)}, u32[]{:S(2)}, u32[]{:S(2)}) collective-permute-start(bf16[128,256]{1,0:T(8,128)(2,1)S(1)} %copy-done), channel_id=1, source_target_pairs={{4,0},{6,2},{0,4},{2,6},{5,1},{7,3},{1,5},{3,7},{12,8},{14,10},{8,... | collective-permute-start | bytes 196616 | tf_op jit(solution)/shard_map/ppermute | solution.py:53
  9.5 1.3 %collective-permute-start = (bf16[128,256]{1,0:T(8,128)(2,1)S(1)}, bf16[128,256]{1,0:T(8,128)(2,1)S(1)}, u32[]{:S(2)}, u32[]{:S(2)}) collective-permute-start(bf16[128,256]{1,0:T(8,128)(2,1)S(1)} %copy-done), channel_id=1, source_target_pairs={{6,0},{4,2},{2,4},{0,6},{7,1},{5,3},{3,5},{1,7},{14,8},{12,10},{10... | collective-permute-start | bytes 196616 | tf_op jit(solution)/shard_map/ppermute | solution.py:53
  11.1 1.5 %collective-permute-start.11 = (bf16[1056,128]{1,0:T(8,128)(2,1)S(1)}, bf16[1056,128]{1,0:T(8,128)(2,1)S(1)}, u32[]{:S(2)}, u32[]{:S(2)}) collective-permute-start(bf16[1056,128]{1,0:T(8,128)(2,1)S(1)} %pack.1.refs_0_), channel_id=1, source_target_pairs={{24,0},{25,1},{16,8},{17,9},{8,16},{9,17},{0,24},{1,25},{26,2},{27... | collective-permute-start | bytes 811016 | tf_op jit(solution)/shard_map/ppermute | solution.py:43
  12.6 1.7 %collective-permute-done.1.refs_1_ = bf16[128,256]{1,0:T(8,128)(2,1)S(1)} collective-permute-done((bf16[128,256]{1,0:T(8,128)(2,1)S(1)}, bf16[128,256]{1,0:T(8,128)(2,1)S(1)}, u32[]{:S(2)}, u32[]{:S(2)}) %collective-permute-start.1) | collective-permute-done | bytes 65568 | tf_op jit(solution)/shard_map/ppermute | solution.py:53
  14.3 1.5 %collective-permute-done.refs_0_ = bf16[128,256]{1,0:T(8,128)(2,1)S(1)} collective-permute-done((bf16[128,256]{1,0:T(8,128)(2,1)S(1)}, bf16[128,256]{1,0:T(8,128)(2,1)S(1)}, u32[]{:S(2)}, u32[]{:S(2)}) %collective-permute-start) | collective-permute-done | bytes 65568 | tf_op jit(solution)/shard_map/ppermute | solution.py:53
  15.9 1.5 %collective-permute-done.3.refs_2_ = bf16[512,256]{1,0:T(8,128)(2,1)S(1)} collective-permute-done((bf16[512,256]{1,0:T(8,128)(2,1)S(1)}, bf16[512,256]{1,0:T(8,128)(2,1)S(1)}, u32[]{:S(2)}, u32[]{:S(2)}) %collective-permute-start.3) | collective-permute-done | bytes 262176 | tf_op jit(solution)/shard_map/ppermute | solution.py:62
  17.4 1.3 %part.3 = (f32[128,512]{1,0:T(8,128)S(1)}, f32[1024,256]{1,0:T(8,128)S(1)}, bf16[1024,128]{1,0:T(8,128)(2,1)S(1)}, bf16[1024,128]{1,0:T(8,128)(2,1)S(1)}, bf16[128,1024]{1,0:T(8,128)(2,1)S(1)}) custom-call(bf16[1056,128]{1,0:T(8,128)(2,1)S(1)} %pack.1.refs_0_, bf16[512,256]{1,0:T(8,128)(2,1)S(1)} %stack.1.refs_1_, ...), custom_call_target="tpu_custom_call" | custom-call | flops 1000 | bytes 1000 | tf_op jit(solution)/shard_map/part/pallas_call | solution.py:316
  18.8 2.1 %part.4 = (bf16[256,512]{1,0:T(8,128)(2,1)S(1)}, f32[1024,256]{1,0:T(8,128)S(1)}) custom-call(bf16[2112,128]{1,0:T(8,128)(2,1)S(1)} %collective-permute-done.9.refs_0_, bf16[1024,128]{1,0:T(8,128)(2,1)S(1)} %get-tuple-element.23.refs_1_, bf16[1024,128]{1,0:T(8,128)(2,1)S(1)} %get-tuple-element.24.refs_2_, bf16[128,1024]{1,0:T(8,128)(2,1)S(1)} %get-tuple-element.25.refs_3_, ...), custom_call_target="tpu_custom_call" | custom-call | flops 2000 | bytes 1000 | tf_op jit(solution)/shard_map/part/pallas_call | solution.py:316
  20.9 0.6 %collective-permute-done.11.refs_0_ = bf16[1056,128]{1,0:T(8,128)(2,1)S(1)} collective-permute-done((bf16[1056,128]{1,0:T(8,128)(2,1)S(1)}, bf16[1056,128]{1,0:T(8,128)(2,1)S(1)}, u32[]{:S(2)}, u32[]{:S(2)}) %collective-permute-start.11) | collective-permute-done | bytes 270368 | tf_op jit(solution)/shard_map/ppermute | solution.py:43
  21.5 1.3 %part.5 = (bf16[128,512]{1,0:T(8,128)(2,1)S(1)}, f32[512,256]{1,0:T(8,128)S(1)}, bf16[512,256]{1,0:T(8,128)(2,1)S(1)}) custom-call(bf16[1056,128]{1,0:T(8,128)(2,1)S(1)} %collective-permute-done.11.refs_0_, bf16[1024,128]{1,0:T(8,128)(2,1)S(1)} %get-tuple-element.23.refs_1_, bf16[1024,128]{1,0:T(8,128)(2,1)S(1)} %get-tuple-element.24.refs_2_, ...), custom_call_target="tpu_custom_call" | custom-call | flops 1000 | bytes 1000 | tf_op jit(solution)/shard_map/part/pallas_call | solution.py:316
  22.9 1.6 %collective-permute-start.10 = (bf16[256,512]{1,0:T(8,128)(2,1)S(1)}, bf16[256,512]{1,0:T(8,128)(2,1)S(1)}, u32[]{:S(2)}, u32[]{:S(2)}) collective-permute-start(bf16[256,512]{1,0:T(8,128)(2,1)S(1)} %get-tuple-element.27), channel_id=1, source_target_pairs={{0,8},{1,17},{8,0},{9,25},{16,24},{17,1},{24,16},{25,9},{2,10},{3,... | collective-permute-start | bytes 786440 | tf_op jit(solution)/shard_map/ppermute | solution.py:48
  24.4 1.0 %collective-permute-start.18 = (bf16[128,512]{1,0:T(8,128)(2,1)S(1)}, bf16[128,512]{1,0:T(8,128)(2,1)S(1)}, u32[]{:S(2)}, u32[]{:S(2)}) collective-permute-start(bf16[128,512]{1,0:T(8,128)(2,1)S(1)} %get-tuple-element.37), channel_id=1, source_target_pairs={{0,24},{1,25},{8,16},{9,17},{16,8},{17,9},{24,0},{25,1},{2,26},{3,... | collective-permute-start | bytes 393224 | tf_op jit(solution)/shard_map/ppermute | solution.py:48
  25.5 2.2 %collective-permute-start.13 = (bf16[128,256]{1,0:T(8,128)(2,1)S(1)}, bf16[128,256]{1,0:T(8,128)(2,1)S(1)}, u32[]{:S(2)}, u32[]{:S(2)}) collective-permute-start(bf16[128,256]{1,0:T(8,128)(2,1)S(1)} %get-tuple-element.31), channel_id=1, source_target_pairs={{0,4},{2,6},{4,0},{6,2},{1,5},{3,7},{5,1},{7,3},{8,12},{10,14},{12... | collective-permute-start | bytes 196616 | tf_op jit(solution)/shard_map/ppermute | solution.py:58
  27.6 1.4 %collective-permute-start.19 = (bf16[128,256]{1,0:T(8,128)(2,1)S(1)}, bf16[128,256]{1,0:T(8,128)(2,1)S(1)}, u32[]{:S(2)}, u32[]{:S(2)}) collective-permute-start(bf16[128,256]{1,0:T(8,128)(2,1)S(1)} %get-tuple-element.39), channel_id=1, source_target_pairs={{0,6},{2,4},{4,2},{6,0},{1,7},{3,5},{5,3},{7,1},{8,14},{10,12},{12... | collective-permute-start | bytes 196616 | tf_op jit(solution)/shard_map/ppermute | solution.py:58
  29.2 1.5 %collective-permute-done.10.ref.refs_1_ = bf16[256,512]{1,0:T(8,128)(2,1)S(1)} collective-permute-done((bf16[256,512]{1,0:T(8,128)(2,1)S(1)}, bf16[256,512]{1,0:T(8,128)(2,1)S(1)}, u32[]{:S(2)}, u32[]{:S(2)}) %collective-permute-start.10) | collective-permute-done | bytes 262176 | tf_op jit(solution)/shard_map/ppermute | solution.py:48
  30.7 1.7 %collective-permute-done.13.refs_9_ = bf16[128,256]{1,0:T(8,128)(2,1)S(1)} collective-permute-done((bf16[128,256]{1,0:T(8,128)(2,1)S(1)}, bf16[128,256]{1,0:T(8,128)(2,1)S(1)}, u32[]{:S(2)}, u32[]{:S(2)}) %collective-permute-start.13) | collective-permute-done | bytes 65568 | tf_op jit(solution)/shard_map/ppermute | solution.py:58
  33.1 1.2 %collective-permute-done.19.refs_8_ = bf16[128,256]{1,0:T(8,128)(2,1)S(1)} collective-permute-done((bf16[128,256]{1,0:T(8,128)(2,1)S(1)}, bf16[128,256]{1,0:T(8,128)(2,1)S(1)}, u32[]{:S(2)}, u32[]{:S(2)}) %collective-permute-start.19) | collective-permute-done | bytes 65568 | tf_op jit(solution)/shard_map/ppermute | solution.py:58
  34.4 0.6 %collective-permute-done.20.refs_10_ = bf16[128,256]{1,0:T(8,128)(2,1)S(1)} collective-permute-done((bf16[128,256]{1,0:T(8,128)(2,1)S(1)}, bf16[128,256]{1,0:T(8,128)(2,1)S(1)}, u32[]{:S(2)}, u32[]{:S(2)}) %collective-permute-start.20) | collective-permute-done | bytes 65568 | tf_op jit(solution)/shard_map/ppermute | solution.py:58
  35.0 0.6 %collective-permute-done.17.refs_5_ = bf16[32,512]{1,0:T(8,128)(2,1)S(1)} collective-permute-done((bf16[32,512]{1,0:T(8,128)(2,1)S(1)}, bf16[32,512]{1,0:T(8,128)(2,1)S(1)}, u32[]{:S(2)}, u32[]{:S(2)}) %collective-permute-start.17) | collective-permute-done | bytes 32800 | tf_op jit(solution)/shard_map/ppermute | solution.py:62
  35.6 0.7 %totals.1 = (bf16[128,512]{1,0:T(8,128)(2,1)}, bf16[128,256]{1,0:T(8,128)(2,1)}) custom-call(f32[128,512]{1,0:T(8,128)S(1)} %get-tuple-element.22.refs_0_, bf16[256,512]{1,0:T(8,128)(2,1)S(1)} %collective-permute-done.10.ref.refs_1_, bf16[32,512]{1,0:T(8,128)(2,1)S(1)} %collective-permute-done.14.refs_2_, ...), custom_call_target="tpu_custom_call" | custom-call | tf_op jit(solution)/shard_map/totals/pallas_call | solution.py:392
  (31 shorter events, 2.3 us)
Async XLA Ops:
  0.6 3.1 %collective-permute-start.4 = (bf16[128,512]{1,0:T(8,128)(2,1)}, bf16[128,512]{1,0:T(8,128)(2,1)S(1)}, u32[]{:S(2)}, u32[]{:S(2)}) collective-permute-start(bf16[128,512]{1,0:T(8,128)(2,1)} %refs_0_.1), channel_id=1, source_target_pairs={{0,1},{1,0},{2,3},{3,2},{4,5},{5,4},{6,7},{7,6},{8,9},{9,8},{10,11... | collective-permute-start | bytes 393224 | tf_op jit(solution)/shard_map/ppermute | solution.py:62
  1.1 2.6 %collective-permute-start.6 = (bf16[128,512]{1,0:T(8,128)(2,1)}, bf16[128,512]{1,0:T(8,128)(2,1)S(1)}, u32[]{:S(2)}, u32[]{:S(2)}) collective-permute-start(bf16[128,512]{1,0:T(8,128)(2,1)} %refs_2_.1), channel_id=1, source_target_pairs={{0,1},{1,0},{2,3},{3,2},{4,5},{5,4},{6,7},{7,6},{8,9},{9,8},{10,11... | collective-permute-start | bytes 393224 | tf_op jit(solution)/shard_map/ppermute | solution.py:62
  1.2 2.5 %collective-permute-start.5 = (bf16[128,512]{1,0:T(8,128)(2,1)}, bf16[128,512]{1,0:T(8,128)(2,1)S(1)}, u32[]{:S(2)}, u32[]{:S(2)}) collective-permute-start(bf16[128,512]{1,0:T(8,128)(2,1)} %refs_1_.1), channel_id=1, source_target_pairs={{0,1},{1,0},{2,3},{3,2},{4,5},{5,4},{6,7},{7,6},{8,9},{9,8},{10,11... | collective-permute-start | bytes 393224 | tf_op jit(solution)/shard_map/ppermute | solution.py:62
  1.7 0.7 %copy-start.1 = (s32[128]{0:T(128)S(1)}, s32[128]{0:T(128)}, u32[]{:S(2)}) copy-start(s32[128]{0:T(128)} %param.11) | copy-start | bytes 1540
  1.7 2.0 %collective-permute-start.7 = (f32[4,128]{1,0:T(4,128)}, f32[4,128]{1,0:T(4,128)S(1)}, u32[]{:S(2)}, u32[]{:S(2)}) collective-permute-start(f32[4,128]{1,0:T(4,128)} %bitcast.2), channel_id=1, source_target_pairs={{0,1},{1,0},{2,3},{3,2},{4,5},{5,4},{6,7},{7,6},{8,9},{9,8},{10,11... | collective-permute-start | bytes 6152 | tf_op jit(solution)/shard_map/ppermute | solution.py:62
  2.3 1.4 %collective-permute-start.8 = (s32[1,128]{1,0:T(1,128)S(1)}, s32[1,128]{1,0:T(1,128)S(1)}, u32[]{:S(2)}, u32[]{:S(2)}) collective-permute-start(s32[1,128]{1,0:T(1,128)S(1)} %bitcast.5), channel_id=1, source_target_pairs={{0,1},{1,0},{2,3},{3,2},{4,5},{5,4},{6,7},{7,6},{8,9},{9,8},{10,11... | collective-permute-start | bytes 1544 | tf_op jit(solution)/shard_map/ppermute | solution.py:62
  3.7 3.2 %copy-start = (bf16[128,256]{1,0:T(8,128)(2,1)S(1)}, bf16[128,256]{1,0:T(8,128)(2,1)}, u32[]{:S(2)}) copy-start(bf16[128,256]{1,0:T(8,128)(2,1)} %refs_3_.1) | copy-start | bytes 196612
  3.9 14.8 %collective-permute-start.9 = (bf16[2112,128]{1,0:T(8,128)(2,1)S(1)}, bf16[2112,128]{1,0:T(8,128)(2,1)S(1)}, u32[]{:S(2)}, u32[]{:S(2)}) collective-permute-start(bf16[2112,128]{1,0:T(8,128)(2,1)S(1)} %pack_chip.1), channel_id=1, source_target_pairs={{8,0},{17,1},{0,8},{25,9},{24,16},{1,17},{16,24},{9,25},{10,2},{19... | collective-permute-start | bytes 1622024 | tf_op jit(solution)/shard_map/ppermute | solution.py:43
  6.9 7.4 %collective-permute-start.1 = (bf16[128,256]{1,0:T(8,128)(2,1)S(1)}, bf16[128,256]{1,0:T(8,128)(2,1)S(1)}, u32[]{:S(2)}, u32[]{:S(2)}) collective-permute-start(bf16[128,256]{1,0:T(8,128)(2,1)S(1)} %copy-done), channel_id=1, source_target_pairs={{4,0},{6,2},{0,4},{2,6},{5,1},{7,3},{1,5},{3,7},{12,8},{14,10},{8,... | collective-permute-start | bytes 196616 | tf_op jit(solution)/shard_map/ppermute | solution.py:53
  9.5 6.2 %collective-permute-start = (bf16[128,256]{1,0:T(8,128)(2,1)S(1)}, bf16[128,256]{1,0:T(8,128)(2,1)S(1)}, u32[]{:S(2)}, u32[]{:S(2)}) collective-permute-start(bf16[128,256]{1,0:T(8,128)(2,1)S(1)} %copy-done), channel_id=1, source_target_pairs={{6,0},{4,2},{2,4},{0,6},{7,1},{5,3},{3,5},{1,7},{14,8},{12,10},{10... | collective-permute-start | bytes 196616 | tf_op jit(solution)/shard_map/ppermute | solution.py:53
  10.8 5.0 %collective-permute-start.2 = (bf16[128,256]{1,0:T(8,128)(2,1)S(1)}, bf16[128,256]{1,0:T(8,128)(2,1)S(1)}, u32[]{:S(2)}, u32[]{:S(2)}) collective-permute-start(bf16[128,256]{1,0:T(8,128)(2,1)S(1)} %copy-done), channel_id=1, source_target_pairs={{2,0},{0,2},{6,4},{4,6},{3,1},{1,3},{7,5},{5,7},{10,8},{8,10},{14,... | collective-permute-start | bytes 196616 | tf_op jit(solution)/shard_map/ppermute | solution.py:53
  11.1 10.4 %collective-permute-start.11 = (bf16[1056,128]{1,0:T(8,128)(2,1)S(1)}, bf16[1056,128]{1,0:T(8,128)(2,1)S(1)}, u32[]{:S(2)}, u32[]{:S(2)}) collective-permute-start(bf16[1056,128]{1,0:T(8,128)(2,1)S(1)} %pack.1.refs_0_), channel_id=1, source_target_pairs={{24,0},{25,1},{16,8},{17,9},{8,16},{9,17},{0,24},{1,25},{26,2},{27... | collective-permute-start | bytes 811016 | tf_op jit(solution)/shard_map/ppermute | solution.py:43
  15.8 1.6 %collective-permute-start.3 = (bf16[512,256]{1,0:T(8,128)(2,1)S(1)}, bf16[512,256]{1,0:T(8,128)(2,1)S(1)}, u32[]{:S(2)}, u32[]{:S(2)}) collective-permute-start(bf16[512,256]{1,0:T(8,128)(2,1)S(1)} %stack.1.refs_1_), channel_id=1, source_target_pairs={{0,1},{1,0},{2,3},{3,2},{4,5},{5,4},{6,7},{7,6},{8,9},{9,8},{10,11... | collective-permute-start | bytes 786440 | tf_op jit(solution)/shard_map/ppermute | solution.py:62
  22.8 2.6 %collective-permute-start.12 = (bf16[512,256]{1,0:T(8,128)(2,1)S(1)}, bf16[512,256]{1,0:T(8,128)(2,1)S(1)}, u32[]{:S(2)}, u32[]{:S(2)}) collective-permute-start(bf16[512,256]{1,0:T(8,128)(2,1)S(1)} %get-tuple-element.30), channel_id=1, source_target_pairs={{0,1},{1,0},{2,3},{3,2},{4,5},{5,4},{6,7},{7,6},{8,9},{9,8},{10,11... | collective-permute-start | bytes 786440 | tf_op jit(solution)/shard_map/ppermute | solution.py:62
  22.9 7.8 %collective-permute-start.10 = (bf16[256,512]{1,0:T(8,128)(2,1)S(1)}, bf16[256,512]{1,0:T(8,128)(2,1)S(1)}, u32[]{:S(2)}, u32[]{:S(2)}) collective-permute-start(bf16[256,512]{1,0:T(8,128)(2,1)S(1)} %get-tuple-element.27), channel_id=1, source_target_pairs={{0,8},{1,17},{8,0},{9,25},{16,24},{17,1},{24,16},{25,9},{2,10},{3,... | collective-permute-start | bytes 786440 | tf_op jit(solution)/shard_map/ppermute | solution.py:48
  24.4 8.6 %collective-permute-start.18 = (bf16[128,512]{1,0:T(8,128)(2,1)S(1)}, bf16[128,512]{1,0:T(8,128)(2,1)S(1)}, u32[]{:S(2)}, u32[]{:S(2)}) collective-permute-start(bf16[128,512]{1,0:T(8,128)(2,1)S(1)} %get-tuple-element.37), channel_id=1, source_target_pairs={{0,24},{1,25},{8,16},{9,17},{16,8},{17,9},{24,0},{25,1},{2,26},{3,... | collective-permute-start | bytes 393224 | tf_op jit(solution)/shard_map/ppermute | solution.py:48
  25.5 7.0 %collective-permute-start.13 = (bf16[128,256]{1,0:T(8,128)(2,1)S(1)}, bf16[128,256]{1,0:T(8,128)(2,1)S(1)}, u32[]{:S(2)}, u32[]{:S(2)}) collective-permute-start(bf16[128,256]{1,0:T(8,128)(2,1)S(1)} %get-tuple-element.31), channel_id=1, source_target_pairs={{0,4},{2,6},{4,0},{6,2},{1,5},{3,7},{5,1},{7,3},{8,12},{10,14},{12... | collective-permute-start | bytes 196616 | tf_op jit(solution)/shard_map/ppermute | solution.py:58
  27.6 6.7 %collective-permute-start.19 = (bf16[128,256]{1,0:T(8,128)(2,1)S(1)}, bf16[128,256]{1,0:T(8,128)(2,1)S(1)}, u32[]{:S(2)}, u32[]{:S(2)}) collective-permute-start(bf16[128,256]{1,0:T(8,128)(2,1)S(1)} %get-tuple-element.39), channel_id=1, source_target_pairs={{0,6},{2,4},{4,2},{6,0},{1,7},{3,5},{5,3},{7,1},{8,14},{10,12},{12... | collective-permute-start | bytes 196616 | tf_op jit(solution)/shard_map/ppermute | solution.py:58
  29.0 6.0 %collective-permute-start.20 = (bf16[128,256]{1,0:T(8,128)(2,1)S(1)}, bf16[128,256]{1,0:T(8,128)(2,1)S(1)}, u32[]{:S(2)}, u32[]{:S(2)}) collective-permute-start(bf16[128,256]{1,0:T(8,128)(2,1)S(1)} %get-tuple-element.41), channel_id=1, source_target_pairs={{0,2},{2,0},{4,6},{6,4},{1,3},{3,1},{5,7},{7,5},{8,10},{10,8},{12,... | collective-permute-start | bytes 196616 | tf_op jit(solution)/shard_map/ppermute | solution.py:58
  32.5 2.5 %collective-permute-start.14 = (bf16[32,512]{1,0:T(8,128)(2,1)S(1)}, bf16[32,512]{1,0:T(8,128)(2,1)S(1)}, u32[]{:S(2)}, u32[]{:S(2)}) collective-permute-start(bf16[32,512]{1,0:T(8,128)(2,1)S(1)} %get-tuple-element.33), channel_id=1, source_target_pairs={{0,1},{1,0},{2,3},{3,2},{4,5},{5,4},{6,7},{7,6},{8,9},{9,8},{10,11... | collective-permute-start | bytes 98312 | tf_op jit(solution)/shard_map/ppermute | solution.py:62
  32.5 2.5 %collective-permute-start.15 = (bf16[32,512]{1,0:T(8,128)(2,1)S(1)}, bf16[32,512]{1,0:T(8,128)(2,1)S(1)}, u32[]{:S(2)}, u32[]{:S(2)}) collective-permute-start(bf16[32,512]{1,0:T(8,128)(2,1)S(1)} %get-tuple-element.34), channel_id=1, source_target_pairs={{0,1},{1,0},{2,3},{3,2},{4,5},{5,4},{6,7},{7,6},{8,9},{9,8},{10,11... | collective-permute-start | bytes 98312 | tf_op jit(solution)/shard_map/ppermute | solution.py:62
  33.0 2.0 %collective-permute-start.16 = (bf16[32,512]{1,0:T(8,128)(2,1)S(1)}, bf16[32,512]{1,0:T(8,128)(2,1)S(1)}, u32[]{:S(2)}, u32[]{:S(2)}) collective-permute-start(bf16[32,512]{1,0:T(8,128)(2,1)S(1)} %get-tuple-element.35), channel_id=1, source_target_pairs={{0,1},{1,0},{2,3},{3,2},{4,5},{5,4},{6,7},{7,6},{8,9},{9,8},{10,11... | collective-permute-start | bytes 98312 | tf_op jit(solution)/shard_map/ppermute | solution.py:62
  34.4 1.2 %collective-permute-start.17 = (bf16[32,512]{1,0:T(8,128)(2,1)S(1)}, bf16[32,512]{1,0:T(8,128)(2,1)S(1)}, u32[]{:S(2)}, u32[]{:S(2)}) collective-permute-start(bf16[32,512]{1,0:T(8,128)(2,1)S(1)} %get-tuple-element.36), channel_id=1, source_target_pairs={{0,1},{1,0},{2,3},{3,2},{4,5},{5,4},{6,7},{7,6},{8,9},{9,8},{10,11... | collective-permute-start | bytes 98312 | tf_op jit(solution)/shard_map/ppermute | solution.py:62

commit v5 on v4

--- a/solution.py
+++ b/solution.py
@@ -11,7 +11,7 @@
 
 LOG2E = math.log2(math.e)
 STATS = 8
-PIECES = 4
+PIECES = 2
 PART_COST = 1000
 VMEM_LIMIT = 32 * 1024 * 1024
 SMALL_LIMIT = 8 * 1024 * 1024
@@ -410,7 +410,8 @@
     own = pack(heads, inputs)
     chip = None
     if any(len(steps) == 2 for steps in rounds):
-        chip = pack_chip(heads, own, [swap_cores(value) for value in inputs])
+        theirs = [swap_cores(value) for value in inputs[:4]] + [swap_cores(doc_start).reshape(1, tok)]
+        chip = pack_chip(heads, own, theirs)
     packs = [fetch(chip if len(steps) == 2 else own, steps) for steps in rounds]
     mine = [keys_values] + [fetch_z(keys_values, s) for s in range(1, zed)]
     far = list(range(zed - 1, -1, -1))

time: 36.5 us -> 35.2 us (0.964)
  waiting for transfers between devices: 11 us -> 9.5 us
  starting transfers between devices: 16.9 us -> 17.8 us
  local copies, waits for them, and re-layouts: 0.58 us -> 0.01 us
    ppermute x3, waiting for transfers between devices: 3.59 us -> 2.63 us  [give_back_z(): lax.ppermute(value, 'z', [(z, peer(z, step, count)) for z in range(count)])]
    ppermute x2, starting transfers between devices: 2.53 us -> 3.17 us  [give_back(): return lax.ppermute(value, ('inner', 'core'), [(b, a) for a, b in pairs])]
    unnamed x4, local copies, waits for them, and re-layouts: 0.58 us -> 0.01 us
    ppermute x11 -> x9, waiting for transfers between devices: 2.1 us -> 1.54 us  [swap_cores(): return lax.ppermute(value, 'core', [(0, 1), (1, 0)])]
    ppermute x2, waiting for transfers between devices: 0.59 us -> 0.16 us  [fetch(): lax.ppermute(value, ('inner', 'core'), inner_pairs(steps, lax.axis_size('...]
    ppermute x3, waiting for transfers between devices: 3.24 us -> 3.63 us  [fetch_z(): lax.ppermute(value, 'z', [(peer(z, step, count), z) for z in range(count)])]
    ppermute x11 -> x9, starting transfers between devices: 1.98 us -> 2.25 us  [swap_cores(): return lax.ppermute(value, 'core', [(0, 1), (1, 0)])]
  transfers between devices with their start and end apart: 21 -> 19, of which waited for: 10 -> 8; matrix products, arithmetic and copies ran while one was open for 0% -> 0% of each run, Pallas kernels for 13% -> 14%
where the time goes in v5:
time: 35.2 us; the launch traced here: 35.1 us
  starting transfers between devices  17.8 us (51%)
  waiting for transfers between devices  9.5 us (27%)
  Pallas kernels  7.02 us (20%)
  between operations  0.79 us (2%)
    pallas_call x3, Pallas kernels, part(): pl.pallas_call(functools.partial(part_kernel, steps, first, last, heads,...  4.74 us
    ppermute x3, starting transfers between devices, fetch_z(): lax.ppermute(value, 'z', [(peer(z, step, count), z) for z in range(count)])  4.17 us
    ppermute x2, starting transfers between devices, fetch(): lax.ppermute(value, ('inner', 'core'), inner_pairs(steps, lax.axis_size('...  4.16 us
    ppermute x3, starting transfers between devices, give_back_z(): lax.ppermute(value, 'z', [(z, peer(z, step, count)) for z in range(count)])  4.01 us
    ppermute x3, waiting for transfers between devices, fetch_z(): lax.ppermute(value, 'z', [(peer(z, step, count), z) for z in range(count)])  3.63 us
    ppermute x2, starting transfers between devices, give_back(): return lax.ppermute(value, ('inner', 'core'), [(b, a) for a, b in pairs])  3.17 us
    ppermute x3, waiting for transfers between devices, give_back_z(): lax.ppermute(value, 'z', [(z, peer(z, step, count)) for z in range(count)])  2.63 us
    ppermute x9, starting transfers between devices, swap_cores(): return lax.ppermute(value, 'core', [(0, 1), (1, 0)])  2.25 us
  transfers between devices with their start and end apart: 19, of which 8 were waited for; matrix products, arithmetic and copies ran while one was open for 0% of the time, Pallas kernels for 14%

profile of v5, /device:TPU:0, one launch (start us, length us, event | category | flops | bytes accessed | tf_op | source)
XLA Modules:
  0.0 35.1 jit_solution(3419330603384401168)
XLA Ops:
  0.6 0.5 %collective-permute-start.4 = (bf16[128,512]{1,0:T(8,128)(2,1)}, bf16[128,512]{1,0:T(8,128)(2,1)S(1)}, u32[]{:S(2)}, u32[]{:S(2)}) collective-permute-start(bf16[128,512]{1,0:T(8,128)(2,1)} %refs_0_.1), channel_id=1, source_target_pairs={{0,1},{1,0},{2,3},{3,2},{4,5},{5,4},{6,7},{7,6},{8,9},{9,8},{10,11... | collective-permute-start | bytes 393224 | tf_op jit(solution)/shard_map/ppermute | solution.py:62
  1.2 0.4 %collective-permute-start.5 = (bf16[128,512]{1,0:T(8,128)(2,1)}, bf16[128,512]{1,0:T(8,128)(2,1)S(1)}, u32[]{:S(2)}, u32[]{:S(2)}) collective-permute-start(bf16[128,512]{1,0:T(8,128)(2,1)} %refs_1_.1), channel_id=1, source_target_pairs={{0,1},{1,0},{2,3},{3,2},{4,5},{5,4},{6,7},{7,6},{8,9},{9,8},{10,11... | collective-permute-start | bytes 393224 | tf_op jit(solution)/shard_map/ppermute | solution.py:62
  1.8 0.4 %collective-permute-start.8 = (s32[128]{0:T(128)S(1)}, s32[128]{0:T(128)S(1)}, u32[]{:S(2)}, u32[]{:S(2)}) collective-permute-start(s32[128]{0:T(128)S(1)} %copy-done.1), channel_id=1, source_target_pairs={{0,1},{1,0},{2,3},{3,2},{4,5},{5,4},{6,7},{7,6},{8,9},{9,8},{10,11... | collective-permute-start | bytes 1544 | tf_op jit(solution)/shard_map/ppermute | solution.py:62
  2.2 1.3 %pack.1.refs_0_ = bf16[1056,128]{1,0:T(8,128)(2,1)S(1)} custom-call(bf16[128,512]{1,0:T(8,128)(2,1)} %refs_0_.1, bf16[128,512]{1,0:T(8,128)(2,1)} %refs_1_.1, bf16[128,512]{1,0:T(8,128)(2,1)} %refs_2_.1, f32[4,128]{1,0:T(4,128)} %bitcast.5, s32[1,128]{1,0:T(1,128)} %bitcast.6), custom_call_target="tpu_custom_call" | custom-call | tf_op jit(solution)/shard_map/pack/pallas_call | solution.py:118
  3.7 2.6 %collective-permute-start.9 = (bf16[2112,128]{1,0:T(8,128)(2,1)S(1)}, bf16[2112,128]{1,0:T(8,128)(2,1)S(1)}, u32[]{:S(2)}, u32[]{:S(2)}) collective-permute-start(bf16[2112,128]{1,0:T(8,128)(2,1)S(1)} %pack_chip.1), channel_id=1, source_target_pairs={{8,0},{17,1},{0,8},{25,9},{24,16},{1,17},{16,24},{9,25},{10,2},{19... | collective-permute-start | bytes 1622024 | tf_op jit(solution)/shard_map/ppermute | solution.py:43
  6.3 2.6 %collective-permute-start.1 = (bf16[128,256]{1,0:T(8,128)(2,1)S(1)}, bf16[128,256]{1,0:T(8,128)(2,1)S(1)}, u32[]{:S(2)}, u32[]{:S(2)}) collective-permute-start(bf16[128,256]{1,0:T(8,128)(2,1)S(1)} %copy-done), channel_id=1, source_target_pairs={{4,0},{6,2},{0,4},{2,6},{5,1},{7,3},{1,5},{3,7},{12,8},{14,10},{8,... | collective-permute-start | bytes 196616 | tf_op jit(solution)/shard_map/ppermute | solution.py:53
  8.9 1.3 %collective-permute-start = (bf16[128,256]{1,0:T(8,128)(2,1)S(1)}, bf16[128,256]{1,0:T(8,128)(2,1)S(1)}, u32[]{:S(2)}, u32[]{:S(2)}) collective-permute-start(bf16[128,256]{1,0:T(8,128)(2,1)S(1)} %copy-done), channel_id=1, source_target_pairs={{6,0},{4,2},{2,4},{0,6},{7,1},{5,3},{3,5},{1,7},{14,8},{12,10},{10... | collective-permute-start | bytes 196616 | tf_op jit(solution)/shard_map/ppermute | solution.py:53
  10.5 1.5 %collective-permute-start.11 = (bf16[1056,128]{1,0:T(8,128)(2,1)S(1)}, bf16[1056,128]{1,0:T(8,128)(2,1)S(1)}, u32[]{:S(2)}, u32[]{:S(2)}) collective-permute-start(bf16[1056,128]{1,0:T(8,128)(2,1)S(1)} %pack.1.refs_0_), channel_id=1, source_target_pairs={{24,0},{25,1},{16,8},{17,9},{8,16},{9,17},{0,24},{1,25},{26,2},{27... | collective-permute-start | bytes 811016 | tf_op jit(solution)/shard_map/ppermute | solution.py:43
  12.1 1.3 %collective-permute-done.1.refs_1_ = bf16[128,256]{1,0:T(8,128)(2,1)S(1)} collective-permute-done((bf16[128,256]{1,0:T(8,128)(2,1)S(1)}, bf16[128,256]{1,0:T(8,128)(2,1)S(1)}, u32[]{:S(2)}, u32[]{:S(2)}) %collective-permute-start.1) | collective-permute-done | bytes 65568 | tf_op jit(solution)/shard_map/ppermute | solution.py:53
  13.4 2.0 %collective-permute-done.refs_0_ = bf16[128,256]{1,0:T(8,128)(2,1)S(1)} collective-permute-done((bf16[128,256]{1,0:T(8,128)(2,1)S(1)}, bf16[128,256]{1,0:T(8,128)(2,1)S(1)}, u32[]{:S(2)}, u32[]{:S(2)}) %collective-permute-start) | collective-permute-done | bytes 65568 | tf_op jit(solution)/shard_map/ppermute | solution.py:53
  15.4 0.3 collective-permute-done.2.refs_2_
  15.8 1.5 %collective-permute-done.3.refs_2_ = bf16[512,256]{1,0:T(8,128)(2,1)S(1)} collective-permute-done((bf16[512,256]{1,0:T(8,128)(2,1)S(1)}, bf16[512,256]{1,0:T(8,128)(2,1)S(1)}, u32[]{:S(2)}, u32[]{:S(2)}) %collective-permute-start.3) | collective-permute-done | bytes 262176 | tf_op jit(solution)/shard_map/ppermute | solution.py:62
  17.3 1.3 %part.3 = (f32[128,512]{1,0:T(8,128)S(1)}, f32[1024,256]{1,0:T(8,128)S(1)}, bf16[1024,128]{1,0:T(8,128)(2,1)S(1)}, bf16[1024,128]{1,0:T(8,128)(2,1)S(1)}, bf16[128,1024]{1,0:T(8,128)(2,1)S(1)}) custom-call(bf16[1056,128]{1,0:T(8,128)(2,1)S(1)} %pack.1.refs_0_, bf16[512,256]{1,0:T(8,128)(2,1)S(1)} %stack.1.refs_1_, ...), custom_call_target="tpu_custom_call" | custom-call | flops 1000 | bytes 1000 | tf_op jit(solution)/shard_map/part/pallas_call | solution.py:316
  18.6 2.2 %part.4 = (bf16[256,512]{1,0:T(8,128)(2,1)S(1)}, f32[1024,256]{1,0:T(8,128)S(1)}) custom-call(bf16[2112,128]{1,0:T(8,128)(2,1)S(1)} %collective-permute-done.9.refs_0_, bf16[1024,128]{1,0:T(8,128)(2,1)S(1)} %get-tuple-element.21.refs_1_, bf16[1024,128]{1,0:T(8,128)(2,1)S(1)} %get-tuple-element.22.refs_2_, bf16[128,1024]{1,0:T(8,128)(2,1)S(1)} %get-tuple-element.23.refs_3_, ...), custom_call_target="tpu_custom_call" | custom-call | flops 2000 | bytes 1000 | tf_op jit(solution)/shard_map/part/pallas_call | solution.py:316
  21.0 1.3 %part.5 = (bf16[128,512]{1,0:T(8,128)(2,1)S(1)}, f32[512,256]{1,0:T(8,128)S(1)}, bf16[512,256]{1,0:T(8,128)(2,1)S(1)}) custom-call(bf16[1056,128]{1,0:T(8,128)(2,1)S(1)} %collective-permute-done.11.refs_0_, bf16[1024,128]{1,0:T(8,128)(2,1)S(1)} %get-tuple-element.21.refs_1_, bf16[1024,128]{1,0:T(8,128)(2,1)S(1)} %get-tuple-element.22.refs_2_, ...), custom_call_target="tpu_custom_call" | custom-call | flops 1000 | bytes 1000 | tf_op jit(solution)/shard_map/part/pallas_call | solution.py:316
  22.3 1.6 %collective-permute-start.10 = (bf16[256,512]{1,0:T(8,128)(2,1)S(1)}, bf16[256,512]{1,0:T(8,128)(2,1)S(1)}, u32[]{:S(2)}, u32[]{:S(2)}) collective-permute-start(bf16[256,512]{1,0:T(8,128)(2,1)S(1)} %get-tuple-element.25), channel_id=1, source_target_pairs={{0,8},{1,17},{8,0},{9,25},{16,24},{17,1},{24,16},{25,9},{2,10},{3,... | collective-permute-start | bytes 786440 | tf_op jit(solution)/shard_map/ppermute | solution.py:48
  23.9 2.6 %collective-permute-start.13 = (bf16[128,256]{1,0:T(8,128)(2,1)S(1)}, bf16[128,256]{1,0:T(8,128)(2,1)S(1)}, u32[]{:S(2)}, u32[]{:S(2)}) collective-permute-start(bf16[128,256]{1,0:T(8,128)(2,1)S(1)} %get-tuple-element.29), channel_id=1, source_target_pairs={{0,4},{2,6},{4,0},{6,2},{1,5},{3,7},{5,1},{7,3},{8,12},{10,14},{12... | collective-permute-start | bytes 196616 | tf_op jit(solution)/shard_map/ppermute | solution.py:58
  26.6 1.6 %collective-permute-start.16 = (bf16[128,512]{1,0:T(8,128)(2,1)S(1)}, bf16[128,512]{1,0:T(8,128)(2,1)S(1)}, u32[]{:S(2)}, u32[]{:S(2)}) collective-permute-start(bf16[128,512]{1,0:T(8,128)(2,1)S(1)} %get-tuple-element.33), channel_id=1, source_target_pairs={{0,24},{1,25},{8,16},{9,17},{16,8},{17,9},{24,0},{25,1},{2,26},{3,... | collective-permute-start | bytes 393224 | tf_op jit(solution)/shard_map/ppermute | solution.py:48
  28.2 1.1 %collective-permute-start.17 = (bf16[128,256]{1,0:T(8,128)(2,1)S(1)}, bf16[128,256]{1,0:T(8,128)(2,1)S(1)}, u32[]{:S(2)}, u32[]{:S(2)}) collective-permute-start(bf16[128,256]{1,0:T(8,128)(2,1)S(1)} %get-tuple-element.35), channel_id=1, source_target_pairs={{0,6},{2,4},{4,2},{6,0},{1,7},{3,5},{5,3},{7,1},{8,14},{10,12},{12... | collective-permute-start | bytes 196616 | tf_op jit(solution)/shard_map/ppermute | solution.py:58
  29.6 1.0 %collective-permute-done.13.refs_7_ = bf16[128,256]{1,0:T(8,128)(2,1)S(1)} collective-permute-done((bf16[128,256]{1,0:T(8,128)(2,1)S(1)}, bf16[128,256]{1,0:T(8,128)(2,1)S(1)}, u32[]{:S(2)}, u32[]{:S(2)}) %collective-permute-start.13) | collective-permute-done | bytes 65568 | tf_op jit(solution)/shard_map/ppermute | solution.py:58
  30.7 0.5 %collective-permute-start.15 = (bf16[64,512]{1,0:T(8,128)(2,1)S(1)}, bf16[64,512]{1,0:T(8,128)(2,1)S(1)}, u32[]{:S(2)}, u32[]{:S(2)}) collective-permute-start(bf16[64,512]{1,0:T(8,128)(2,1)S(1)} %get-tuple-element.32), channel_id=1, source_target_pairs={{0,1},{1,0},{2,3},{3,2},{4,5},{5,4},{6,7},{7,6},{8,9},{9,8},{10,11... | collective-permute-start | bytes 196616 | tf_op jit(solution)/shard_map/ppermute | solution.py:62
  31.2 1.5 %collective-permute-done.16.refs_4_ = bf16[128,512]{1,0:T(8,128)(2,1)S(1)} collective-permute-done((bf16[128,512]{1,0:T(8,128)(2,1)S(1)}, bf16[128,512]{1,0:T(8,128)(2,1)S(1)}, u32[]{:S(2)}, u32[]{:S(2)}) %collective-permute-start.16) | collective-permute-done | bytes 131104 | tf_op jit(solution)/shard_map/ppermute | solution.py:48
  32.7 1.6 %collective-permute-done.17.refs_6_ = bf16[128,256]{1,0:T(8,128)(2,1)S(1)} collective-permute-done((bf16[128,256]{1,0:T(8,128)(2,1)S(1)}, bf16[128,256]{1,0:T(8,128)(2,1)S(1)}, u32[]{:S(2)}, u32[]{:S(2)}) %collective-permute-start.17) | collective-permute-done | bytes 65568 | tf_op jit(solution)/shard_map/ppermute | solution.py:58
  34.3 0.7 %totals.1 = (bf16[128,512]{1,0:T(8,128)(2,1)}, bf16[128,256]{1,0:T(8,128)(2,1)}) custom-call(f32[128,512]{1,0:T(8,128)S(1)} %get-tuple-element.20.refs_0_, bf16[256,512]{1,0:T(8,128)(2,1)S(1)} %collective-permute-done.10.ref.refs_1_, bf16[64,512]{1,0:T(8,128)(2,1)S(1)} %collective-permute-done.14.refs_2_, ...), custom_call_target="tpu_custom_call" | custom-call | tf_op jit(solution)/shard_map/totals/pallas_call | solution.py:392
  (27 shorter events, 1.3 us)
Async XLA Ops:
  0.6 1.1 %copy-start.1 = (s32[128]{0:T(128)S(1)}, s32[128]{0:T(128)}, u32[]{:S(2)}) copy-start(s32[128]{0:T(128)} %param.11) | copy-start | bytes 1540
  0.6 2.8 %collective-permute-start.4 = (bf16[128,512]{1,0:T(8,128)(2,1)}, bf16[128,512]{1,0:T(8,128)(2,1)S(1)}, u32[]{:S(2)}, u32[]{:S(2)}) collective-permute-start(bf16[128,512]{1,0:T(8,128)(2,1)} %refs_0_.1), channel_id=1, source_target_pairs={{0,1},{1,0},{2,3},{3,2},{4,5},{5,4},{6,7},{7,6},{8,9},{9,8},{10,11... | collective-permute-start | bytes 393224 | tf_op jit(solution)/shard_map/ppermute | solution.py:62
  1.2 2.3 %collective-permute-start.6 = (bf16[128,512]{1,0:T(8,128)(2,1)}, bf16[128,512]{1,0:T(8,128)(2,1)S(1)}, u32[]{:S(2)}, u32[]{:S(2)}) collective-permute-start(bf16[128,512]{1,0:T(8,128)(2,1)} %refs_2_.1), channel_id=1, source_target_pairs={{0,1},{1,0},{2,3},{3,2},{4,5},{5,4},{6,7},{7,6},{8,9},{9,8},{10,11... | collective-permute-start | bytes 393224 | tf_op jit(solution)/shard_map/ppermute | solution.py:62
  1.2 2.3 %collective-permute-start.5 = (bf16[128,512]{1,0:T(8,128)(2,1)}, bf16[128,512]{1,0:T(8,128)(2,1)S(1)}, u32[]{:S(2)}, u32[]{:S(2)}) collective-permute-start(bf16[128,512]{1,0:T(8,128)(2,1)} %refs_1_.1), channel_id=1, source_target_pairs={{0,1},{1,0},{2,3},{3,2},{4,5},{5,4},{6,7},{7,6},{8,9},{9,8},{10,11... | collective-permute-start | bytes 393224 | tf_op jit(solution)/shard_map/ppermute | solution.py:62
  1.7 1.8 %collective-permute-start.7 = (f32[4,128]{1,0:T(4,128)}, f32[4,128]{1,0:T(4,128)S(1)}, u32[]{:S(2)}, u32[]{:S(2)}) collective-permute-start(f32[4,128]{1,0:T(4,128)} %bitcast.4), channel_id=1, source_target_pairs={{0,1},{1,0},{2,3},{3,2},{4,5},{5,4},{6,7},{7,6},{8,9},{9,8},{10,11... | collective-permute-start | bytes 6152 | tf_op jit(solution)/shard_map/ppermute | solution.py:62
  1.8 1.7 %collective-permute-start.8 = (s32[128]{0:T(128)S(1)}, s32[128]{0:T(128)S(1)}, u32[]{:S(2)}, u32[]{:S(2)}) collective-permute-start(s32[128]{0:T(128)S(1)} %copy-done.1), channel_id=1, source_target_pairs={{0,1},{1,0},{2,3},{3,2},{4,5},{5,4},{6,7},{7,6},{8,9},{9,8},{10,11... | collective-permute-start | bytes 1544 | tf_op jit(solution)/shard_map/ppermute | solution.py:62
  3.5 2.8 %copy-start = (bf16[128,256]{1,0:T(8,128)(2,1)S(1)}, bf16[128,256]{1,0:T(8,128)(2,1)}, u32[]{:S(2)}) copy-start(bf16[128,256]{1,0:T(8,128)(2,1)} %refs_3_.1) | copy-start | bytes 196612
  3.7 14.9 %collective-permute-start.9 = (bf16[2112,128]{1,0:T(8,128)(2,1)S(1)}, bf16[2112,128]{1,0:T(8,128)(2,1)S(1)}, u32[]{:S(2)}, u32[]{:S(2)}) collective-permute-start(bf16[2112,128]{1,0:T(8,128)(2,1)S(1)} %pack_chip.1), channel_id=1, source_target_pairs={{8,0},{17,1},{0,8},{25,9},{24,16},{1,17},{16,24},{9,25},{10,2},{19... | collective-permute-start | bytes 1622024 | tf_op jit(solution)/shard_map/ppermute | solution.py:43
  6.3 7.0 %collective-permute-start.1 = (bf16[128,256]{1,0:T(8,128)(2,1)S(1)}, bf16[128,256]{1,0:T(8,128)(2,1)S(1)}, u32[]{:S(2)}, u32[]{:S(2)}) collective-permute-start(bf16[128,256]{1,0:T(8,128)(2,1)S(1)} %copy-done), channel_id=1, source_target_pairs={{4,0},{6,2},{0,4},{2,6},{5,1},{7,3},{1,5},{3,7},{12,8},{14,10},{8,... | collective-permute-start | bytes 196616 | tf_op jit(solution)/shard_map/ppermute | solution.py:53
  8.9 6.4 %collective-permute-start = (bf16[128,256]{1,0:T(8,128)(2,1)S(1)}, bf16[128,256]{1,0:T(8,128)(2,1)S(1)}, u32[]{:S(2)}, u32[]{:S(2)}) collective-permute-start(bf16[128,256]{1,0:T(8,128)(2,1)S(1)} %copy-done), channel_id=1, source_target_pairs={{6,0},{4,2},{2,4},{0,6},{7,1},{5,3},{3,5},{1,7},{14,8},{12,10},{10... | collective-permute-start | bytes 196616 | tf_op jit(solution)/shard_map/ppermute | solution.py:53
  10.3 5.4 %collective-permute-start.2 = (bf16[128,256]{1,0:T(8,128)(2,1)S(1)}, bf16[128,256]{1,0:T(8,128)(2,1)S(1)}, u32[]{:S(2)}, u32[]{:S(2)}) collective-permute-start(bf16[128,256]{1,0:T(8,128)(2,1)S(1)} %copy-done), channel_id=1, source_target_pairs={{2,0},{0,2},{6,4},{4,6},{3,1},{1,3},{7,5},{5,7},{10,8},{8,10},{14,... | collective-permute-start | bytes 196616 | tf_op jit(solution)/shard_map/ppermute | solution.py:53
  10.5 10.4 %collective-permute-start.11 = (bf16[1056,128]{1,0:T(8,128)(2,1)S(1)}, bf16[1056,128]{1,0:T(8,128)(2,1)S(1)}, u32[]{:S(2)}, u32[]{:S(2)}) collective-permute-start(bf16[1056,128]{1,0:T(8,128)(2,1)S(1)} %pack.1.refs_0_), channel_id=1, source_target_pairs={{24,0},{25,1},{16,8},{17,9},{8,16},{9,17},{0,24},{1,25},{26,2},{27... | collective-permute-start | bytes 811016 | tf_op jit(solution)/shard_map/ppermute | solution.py:43
  15.7 1.6 %collective-permute-start.3 = (bf16[512,256]{1,0:T(8,128)(2,1)S(1)}, bf16[512,256]{1,0:T(8,128)(2,1)S(1)}, u32[]{:S(2)}, u32[]{:S(2)}) collective-permute-start(bf16[512,256]{1,0:T(8,128)(2,1)S(1)} %stack.1.refs_1_), channel_id=1, source_target_pairs={{0,1},{1,0},{2,3},{3,2},{4,5},{5,4},{6,7},{7,6},{8,9},{9,8},{10,11... | collective-permute-start | bytes 786440 | tf_op jit(solution)/shard_map/ppermute | solution.py:62
  22.2 1.6 %collective-permute-start.12 = (bf16[512,256]{1,0:T(8,128)(2,1)S(1)}, bf16[512,256]{1,0:T(8,128)(2,1)S(1)}, u32[]{:S(2)}, u32[]{:S(2)}) collective-permute-start(bf16[512,256]{1,0:T(8,128)(2,1)S(1)} %get-tuple-element.28), channel_id=1, source_target_pairs={{0,1},{1,0},{2,3},{3,2},{4,5},{5,4},{6,7},{7,6},{8,9},{9,8},{10,11... | collective-permute-start | bytes 786440 | tf_op jit(solution)/shard_map/ppermute | solution.py:62
  22.3 7.2 %collective-permute-start.10 = (bf16[256,512]{1,0:T(8,128)(2,1)S(1)}, bf16[256,512]{1,0:T(8,128)(2,1)S(1)}, u32[]{:S(2)}, u32[]{:S(2)}) collective-permute-start(bf16[256,512]{1,0:T(8,128)(2,1)S(1)} %get-tuple-element.25), channel_id=1, source_target_pairs={{0,8},{1,17},{8,0},{9,25},{16,24},{17,1},{24,16},{25,9},{2,10},{3,... | collective-permute-start | bytes 786440 | tf_op jit(solution)/shard_map/ppermute | solution.py:48
  23.9 6.6 %collective-permute-start.13 = (bf16[128,256]{1,0:T(8,128)(2,1)S(1)}, bf16[128,256]{1,0:T(8,128)(2,1)S(1)}, u32[]{:S(2)}, u32[]{:S(2)}) collective-permute-start(bf16[128,256]{1,0:T(8,128)(2,1)S(1)} %get-tuple-element.29), channel_id=1, source_target_pairs={{0,4},{2,6},{4,0},{6,2},{1,5},{3,7},{5,1},{7,3},{8,12},{10,14},{12... | collective-permute-start | bytes 196616 | tf_op jit(solution)/shard_map/ppermute | solution.py:58
  26.6 6.1 %collective-permute-start.16 = (bf16[128,512]{1,0:T(8,128)(2,1)S(1)}, bf16[128,512]{1,0:T(8,128)(2,1)S(1)}, u32[]{:S(2)}, u32[]{:S(2)}) collective-permute-start(bf16[128,512]{1,0:T(8,128)(2,1)S(1)} %get-tuple-element.33), channel_id=1, source_target_pairs={{0,24},{1,25},{8,16},{9,17},{16,8},{17,9},{24,0},{25,1},{2,26},{3,... | collective-permute-start | bytes 393224 | tf_op jit(solution)/shard_map/ppermute | solution.py:48
  28.2 6.1 %collective-permute-start.17 = (bf16[128,256]{1,0:T(8,128)(2,1)S(1)}, bf16[128,256]{1,0:T(8,128)(2,1)S(1)}, u32[]{:S(2)}, u32[]{:S(2)}) collective-permute-start(bf16[128,256]{1,0:T(8,128)(2,1)S(1)} %get-tuple-element.35), channel_id=1, source_target_pairs={{0,6},{2,4},{4,2},{6,0},{1,7},{3,5},{5,3},{7,1},{8,14},{10,12},{12... | collective-permute-start | bytes 196616 | tf_op jit(solution)/shard_map/ppermute | solution.py:58
  29.3 5.0 %collective-permute-start.18 = (bf16[128,256]{1,0:T(8,128)(2,1)S(1)}, bf16[128,256]{1,0:T(8,128)(2,1)S(1)}, u32[]{:S(2)}, u32[]{:S(2)}) collective-permute-start(bf16[128,256]{1,0:T(8,128)(2,1)S(1)} %get-tuple-element.37), channel_id=1, source_target_pairs={{0,2},{2,0},{4,6},{6,4},{1,3},{3,1},{5,7},{7,5},{8,10},{10,8},{12,... | collective-permute-start | bytes 196616 | tf_op jit(solution)/shard_map/ppermute | solution.py:58
  30.6 3.7 %collective-permute-start.14 = (bf16[64,512]{1,0:T(8,128)(2,1)S(1)}, bf16[64,512]{1,0:T(8,128)(2,1)S(1)}, u32[]{:S(2)}, u32[]{:S(2)}) collective-permute-start(bf16[64,512]{1,0:T(8,128)(2,1)S(1)} %get-tuple-element.31), channel_id=1, source_target_pairs={{0,1},{1,0},{2,3},{3,2},{4,5},{5,4},{6,7},{7,6},{8,9},{9,8},{10,11... | collective-permute-start | bytes 196616 | tf_op jit(solution)/shard_map/ppermute | solution.py:62
  30.7 3.7 %collective-permute-start.15 = (bf16[64,512]{1,0:T(8,128)(2,1)S(1)}, bf16[64,512]{1,0:T(8,128)(2,1)S(1)}, u32[]{:S(2)}, u32[]{:S(2)}) collective-permute-start(bf16[64,512]{1,0:T(8,128)(2,1)S(1)} %get-tuple-element.32), channel_id=1, source_target_pairs={{0,1},{1,0},{2,3},{3,2},{4,5},{5,4},{6,7},{7,6},{8,9},{9,8},{10,11... | collective-permute-start | bytes 196616 | tf_op jit(solution)/shard_map/ppermute | solution.py:62

commit v6 on v5

--- a/solution.py
+++ b/solution.py
@@ -11,8 +11,10 @@
 
 LOG2E = math.log2(math.e)
 STATS = 8
+SENDS = 2
+KEY_SENDS = 2
 PIECES = 2
-PART_COST = 1000
+PART_COST = 150000000
 VMEM_LIMIT = 32 * 1024 * 1024
 SMALL_LIMIT = 8 * 1024 * 1024
 BF16 = jnp.bfloat16
@@ -163,186 +165,229 @@
     )(*values)
 
 
-def part_kernel(steps, first, last, heads, sizes, *refs):
+def visit_kernel(groups, side, fresh, resume, finish, heads, sizes, *refs):
     inner, zed = sizes
-    pack_ref, refs = refs[0], refs[1:]
-    if first:
-        blocks, refs = refs[:2], refs[2:]
-        dq_ref, acc_ref, k_ref, v_ref, kt_ref, dqt_ref = refs
-    elif last:
-        k_ref, v_ref, kt_ref, acc_in, dq_ref, kept_ref, sent_ref, dqt_ref, acc_ref = refs
+    refs = list(refs)
+
+    def take(count):
+        taken = refs[:count]
+        del refs[:count]
+        return taken
+
+    jobs = [(g, n) for g, steps in enumerate(groups) for n in range(max(1, len(steps)))]
+    packs = take(len(groups))
+    if fresh:
+        stack_refs = take(KEY_SENDS)
     else:
-        k_ref, v_ref, kt_ref, acc_in, dq_ref, acc_ref, dqt_ref = refs
+        k_ref, v_ref, kt_ref, acc_in = take(4)
+    partials = take(len(jobs)) if resume else None
+    dq_refs = take(len(groups) if resume else len(jobs))
+    sum_refs = take(SENDS if finish and side else 1)
+    if fresh:
+        k_ref, v_ref, kt_ref = take(3)
+    (dqt_ref,) = take(1)
+    acc_ref = take(1)[0] if finish else sum_refs[0]
     me = lax.axis_index("inner")
     z_me = lax.axis_index("z")
     core = lax.axis_index("core")
-    width = dq_ref.shape[1] // heads
-    tok = k_ref.shape[0] // (2 * zed)
+    key_core = 1 - core if side else core
+    keys, width = k_ref.shape
+    tok = keys // zed
     half = tok // 2
     lanes = heads * half
-    front = zed * tok
+    front = zed * half
+    wide = 2 if zed % 2 == 0 else 1
+    size = wide * half
+    tiles = zed // wide
     band_len = inner * half
     bands = 4 * zed
     scale = width**-0.5
     nt = (((1,), (1,)), ((), ()))
     per = lanes // width
     rows_each = 4 * lanes + STATS * 2 * per
-    jobs = pack_ref.shape[0] // rows_each
     lane = lax.broadcasted_iota(jnp.int32, (1, lanes), 1) % half
-    row = lax.broadcasted_iota(jnp.int32, (tok, 1), 0)
-
-    if first:
-        for n, block in enumerate(blocks):
-            for m, s in enumerate(range(zed - 1, -1, -1)):
-                source = 2 * peer(z_me, s, zed) + (1 - core if n else core)
-                for late in range(2):
-                    here = pl.ds(pl.multiple_of(late * front + source * half, half), half)
-                    rows = slice(m * tok + late * half, m * tok + (late + 1) * half)
-                    k_ref[here, :] = block[rows, :width]
-                    v_ref[here, :] = block[rows, width:]
+
+    def positions(late, chip, count):
+        row = lax.broadcasted_iota(jnp.int32, (count, 1), 0)
+        place = row // half
+        source = 2 * jnp.where(late, chip - place, chip + place) + key_core
+        return jnp.where(late, bands - 1 - source, source) * band_len + me * half + row % half
+
+    if fresh:
+        for m, s in enumerate(range(zed - 1, -1, -1)):
+            chip = peer(z_me, s, zed)
+            for late in range(2):
+                here = pl.ds(pl.multiple_of((front + (zed - 1 - chip) * half) if late else chip * half, half), half)
+                stack_ref = stack_refs[m * KEY_SENDS // zed]
+                at = m % (zed // KEY_SENDS) * tok + late * half
+                rows = slice(at, at + half)
+                k_ref[here, :] = stack_ref[rows, :width]
+                v_ref[here, :] = stack_ref[rows, width:]
         kt_ref[...] = k_ref[...].T
 
-    member = peer(me, jnp.where(core == 0, steps[0], steps[-1]), inner) if steps else me
-
-    def tile(keys, values, q, g, lse, delta, mask):
-        s = lax.dot_general(keys, q, nt, preferred_element_type=F32)
-        dp = lax.dot_general(values, g, nt, preferred_element_type=F32)
+    def products(rows, pos, q, g, info, ordered):
+        lse, delta, start, q_pos = info
+        mask = pos >= start
+        if ordered:
+            mask = jnp.logical_and(pos <= q_pos, mask)
+        s = lax.dot_general(k_ref[rows, :], q, nt, preferred_element_type=F32)
+        dp = lax.dot_general(v_ref[rows, :], g, nt, preferred_element_type=F32)
         prob = jnp.where(mask, jnp.exp2(s * (scale * LOG2E) - lse), 0.0)
-        dscore = prob * (dp - delta)
-        return prob.astype(BF16), dscore.astype(BF16)
-
-    def pick(early, pair):
-        return jnp.where(early, pair[0], pair[1])
-
-    for job in range(jobs):
-        base = job * rows_each
-        outer = 2 * z_me + (core if job == 0 else 1 - core)
+        dscore = (prob * (dp - delta)).astype(BF16)
+        prob = prob.astype(BF16)
+        return prob, dscore, q, g, rows
+
+    def sums(prob, dscore, q, g, rows):
+        return (
+            jnp.dot(dscore, q, preferred_element_type=F32),
+            jnp.dot(prob, g, preferred_element_type=F32),
+            jnp.dot(kt_ref[:, rows], dscore, preferred_element_type=F32),
+        )
+
+    for at, (group, second) in enumerate(jobs):
+        steps, pack_ref = groups[group], packs[group]
+        base = second * rows_each
+        outer = 2 * z_me + (1 - core if second else core)
+        member = peer(me, jnp.where(core == 0, steps[0], steps[-1]), inner) if steps else me
         rows = pack_ref[base + 4 * lanes : base + rows_each, :].astype(F32)
         info = []
         for late in range(2):
 
             def stat(n):
-                at = (late * STATS + n) * per
-                return jnp.concatenate([rows[at + i : at + i + 1] for i in range(per)], axis=1)
+                first = (late * STATS + n) * per
+                return jnp.concatenate([rows[first + i : first + i + 1] for i in range(per)], axis=1)
 
             lse = (stat(0) + stat(1) + stat(2)) * LOG2E
             delta = stat(3) + stat(4) + stat(5)
             start = (stat(6) * 256.0 + stat(7)).astype(jnp.int32)
             band = bands - 1 - outer if late else outer
             info.append((lse, delta, start, band * band_len + member * half + lane))
-
-        lse, delta, start, _ = info[1]
-        pos = jnp.concatenate(
-            [(2 * j + row // half) * band_len + me * half + row % half for j in range(zed)], axis=0
-        )
-        q_late = pack_ref[base + lanes : base + 2 * lanes, :]
-        g_late = pack_ref[base + 3 * lanes : base + 4 * lanes, :]
-        prob, dscore = tile(k_ref[:front, :], v_ref[:front, :], q_late, g_late, lse, delta, pos >= start)
-        dk = jnp.dot(dscore, q_late, preferred_element_type=F32)
-        dv = jnp.dot(prob, g_late, preferred_element_type=F32)
-        dqt_ref[:, lanes:] = jnp.dot(kt_ref[:, :front], dscore, preferred_element_type=F32)
-        dqt_ref[:, :lanes] = jnp.zeros((width, lanes), F32)
-        if first:
-            acc_ref[:front, :width] = dk
-            acc_ref[:front, width:] = dv
-            acc_ref[front:, :] = jnp.zeros((front, 2 * width), F32)
-        else:
-            before = acc_in if job == 0 else acc_ref
-            acc_ref[:front, :width] = before[:front, :width] + dk
-            acc_ref[:front, width:] = before[:front, width:] + dv
-            if job == 0:
-                acc_ref[front:, :] = acc_in[front:, :]
-
-        done = []
-        for t in range(zed + 1):
-            early = t <= z_me
-            j = jnp.where(early, t, t - 1)
-            first_key = pl.multiple_of(jnp.where(early, 0, front) + j * tok, tok)
-            first_query = pl.multiple_of(jnp.where(early, 0, lanes), lanes)
-            source = 2 * j + row // half
-            band = jnp.where(early, source, bands - 1 - source)
-            pos = band * band_len + me * half + row % half
-            lse, delta, start, q_pos = (pick(early, (a, b)) for a, b in zip(*info))
-            keys = pl.ds(first_key, tok)
-            q = pack_ref[pl.ds(pl.multiple_of(base + first_query, 16), lanes), :]
-            g = pack_ref[pl.ds(pl.multiple_of(base + 2 * lanes + first_query, 16), lanes), :]
-            mask = jnp.logical_and(pos <= q_pos, pos >= start)
-            prob, dscore = tile(k_ref[keys, :], v_ref[keys, :], q, g, lse, delta, mask)
-            done.append((keys, pl.ds(first_query, lanes), q, g, prob, dscore))
-        parts = []
-        for keys, here, q, g, prob, dscore in done:
-            dk = jnp.dot(dscore, q, preferred_element_type=F32)
-            dv = jnp.dot(prob, g, preferred_element_type=F32)
-            dq = jnp.dot(kt_ref[:, keys], dscore, preferred_element_type=F32)
-            parts.append((keys, here, dk, dv, dq))
-        for keys, here, dk, dv, dq in parts:
-            acc_ref[keys, :width] += dk
-            acc_ref[keys, width:] += dv
-            dqt_ref[:, here] += dq
-
+        q_early, q_late, g_early, g_late = (pack_ref[base + n * lanes : base + (n + 1) * lanes, :] for n in range(4))
+
+        early_all = slice(0, front)
+        early_first = slice(0, size)
+        late_first = slice(front, front + size)
+        one = products(early_all, positions(False, 0, front), q_late, g_late, info[1], False)
+        two = products(late_first, positions(True, zed - 1, size), q_late, g_late, info[1], True)
+        three = products(early_first, positions(False, 0, size), q_early, g_early, info[0], True)
+        moving = []
+        for n in range(tiles - 1):
+            early = n < z_me // wide
+            place = jnp.where(early, n + 1, tiles - 1 - n) * size
+            here = pl.ds(pl.multiple_of(jnp.where(early, 0, front) + place, size), size)
+            chip = jnp.where(early, place // half, zed - 1 - place // half)
+            first = base + jnp.where(early, 0, lanes)
+            q = pack_ref[pl.ds(pl.multiple_of(first, 16), lanes), :]
+            g = pack_ref[pl.ds(pl.multiple_of(first + 2 * lanes, 16), lanes), :]
+            picked = tuple(jnp.where(early, a, b) for a, b in zip(*info))
+            to = pl.ds(pl.multiple_of(jnp.where(early, 0, lanes), lanes), lanes)
+            moving.append((here, to, products(here, positions(jnp.logical_not(early), chip, size), q, g, picked, True)))
+
+        dk0, dv0, dq0 = sums(*one)
+        dk1, dv1, dq1 = sums(*two)
+        dk2, dv2, dq2 = sums(*three)
+        moving = [(here, to, sums(*values)) for here, to, values in moving]
+
+        dqt_ref[:, :lanes] = dq2
+        dqt_ref[:, lanes:] = dq0 + dq1
+        before = None if fresh and at == 0 else acc_in if not fresh and at == 0 else acc_ref
+        for columns, all_early, one_early, one_late in (
+            (slice(0, width), dk0, dk2, dk1),
+            (slice(width, 2 * width), dv0, dv2, dv1),
+        ):
+            pieces = [
+                (early_first, all_early[:size] + one_early),
+                (slice(size, front), all_early[size:]),
+                (late_first, one_late),
+            ]
+            for here, value in pieces:
+                if here.start < here.stop:
+                    acc_ref[here, columns] = value if before is None else before[here, columns] + value
+        if at == 0 and front + size < keys:
+            rest = slice(front + size, keys)
+            acc_ref[rest, :] = jnp.zeros((keys - front - size, 2 * width), F32) if fresh else acc_in[rest, :]
+        for here, to, (dk, dv, dq) in moving:
+            acc_ref[here, :width] += dk
+            acc_ref[here, width:] += dv
+            dqt_ref[:, to] += dq
+
+        if not resume:
+            dq_refs[at][...] = dqt_ref[...]
+            continue
+        dq_ref = dq_refs[group]
         for late in range(2):
-            turned = (dqt_ref[:, late * lanes : (late + 1) * lanes] * scale).T.astype(dq_ref.dtype)
-            to = slice(job * tok + late * half, job * tok + (late + 1) * half)
+            part = slice(late * lanes, (late + 1) * lanes)
+            turned = ((dqt_ref[:, part] + partials[at][:, part]) * scale).T.astype(dq_ref.dtype)
+            to = slice(second * tok + late * half, second * tok + (late + 1) * half)
             for h in range(heads):
                 dq_ref[to, h * width : (h + 1) * width] = turned[h * half : (h + 1) * half]
 
-    if last:
-        low = core == 0
-        for n in range(2 * zed):
-            to = slice(n * half, (n + 1) * half)
-            for columns, factor in ((slice(0, width), scale), (slice(width, 2 * width), 1.0)):
-                one = acc_ref[n * tok : n * tok + half, columns] * factor
-                two = acc_ref[n * tok + half : (n + 1) * tok, columns] * factor
-                kept_ref[to, columns] = jnp.where(low, one, two)
-                sent_ref[to, columns] = jnp.where(low, two, one).astype(sent_ref.dtype)
-
-
-def part(steps, packed, state, last, heads, sizes, tok, width):
+    if finish:
+        each = sum_refs[0].shape[0]
+        for n, sum_ref in enumerate(sum_refs):
+            here = slice(n * each, (n + 1) * each)
+            sum_ref[:, :width] = (acc_ref[here, :width] * scale).astype(sum_ref.dtype)
+            sum_ref[:, width:] = acc_ref[here, width:].astype(sum_ref.dtype)
+
+
+def visit(groups, side, packs, key_state, partials, finish, heads, sizes, tok, width):
     zed = sizes[1]
-    first = not steps
-    jobs = max(1, len(steps))
-    keys = 2 * zed * tok
-    outs = [jax.ShapeDtypeStruct((jobs * tok, heads * width), F32 if first else BF16)]
-    acc = ((keys, 2 * width), F32)
+    fresh, resume = len(key_state) == KEY_SENDS, partials is not None
+    jobs = sum(max(1, len(steps)) for steps in groups)
+    keys = zed * tok
+    if resume:
+        outs = [
+            jax.ShapeDtypeStruct((max(1, len(steps)) * tok, heads * width), BF16 if steps else F32) for steps in groups
+        ]
+    else:
+        outs = [jax.ShapeDtypeStruct((width, heads * tok), F32)] * jobs
+    count = len(outs)
+    pieces = SENDS if finish and side else 1
+    outs += [jax.ShapeDtypeStruct((keys // pieces, 2 * width), BF16 if finish and side else F32)] * pieces
+    if fresh:
+        outs += [jax.ShapeDtypeStruct(s, BF16) for s in ((keys, width), (keys, width), (width, keys))]
     scratch = [pltpu.VMEM((width, heads * tok), F32)]
-    if last:
-        outs += [jax.ShapeDtypeStruct((zed * tok, 2 * width), t) for t in (F32, BF16)]
-        scratch.append(pltpu.VMEM(*acc))
-    else:
-        outs.append(jax.ShapeDtypeStruct(*acc))
-    if first:
-        outs += [jax.ShapeDtypeStruct(s, BF16) for s in ((keys, width), (keys, width), (width, keys))]
-    args = [packed] + list(state)
-    return pl.pallas_call(
-        functools.partial(part_kernel, steps, first, last, heads, sizes),
+    if finish:
+        scratch.append(pltpu.VMEM((keys, 2 * width), F32))
+    args = list(packs) + list(key_state) + list(partials or [])
+    out = pl.pallas_call(
+        functools.partial(visit_kernel, groups, side, fresh, resume, finish, heads, sizes),
         out_shape=outs,
         in_specs=[VMEM] * len(args),
         out_specs=[VMEM] * len(outs),
         scratch_shapes=scratch,
         compiler_params=pltpu.CompilerParams(vmem_limit_bytes=VMEM_LIMIT),
         cost_estimate=pl.CostEstimate(flops=jobs * PART_COST, bytes_accessed=1000, transcendentals=0),
-        name="part",
+        name="visit",
     )(*args)
-
-
-def join_kernel(zed, kept_ref, other_ref, *outs):
+    return out[:count], out[count : count + pieces], out[count + pieces :]
+
+
+def join_kernel(zed, kept_ref, *refs):
+    other_refs, outs = refs[:SENDS], refs[SENDS:]
+    each = other_refs[0].shape[0]
     z_me = lax.axis_index("z")
     tok = outs[0].shape[0]
     half = tok // 2
     for s, out in enumerate(outs):
         for late in range(2):
-            here = pl.ds(pl.multiple_of((late * zed + peer(z_me, s, zed)) * half, half), half)
-            both = kept_ref[here, :] + other_ref[here, :].astype(F32)
+            there = peer(z_me, s, zed)
+            first = pl.multiple_of((2 * zed - 1 - there if late else there) * half, half)
+            if SENDS == 2:
+                other_ref, at = other_refs[late], first - late * each
+            else:
+                other_ref, at = other_refs[0], first
+            both = kept_ref[pl.ds(first, half), :] + other_ref[pl.ds(pl.multiple_of(at, half), half), :].astype(F32)
             out[late * half : (late + 1) * half, :] = both.astype(out.dtype)
 
 
-def join(kept, other, zed):
+def join(kept, others, zed):
     tok, two = kept.shape[0] // zed, kept.shape[1]
     outs = [jax.ShapeDtypeStruct((tok, two), F32 if s == 0 else BF16) for s in range(zed)]
     return pl.pallas_call(
-        functools.partial(join_kernel, zed), out_shape=outs, in_specs=[VMEM] * 2, out_specs=[VMEM] * zed, name="join",
-        compiler_params=pltpu.CompilerParams(vmem_limit_bytes=SMALL_LIMIT),
-    )(kept, other)
+        functools.partial(join_kernel, zed), out_shape=outs, in_specs=[VMEM] * (1 + SENDS), out_specs=[VMEM] * zed, name="join",
+        compiler_params=pltpu.CompilerParams(vmem_limit_bytes=SMALL_LIMIT),
+    )(kept, *others)
 
 
 def split_kernel(ref, *outs):
@@ -415,18 +460,21 @@
     packs = [fetch(chip if len(steps) == 2 else own, steps) for steps in rounds]
     mine = [keys_values] + [fetch_z(keys_values, s) for s in range(1, zed)]
     far = list(range(zed - 1, -1, -1))
-    arrived = stack(*[mine[s] for s in far])
-    out = part((), own, [arrived, swap_cores(arrived)], False, heads, sizes, tok, width)
-    dq_parts = [out[0]]
-    acc, state = out[1], list(out[2:])
-    returned = []
-    for steps, packed in zip(rounds, packs):
-        last = steps == rounds[-1]
-        out = part(steps, packed, state + [acc], last, heads, sizes, tok, width)
-        returned.append(give_back(out[0], steps))
-        acc = out[1]
-    kept, sent = out[1:]
-    joined = join(kept, swap_cores(sent), zed)
+    each = zed // KEY_SENDS
+    arrived = [stack(*[mine[s] for s in far[n * each : (n + 1) * each]]) for n in range(KEY_SENDS)]
+    groups = [()] + rounds[:-1]
+    firsts = [own] + packs[:-1]
+    partials, mine_sums, mine_keys = visit(groups, 0, firsts, arrived, None, False, heads, sizes, tok, width)
+    theirs = [swap_cores(some) for some in arrived]
+    dqs, their_sums, their_keys = visit(groups, 1, firsts, theirs, partials, False, heads, sizes, tok, width)
+    returned = [give_back(dq, steps) for dq, steps in zip(dqs[1:], rounds)]
+    ends = rounds[-1:]
+    their_state, mine_state = list(their_keys) + list(their_sums), list(mine_keys) + list(mine_sums)
+    partials, sent, _ = visit(ends, 1, packs[-1:], their_state, None, True, heads, sizes, tok, width)
+    (dq_last,), (kept,), _ = visit(ends, 0, packs[-1:], mine_state, partials, True, heads, sizes, tok, width)
+    returned.append(give_back(dq_last, ends[0]))
+    dq_parts = [dqs[0]]
+    joined = join(kept, [swap_cores(some) for some in sent], zed)
     dkv_parts = [joined[0]] + [give_back_z(joined[s], s) for s in range(zed - 1, 0, -1)]
     for steps, back in zip(rounds, returned):
         dq_parts.append(back)

time: 35.2 us -> 34.9 us (level)
  waiting for transfers between devices: 9.5 us -> 8.06 us
  Pallas kernels: 7.02 us -> 7.54 us
  starting transfers between devices: 17.8 us -> 18.3 us
    ppermute x9 -> x11, waiting for transfers between devices: 1.54 us -> 0.19 us  [swap_cores(): return lax.ppermute(value, 'core', [(0, 1), (1, 0)])]
    ppermute x9 -> x11, starting transfers between devices: 2.25 us -> 3.29 us  [swap_cores(): return lax.ppermute(value, 'core', [(0, 1), (1, 0)])]
    pallas_call x3 -> x4, Pallas kernels: 4.74 us -> 5.27 us  [visit(): pl.pallas_call(functools.partial(visit_kernel, groups, side, fresh, resum...]
    ppermute x3, waiting for transfers between devices: 2.63 us -> 3.07 us  [give_back_z(): lax.ppermute(value, 'z', [(z, peer(z, step, count)) for z in range(count)])]
    ppermute x3, starting transfers between devices: 4.01 us -> 3.57 us  [give_back_z(): lax.ppermute(value, 'z', [(z, peer(z, step, count)) for z in range(count)])]
  transfers between devices with their start and end apart: 19 -> 21, of which waited for: 8 -> 6; matrix products, arithmetic and copies ran while one was open for 0% -> 0% of each run, Pallas kernels for 14% -> 19%
where the time goes in v6:
time: 34.9 us; the launch traced here: 34.8 us
  starting transfers between devices  18.3 us (52%)
  waiting for transfers between devices  8.06 us (23%)
  Pallas kernels  7.54 us (22%)
  between operations  0.81 us (2%)
    pallas_call x4, Pallas kernels, visit(): pl.pallas_call(functools.partial(visit_kernel, groups, side, fresh, resum...  5.27 us
    ppermute x3, starting transfers between devices, fetch_z(): lax.ppermute(value, 'z', [(peer(z, step, count), z) for z in range(count)])  4.39 us
    ppermute x2, starting transfers between devices, fetch(): lax.ppermute(value, ('inner', 'core'), inner_pairs(steps, lax.axis_size('...  4.16 us
    ppermute x3, starting transfers between devices, give_back_z(): lax.ppermute(value, 'z', [(z, peer(z, step, count)) for z in range(count)])  3.57 us
    ppermute x3, waiting for transfers between devices, fetch_z(): lax.ppermute(value, 'z', [(peer(z, step, count), z) for z in range(count)])  3.57 us
    ppermute x11, starting transfers between devices, swap_cores(): return lax.ppermute(value, 'core', [(0, 1), (1, 0)])  3.29 us
    ppermute x3, waiting for transfers between devices, give_back_z(): lax.ppermute(value, 'z', [(z, peer(z, step, count)) for z in range(count)])  3.07 us
    ppermute x2, starting transfers between devices, give_back(): return lax.ppermute(value, ('inner', 'core'), [(b, a) for a, b in pairs])  2.92 us
  transfers between devices with their start and end apart: 21, of which 6 were waited for; matrix products, arithmetic and copies ran while one was open for 0% of the time, Pallas kernels for 19%

profile of v6, /device:TPU:0, one launch (start us, length us, event | category | flops | bytes accessed | tf_op | source)
XLA Modules:
  0.0 34.8 jit_solution(5701917049595564069)
XLA Ops:
  0.6 0.5 %collective-permute-start = (bf16[128,512]{1,0:T(8,128)(2,1)}, bf16[128,512]{1,0:T(8,128)(2,1)S(1)}, u32[]{:S(2)}, u32[]{:S(2)}) collective-permute-start(bf16[128,512]{1,0:T(8,128)(2,1)} %refs_0_.1), channel_id=1, source_target_pairs={{0,1},{1,0},{2,3},{3,2},{4,5},{5,4},{6,7},{7,6},{8,9},{9,8},{10,11... | collective-permute-start | bytes 393224 | tf_op jit(solution)/shard_map/ppermute | solution.py:64
  1.2 0.4 %collective-permute-start.2 = (bf16[128,512]{1,0:T(8,128)(2,1)}, bf16[128,512]{1,0:T(8,128)(2,1)S(1)}, u32[]{:S(2)}, u32[]{:S(2)}) collective-permute-start(bf16[128,512]{1,0:T(8,128)(2,1)} %refs_2_.1), channel_id=1, source_target_pairs={{0,1},{1,0},{2,3},{3,2},{4,5},{5,4},{6,7},{7,6},{8,9},{9,8},{10,11... | collective-permute-start | bytes 393224 | tf_op jit(solution)/shard_map/ppermute | solution.py:64
  1.8 0.4 %collective-permute-start.4 = (s32[128]{0:T(128)S(1)}, s32[128]{0:T(128)S(1)}, u32[]{:S(2)}, u32[]{:S(2)}) collective-permute-start(s32[128]{0:T(128)S(1)} %copy-done.1), channel_id=1, source_target_pairs={{0,1},{1,0},{2,3},{3,2},{4,5},{5,4},{6,7},{7,6},{8,9},{9,8},{10,11... | collective-permute-start | bytes 1544 | tf_op jit(solution)/shard_map/ppermute | solution.py:64
  2.2 1.3 %pack.1.refs_0_ = bf16[1056,128]{1,0:T(8,128)(2,1)S(1)} custom-call(bf16[128,512]{1,0:T(8,128)(2,1)} %refs_0_.1, bf16[128,512]{1,0:T(8,128)(2,1)} %refs_1_.2, bf16[128,512]{1,0:T(8,128)(2,1)} %refs_2_.1, f32[4,128]{1,0:T(4,128)} %bitcast.5, s32[1,128]{1,0:T(1,128)} %bitcast.6), custom_call_target="tpu_custom_call" | custom-call | tf_op jit(solution)/shard_map/pack/pallas_call | solution.py:120
  3.7 2.6 %collective-permute-start.5 = (bf16[2112,128]{1,0:T(8,128)(2,1)S(1)}, bf16[2112,128]{1,0:T(8,128)(2,1)S(1)}, u32[]{:S(2)}, u32[]{:S(2)}) collective-permute-start(bf16[2112,128]{1,0:T(8,128)(2,1)S(1)} %pack_chip.1), channel_id=1, source_target_pairs={{8,0},{17,1},{0,8},{25,9},{24,16},{1,17},{16,24},{9,25},{10,2},{19... | collective-permute-start | bytes 1622024 | tf_op jit(solution)/shard_map/ppermute | solution.py:45
  6.3 3.6 %collective-permute-start.6 = (bf16[128,256]{1,0:T(8,128)(2,1)S(1)}, bf16[128,256]{1,0:T(8,128)(2,1)S(1)}, u32[]{:S(2)}, u32[]{:S(2)}) collective-permute-start(bf16[128,256]{1,0:T(8,128)(2,1)S(1)} %copy-done), channel_id=1, source_target_pairs={{6,0},{4,2},{2,4},{0,6},{7,1},{5,3},{3,5},{1,7},{14,8},{12,10},{10... | collective-permute-start | bytes 196616 | tf_op jit(solution)/shard_map/ppermute | solution.py:55
  10.0 0.8 %collective-permute-start.9 = (bf16[128,256]{1,0:T(8,128)(2,1)S(1)}, bf16[128,256]{1,0:T(8,128)(2,1)S(1)}, u32[]{:S(2)}, u32[]{:S(2)}) collective-permute-start(bf16[128,256]{1,0:T(8,128)(2,1)S(1)} %copy-done), channel_id=1, source_target_pairs={{2,0},{0,2},{6,4},{4,6},{3,1},{1,3},{7,5},{5,7},{10,8},{8,10},{14,... | collective-permute-start | bytes 196616 | tf_op jit(solution)/shard_map/ppermute | solution.py:55
  10.7 1.5 %collective-permute-start.12 = (bf16[1056,128]{1,0:T(8,128)(2,1)S(1)}, bf16[1056,128]{1,0:T(8,128)(2,1)S(1)}, u32[]{:S(2)}, u32[]{:S(2)}) collective-permute-start(bf16[1056,128]{1,0:T(8,128)(2,1)S(1)} %pack.1.refs_0_), channel_id=1, source_target_pairs={{24,0},{25,1},{16,8},{17,9},{8,16},{9,17},{0,24},{1,25},{26,2},{27... | collective-permute-start | bytes 811016 | tf_op jit(solution)/shard_map/ppermute | solution.py:45
  12.6 3.2 %collective-permute-done.7.refs_1_ = bf16[128,256]{1,0:T(8,128)(2,1)S(1)} collective-permute-done((bf16[128,256]{1,0:T(8,128)(2,1)S(1)}, bf16[128,256]{1,0:T(8,128)(2,1)S(1)}, u32[]{:S(2)}, u32[]{:S(2)}) %collective-permute-start.7) | collective-permute-done | bytes 65568 | tf_op jit(solution)/shard_map/ppermute | solution.py:55
  16.0 0.5 %collective-permute-start.10 = (bf16[256,256]{1,0:T(8,128)(2,1)S(1)}, bf16[256,256]{1,0:T(8,128)(2,1)S(1)}, u32[]{:S(2)}, u32[]{:S(2)}) collective-permute-start(bf16[256,256]{1,0:T(8,128)(2,1)S(1)} %stack.3.refs_3_), channel_id=1, source_target_pairs={{0,1},{1,0},{2,3},{3,2},{4,5},{5,4},{6,7},{7,6},{8,9},{9,8},{10,11... | collective-permute-start | bytes 393224 | tf_op jit(solution)/shard_map/ppermute | solution.py:64
  16.5 1.7 %visit.4 = (f32[128,512]{1,0:T(8,128)S(1)}, f32[128,512]{1,0:T(8,128)S(1)}, f32[128,512]{1,0:T(8,128)S(1)}, f32[512,256]{1,0:T(8,128)S(1)}, bf16[512,128]{1,0:T(...) custom-call(bf16[1056,128]{1,0:T(8,128)(2,1)S(1)} %pack.1.refs_0_, ...), custom_call_target="tpu_custom_call" | custom-call | flops 450000000 | bytes 1000 | tf_op jit(solution)/shard_map/visit/pallas_call | solution.py:353
  18.3 1.9 %visit.5 = (f32[128,512]{1,0:T(8,128)S(1)}, bf16[256,512]{1,0:T(8,128)(2,1)S(1)}, f32[512,256]{1,0:T(8,128)S(1)}, bf16[512,128]{1,0:T(8,128)(2,1)S(1)}, bf16[512...) custom-call(bf16[1056,128]{1,0:T(8,128)(2,1)S(1)} %pack.1.refs_0_, ...), custom_call_target="tpu_custom_call" | custom-call | flops 450000000 | bytes 1000 | tf_op jit(solution)/shard_map/visit/pallas_call | solution.py:353
  20.2 1.2 %collective-permute-start.11 = (bf16[256,512]{1,0:T(8,128)(2,1)S(1)}, bf16[256,512]{1,0:T(8,128)(2,1)S(1)}, u32[]{:S(2)}, u32[]{:S(2)}) collective-permute-start(bf16[256,512]{1,0:T(8,128)(2,1)S(1)} %get-tuple-element.32), channel_id=1, source_target_pairs={{0,8},{1,17},{8,0},{9,25},{16,24},{17,1},{24,16},{25,9},{2,10},{3,... | collective-permute-start | bytes 786440 | tf_op jit(solution)/shard_map/ppermute | solution.py:50
  21.5 0.7 %visit.6 = (f32[128,512]{1,0:T(8,128)S(1)}, bf16[256,256]{1,0:T(8,128)(2,1)S(1)}, bf16[256,256]{1,0:T(8,128)(2,1)S(1)}) custom-call(bf16[1056,128]{1,0:T(8,128)(2,1)S(1)} %collective-permute-done.12.refs_0_, bf16[512,128]{1,0:T(8,128)(2,1)S(1)} %get-tuple-element.37.refs_1_, bf16[512,128]{1,0:T(8,128)(2,1)S(1)} %get-tuple-element.38.refs_2_, ...), custom_call_target="tpu_custom_call" | custom-call | flops 150000000 | bytes 1000 | tf_op jit(solution)/shard_map/visit/pallas_call | solution.py:353
  22.3 0.5 %collective-permute-start.14 = (bf16[256,256]{1,0:T(8,128)(2,1)S(1)}, bf16[256,256]{1,0:T(8,128)(2,1)S(1)}, u32[]{:S(2)}, u32[]{:S(2)}) collective-permute-start(bf16[256,256]{1,0:T(8,128)(2,1)S(1)} %get-tuple-element.44), channel_id=1, source_target_pairs={{0,1},{1,0},{2,3},{3,2},{4,5},{5,4},{6,7},{7,6},{8,9},{9,8},{10,11... | collective-permute-start | bytes 393224 | tf_op jit(solution)/shard_map/ppermute | solution.py:64
  22.8 0.8 %visit.7 = (bf16[128,512]{1,0:T(8,128)(2,1)S(1)}, f32[512,256]{1,0:T(8,128)S(1)}) custom-call(bf16[1056,128]{1,0:T(8,128)(2,1)S(1)} %collective-permute-done.12.refs_0_, bf16[512,128]{1,0:T(8,128)(2,1)S(1)} %get-tuple-element.33.refs_1_, bf16[512,128]{1,0:T(8,128)(2,1)S(1)} %get-tuple-element.34.refs_2_, bf16[128,512]{1,0:T(8,128)(2,1)S(1)} %get-tuple-element.35.refs_3_, ...), custom_call_target="tpu_custom_call" | custom-call | flops 150000000 | bytes 1000 | tf_op jit(solution)/shard_map/visit/pallas_call | solution.py:353
  23.8 2.2 %collective-permute-start.15 = (bf16[128,256]{1,0:T(8,128)(2,1)S(1)}, bf16[128,256]{1,0:T(8,128)(2,1)S(1)}, u32[]{:S(2)}, u32[]{:S(2)}) collective-permute-start(bf16[128,256]{1,0:T(8,128)(2,1)S(1)} %get-tuple-element.45), channel_id=1, source_target_pairs={{0,4},{2,6},{4,0},{6,2},{1,5},{3,7},{5,1},{7,3},{8,12},{10,14},{12... | collective-permute-start | bytes 196616 | tf_op jit(solution)/shard_map/ppermute | solution.py:60
  26.0 1.7 %collective-permute-start.18 = (bf16[128,512]{1,0:T(8,128)(2,1)S(1)}, bf16[128,512]{1,0:T(8,128)(2,1)S(1)}, u32[]{:S(2)}, u32[]{:S(2)}) collective-permute-start(bf16[128,512]{1,0:T(8,128)(2,1)S(1)} %get-tuple-element.49), channel_id=1, source_target_pairs={{0,24},{1,25},{8,16},{9,17},{16,8},{17,9},{24,0},{25,1},{2,26},{3,... | collective-permute-start | bytes 393224 | tf_op jit(solution)/shard_map/ppermute | solution.py:50
  27.7 1.2 %collective-permute-start.19 = (bf16[128,256]{1,0:T(8,128)(2,1)S(1)}, bf16[128,256]{1,0:T(8,128)(2,1)S(1)}, u32[]{:S(2)}, u32[]{:S(2)}) collective-permute-start(bf16[128,256]{1,0:T(8,128)(2,1)S(1)} %get-tuple-element.51), channel_id=1, source_target_pairs={{0,6},{2,4},{4,2},{6,0},{1,7},{3,5},{5,3},{7,1},{8,14},{10,12},{12... | collective-permute-start | bytes 196616 | tf_op jit(solution)/shard_map/ppermute | solution.py:60
  29.1 1.4 %collective-permute-done.15.refs_7_ = bf16[128,256]{1,0:T(8,128)(2,1)S(1)} collective-permute-done((bf16[128,256]{1,0:T(8,128)(2,1)S(1)}, bf16[128,256]{1,0:T(8,128)(2,1)S(1)}, u32[]{:S(2)}, u32[]{:S(2)}) %collective-permute-start.15) | collective-permute-done | bytes 65568 | tf_op jit(solution)/shard_map/ppermute | solution.py:60
  30.6 0.5 %collective-permute-start.17 = (bf16[64,512]{1,0:T(8,128)(2,1)S(1)}, bf16[64,512]{1,0:T(8,128)(2,1)S(1)}, u32[]{:S(2)}, u32[]{:S(2)}) collective-permute-start(bf16[64,512]{1,0:T(8,128)(2,1)S(1)} %get-tuple-element.48), channel_id=1, source_target_pairs={{0,1},{1,0},{2,3},{3,2},{4,5},{5,4},{6,7},{7,6},{8,9},{9,8},{10,11... | collective-permute-start | bytes 196616 | tf_op jit(solution)/shard_map/ppermute | solution.py:64
  31.1 1.2 %collective-permute-done.18.refs_4_ = bf16[128,512]{1,0:T(8,128)(2,1)S(1)} collective-permute-done((bf16[128,512]{1,0:T(8,128)(2,1)S(1)}, bf16[128,512]{1,0:T(8,128)(2,1)S(1)}, u32[]{:S(2)}, u32[]{:S(2)}) %collective-permute-start.18) | collective-permute-done | bytes 131104 | tf_op jit(solution)/shard_map/ppermute | solution.py:50
  32.3 1.7 %collective-permute-done.19.refs_6_ = bf16[128,256]{1,0:T(8,128)(2,1)S(1)} collective-permute-done((bf16[128,256]{1,0:T(8,128)(2,1)S(1)}, bf16[128,256]{1,0:T(8,128)(2,1)S(1)}, u32[]{:S(2)}, u32[]{:S(2)}) %collective-permute-start.19) | collective-permute-done | bytes 65568 | tf_op jit(solution)/shard_map/ppermute | solution.py:60
  34.0 0.7 %totals.1 = (bf16[128,512]{1,0:T(8,128)(2,1)}, bf16[128,256]{1,0:T(8,128)(2,1)}) custom-call(f32[128,512]{1,0:T(8,128)S(1)} %get-tuple-element.31.refs_0_, bf16[256,512]{1,0:T(8,128)(2,1)S(1)} %collective-permute-done.11.ref.refs_1_, bf16[64,512]{1,0:T(8,128)(2,1)S(1)} %collective-permute-done.16.refs_2_, ...), custom_call_target="tpu_custom_call" | custom-call | tf_op jit(solution)/shard_map/totals/pallas_call | solution.py:437
  (33 shorter events, 1.4 us)
Async XLA Ops:
  0.6 1.1 %copy-start.1 = (s32[128]{0:T(128)S(1)}, s32[128]{0:T(128)}, u32[]{:S(2)}) copy-start(s32[128]{0:T(128)} %param.11) | copy-start | bytes 1540
  0.6 2.8 %collective-permute-start = (bf16[128,512]{1,0:T(8,128)(2,1)}, bf16[128,512]{1,0:T(8,128)(2,1)S(1)}, u32[]{:S(2)}, u32[]{:S(2)}) collective-permute-start(bf16[128,512]{1,0:T(8,128)(2,1)} %refs_0_.1), channel_id=1, source_target_pairs={{0,1},{1,0},{2,3},{3,2},{4,5},{5,4},{6,7},{7,6},{8,9},{9,8},{10,11... | collective-permute-start | bytes 393224 | tf_op jit(solution)/shard_map/ppermute | solution.py:64
  1.2 2.3 %collective-permute-start.1 = (bf16[128,512]{1,0:T(8,128)(2,1)}, bf16[128,512]{1,0:T(8,128)(2,1)S(1)}, u32[]{:S(2)}, u32[]{:S(2)}) collective-permute-start(bf16[128,512]{1,0:T(8,128)(2,1)} %refs_1_.2), channel_id=1, source_target_pairs={{0,1},{1,0},{2,3},{3,2},{4,5},{5,4},{6,7},{7,6},{8,9},{9,8},{10,11... | collective-permute-start | bytes 393224 | tf_op jit(solution)/shard_map/ppermute | solution.py:64
  1.2 2.3 %collective-permute-start.2 = (bf16[128,512]{1,0:T(8,128)(2,1)}, bf16[128,512]{1,0:T(8,128)(2,1)S(1)}, u32[]{:S(2)}, u32[]{:S(2)}) collective-permute-start(bf16[128,512]{1,0:T(8,128)(2,1)} %refs_2_.1), channel_id=1, source_target_pairs={{0,1},{1,0},{2,3},{3,2},{4,5},{5,4},{6,7},{7,6},{8,9},{9,8},{10,11... | collective-permute-start | bytes 393224 | tf_op jit(solution)/shard_map/ppermute | solution.py:64
  1.7 1.8 %collective-permute-start.3 = (f32[4,128]{1,0:T(4,128)}, f32[4,128]{1,0:T(4,128)S(1)}, u32[]{:S(2)}, u32[]{:S(2)}) collective-permute-start(f32[4,128]{1,0:T(4,128)} %bitcast.4), channel_id=1, source_target_pairs={{0,1},{1,0},{2,3},{3,2},{4,5},{5,4},{6,7},{7,6},{8,9},{9,8},{10,11... | collective-permute-start | bytes 6152 | tf_op jit(solution)/shard_map/ppermute | solution.py:64
  1.8 1.7 %collective-permute-start.4 = (s32[128]{0:T(128)S(1)}, s32[128]{0:T(128)S(1)}, u32[]{:S(2)}, u32[]{:S(2)}) collective-permute-start(s32[128]{0:T(128)S(1)} %copy-done.1), channel_id=1, source_target_pairs={{0,1},{1,0},{2,3},{3,2},{4,5},{5,4},{6,7},{7,6},{8,9},{9,8},{10,11... | collective-permute-start | bytes 1544 | tf_op jit(solution)/shard_map/ppermute | solution.py:64
  3.5 2.8 %copy-start = (bf16[128,256]{1,0:T(8,128)(2,1)S(1)}, bf16[128,256]{1,0:T(8,128)(2,1)}, u32[]{:S(2)}) copy-start(bf16[128,256]{1,0:T(8,128)(2,1)} %refs_1_.3) | copy-start | bytes 196612
  3.7 12.8 %collective-permute-start.5 = (bf16[2112,128]{1,0:T(8,128)(2,1)S(1)}, bf16[2112,128]{1,0:T(8,128)(2,1)S(1)}, u32[]{:S(2)}, u32[]{:S(2)}) collective-permute-start(bf16[2112,128]{1,0:T(8,128)(2,1)S(1)} %pack_chip.1), channel_id=1, source_target_pairs={{8,0},{17,1},{0,8},{25,9},{24,16},{1,17},{16,24},{9,25},{10,2},{19... | collective-permute-start | bytes 1622024 | tf_op jit(solution)/shard_map/ppermute | solution.py:45
  6.3 6.3 %collective-permute-start.6 = (bf16[128,256]{1,0:T(8,128)(2,1)S(1)}, bf16[128,256]{1,0:T(8,128)(2,1)S(1)}, u32[]{:S(2)}, u32[]{:S(2)}) collective-permute-start(bf16[128,256]{1,0:T(8,128)(2,1)S(1)} %copy-done), channel_id=1, source_target_pairs={{6,0},{4,2},{2,4},{0,6},{7,1},{5,3},{3,5},{1,7},{14,8},{12,10},{10... | collective-permute-start | bytes 196616 | tf_op jit(solution)/shard_map/ppermute | solution.py:55
  9.9 5.9 %collective-permute-start.7 = (bf16[128,256]{1,0:T(8,128)(2,1)S(1)}, bf16[128,256]{1,0:T(8,128)(2,1)S(1)}, u32[]{:S(2)}, u32[]{:S(2)}) collective-permute-start(bf16[128,256]{1,0:T(8,128)(2,1)S(1)} %copy-done), channel_id=1, source_target_pairs={{4,0},{6,2},{0,4},{2,6},{5,1},{7,3},{1,5},{3,7},{12,8},{14,10},{8,... | collective-permute-start | bytes 196616 | tf_op jit(solution)/shard_map/ppermute | solution.py:55
  10.0 6.0 %collective-permute-start.9 = (bf16[128,256]{1,0:T(8,128)(2,1)S(1)}, bf16[128,256]{1,0:T(8,128)(2,1)S(1)}, u32[]{:S(2)}, u32[]{:S(2)}) collective-permute-start(bf16[128,256]{1,0:T(8,128)(2,1)S(1)} %copy-done), channel_id=1, source_target_pairs={{2,0},{0,2},{6,4},{4,6},{3,1},{1,3},{7,5},{5,7},{10,8},{8,10},{14,... | collective-permute-start | bytes 196616 | tf_op jit(solution)/shard_map/ppermute | solution.py:55
  10.7 10.7 %collective-permute-start.12 = (bf16[1056,128]{1,0:T(8,128)(2,1)S(1)}, bf16[1056,128]{1,0:T(8,128)(2,1)S(1)}, u32[]{:S(2)}, u32[]{:S(2)}) collective-permute-start(bf16[1056,128]{1,0:T(8,128)(2,1)S(1)} %pack.1.refs_0_), channel_id=1, source_target_pairs={{24,0},{25,1},{16,8},{17,9},{8,16},{9,17},{0,24},{1,25},{26,2},{27... | collective-permute-start | bytes 811016 | tf_op jit(solution)/shard_map/ppermute | solution.py:45
  15.9 2.4 %collective-permute-start.8 = (bf16[256,256]{1,0:T(8,128)(2,1)S(1)}, bf16[256,256]{1,0:T(8,128)(2,1)S(1)}, u32[]{:S(2)}, u32[]{:S(2)}) collective-permute-start(bf16[256,256]{1,0:T(8,128)(2,1)S(1)} %stack.2.refs_2_), channel_id=1, source_target_pairs={{0,1},{1,0},{2,3},{3,2},{4,5},{5,4},{6,7},{7,6},{8,9},{9,8},{10,11... | collective-permute-start | bytes 393224 | tf_op jit(solution)/shard_map/ppermute | solution.py:64
  16.0 2.3 %collective-permute-start.10 = (bf16[256,256]{1,0:T(8,128)(2,1)S(1)}, bf16[256,256]{1,0:T(8,128)(2,1)S(1)}, u32[]{:S(2)}, u32[]{:S(2)}) collective-permute-start(bf16[256,256]{1,0:T(8,128)(2,1)S(1)} %stack.3.refs_3_), channel_id=1, source_target_pairs={{0,1},{1,0},{2,3},{3,2},{4,5},{5,4},{6,7},{7,6},{8,9},{9,8},{10,11... | collective-permute-start | bytes 393224 | tf_op jit(solution)/shard_map/ppermute | solution.py:64
  20.2 10.3 %collective-permute-start.11 = (bf16[256,512]{1,0:T(8,128)(2,1)S(1)}, bf16[256,512]{1,0:T(8,128)(2,1)S(1)}, u32[]{:S(2)}, u32[]{:S(2)}) collective-permute-start(bf16[256,512]{1,0:T(8,128)(2,1)S(1)} %get-tuple-element.32), channel_id=1, source_target_pairs={{0,8},{1,17},{8,0},{9,25},{16,24},{17,1},{24,16},{25,9},{2,10},{3,... | collective-permute-start | bytes 786440 | tf_op jit(solution)/shard_map/ppermute | solution.py:50
  22.2 1.4 %collective-permute-start.13 = (bf16[256,256]{1,0:T(8,128)(2,1)S(1)}, bf16[256,256]{1,0:T(8,128)(2,1)S(1)}, u32[]{:S(2)}, u32[]{:S(2)}) collective-permute-start(bf16[256,256]{1,0:T(8,128)(2,1)S(1)} %get-tuple-element.43), channel_id=1, source_target_pairs={{0,1},{1,0},{2,3},{3,2},{4,5},{5,4},{6,7},{7,6},{8,9},{9,8},{10,11... | collective-permute-start | bytes 393224 | tf_op jit(solution)/shard_map/ppermute | solution.py:64
  22.3 1.5 %collective-permute-start.14 = (bf16[256,256]{1,0:T(8,128)(2,1)S(1)}, bf16[256,256]{1,0:T(8,128)(2,1)S(1)}, u32[]{:S(2)}, u32[]{:S(2)}) collective-permute-start(bf16[256,256]{1,0:T(8,128)(2,1)S(1)} %get-tuple-element.44), channel_id=1, source_target_pairs={{0,1},{1,0},{2,3},{3,2},{4,5},{5,4},{6,7},{7,6},{8,9},{9,8},{10,11... | collective-permute-start | bytes 393224 | tf_op jit(solution)/shard_map/ppermute | solution.py:64
  23.8 6.7 %collective-permute-start.15 = (bf16[128,256]{1,0:T(8,128)(2,1)S(1)}, bf16[128,256]{1,0:T(8,128)(2,1)S(1)}, u32[]{:S(2)}, u32[]{:S(2)}) collective-permute-start(bf16[128,256]{1,0:T(8,128)(2,1)S(1)} %get-tuple-element.45), channel_id=1, source_target_pairs={{0,4},{2,6},{4,0},{6,2},{1,5},{3,7},{5,1},{7,3},{8,12},{10,14},{12... | collective-permute-start | bytes 196616 | tf_op jit(solution)/shard_map/ppermute | solution.py:60
  26.0 6.3 %collective-permute-start.18 = (bf16[128,512]{1,0:T(8,128)(2,1)S(1)}, bf16[128,512]{1,0:T(8,128)(2,1)S(1)}, u32[]{:S(2)}, u32[]{:S(2)}) collective-permute-start(bf16[128,512]{1,0:T(8,128)(2,1)S(1)} %get-tuple-element.49), channel_id=1, source_target_pairs={{0,24},{1,25},{8,16},{9,17},{16,8},{17,9},{24,0},{25,1},{2,26},{3,... | collective-permute-start | bytes 393224 | tf_op jit(solution)/shard_map/ppermute | solution.py:50
  27.7 6.3 %collective-permute-start.19 = (bf16[128,256]{1,0:T(8,128)(2,1)S(1)}, bf16[128,256]{1,0:T(8,128)(2,1)S(1)}, u32[]{:S(2)}, u32[]{:S(2)}) collective-permute-start(bf16[128,256]{1,0:T(8,128)(2,1)S(1)} %get-tuple-element.51), channel_id=1, source_target_pairs={{0,6},{2,4},{4,2},{6,0},{1,7},{3,5},{5,3},{7,1},{8,14},{10,12},{12... | collective-permute-start | bytes 196616 | tf_op jit(solution)/shard_map/ppermute | solution.py:60
  29.0 5.1 %collective-permute-start.20 = (bf16[128,256]{1,0:T(8,128)(2,1)S(1)}, bf16[128,256]{1,0:T(8,128)(2,1)S(1)}, u32[]{:S(2)}, u32[]{:S(2)}) collective-permute-start(bf16[128,256]{1,0:T(8,128)(2,1)S(1)} %get-tuple-element.53), channel_id=1, source_target_pairs={{0,2},{2,0},{4,6},{6,4},{1,3},{3,1},{5,7},{7,5},{8,10},{10,8},{12,... | collective-permute-start | bytes 196616 | tf_op jit(solution)/shard_map/ppermute | solution.py:60
  30.6 3.5 %collective-permute-start.16 = (bf16[64,512]{1,0:T(8,128)(2,1)S(1)}, bf16[64,512]{1,0:T(8,128)(2,1)S(1)}, u32[]{:S(2)}, u32[]{:S(2)}) collective-permute-start(bf16[64,512]{1,0:T(8,128)(2,1)S(1)} %get-tuple-element.47), channel_id=1, source_target_pairs={{0,1},{1,0},{2,3},{3,2},{4,5},{5,4},{6,7},{7,6},{8,9},{9,8},{10,11... | collective-permute-start | bytes 196616 | tf_op jit(solution)/shard_map/ppermute | solution.py:64
  30.6 3.4 %collective-permute-start.17 = (bf16[64,512]{1,0:T(8,128)(2,1)S(1)}, bf16[64,512]{1,0:T(8,128)(2,1)S(1)}, u32[]{:S(2)}, u32[]{:S(2)}) collective-permute-start(bf16[64,512]{1,0:T(8,128)(2,1)S(1)} %get-tuple-element.48), channel_id=1, source_target_pairs={{0,1},{1,0},{2,3},{3,2},{4,5},{5,4},{6,7},{7,6},{8,9},{9,8},{10,11... | collective-permute-start | bytes 196616 | tf_op jit(solution)/shard_map/ppermute | solution.py:64

commit v7 on v6

--- a/solution.py
+++ b/solution.py
@@ -479,7 +479,8 @@
     for steps, back in zip(rounds, returned):
         dq_parts.append(back)
         if len(steps) == 2:
-            back, dkv_parts[2] = lax.optimization_barrier((back, dkv_parts[2]))
+            last = min(2, zed - 1)
+            back, dkv_parts[last] = lax.optimization_barrier((back, dkv_parts[last]))
             dq_parts += [swap_cores(piece) for piece in split(back, PIECES)]
     return tuple(totals([dq_parts, dkv_parts], tok))
 

time: 34.9 us -> 34.9 us (level)
  no operation moved by 1% of the time
where the time goes in v7:
time: 34.9 us; the launch traced here: 34.8 us
  starting transfers between devices  18.3 us (52%)
  waiting for transfers between devices  8.06 us (23%)
  Pallas kernels  7.54 us (22%)
  between operations  0.81 us (2%)
    pallas_call x4, Pallas kernels, visit(): pl.pallas_call(functools.partial(visit_kernel, groups, side, fresh, resum...  5.27 us
    ppermute x3, starting transfers between devices, fetch_z(): lax.ppermute(value, 'z', [(peer(z, step, count), z) for z in range(count)])  4.39 us
    ppermute x2, starting transfers between devices, fetch(): lax.ppermute(value, ('inner', 'core'), inner_pairs(steps, lax.axis_size('...  4.16 us
    ppermute x3, starting transfers between devices, give_back_z(): lax.ppermute(value, 'z', [(z, peer(z, step, count)) for z in range(count)])  3.57 us
    ppermute x3, waiting for transfers between devices, fetch_z(): lax.ppermute(value, 'z', [(peer(z, step, count), z) for z in range(count)])  3.57 us
    ppermute x11, starting transfers between devices, swap_cores(): return lax.ppermute(value, 'core', [(0, 1), (1, 0)])  3.29 us
    ppermute x3, waiting for transfers between devices, give_back_z(): lax.ppermute(value, 'z', [(z, peer(z, step, count)) for z in range(count)])  3.07 us
    ppermute x2, starting transfers between devices, give_back(): return lax.ppermute(value, ('inner', 'core'), [(b, a) for a, b in pairs])  2.92 us
  transfers between devices with their start and end apart: 21, of which 6 were waited for; matrix products, arithmetic and copies ran while one was open for 0% of the time, Pallas kernels for 19%

profile of v7, /device:TPU:0, one launch (start us, length us, event | category | flops | bytes accessed | tf_op | source)
XLA Modules:
  0.0 34.8 jit_solution(5701917049595564069)
XLA Ops:
  0.6 0.5 %collective-permute-start = (bf16[128,512]{1,0:T(8,128)(2,1)}, bf16[128,512]{1,0:T(8,128)(2,1)S(1)}, u32[]{:S(2)}, u32[]{:S(2)}) collective-permute-start(bf16[128,512]{1,0:T(8,128)(2,1)} %refs_0_.1), channel_id=1, source_target_pairs={{0,1},{1,0},{2,3},{3,2},{4,5},{5,4},{6,7},{7,6},{8,9},{9,8},{10,11... | collective-permute-start | bytes 393224 | tf_op jit(solution)/shard_map/ppermute | solution.py:64
  1.2 0.4 %collective-permute-start.2 = (bf16[128,512]{1,0:T(8,128)(2,1)}, bf16[128,512]{1,0:T(8,128)(2,1)S(1)}, u32[]{:S(2)}, u32[]{:S(2)}) collective-permute-start(bf16[128,512]{1,0:T(8,128)(2,1)} %refs_2_.1), channel_id=1, source_target_pairs={{0,1},{1,0},{2,3},{3,2},{4,5},{5,4},{6,7},{7,6},{8,9},{9,8},{10,11... | collective-permute-start | bytes 393224 | tf_op jit(solution)/shard_map/ppermute | solution.py:64
  1.8 0.4 %collective-permute-start.4 = (s32[128]{0:T(128)S(1)}, s32[128]{0:T(128)S(1)}, u32[]{:S(2)}, u32[]{:S(2)}) collective-permute-start(s32[128]{0:T(128)S(1)} %copy-done.1), channel_id=1, source_target_pairs={{0,1},{1,0},{2,3},{3,2},{4,5},{5,4},{6,7},{7,6},{8,9},{9,8},{10,11... | collective-permute-start | bytes 1544 | tf_op jit(solution)/shard_map/ppermute | solution.py:64
  2.2 1.3 %pack.1.refs_0_ = bf16[1056,128]{1,0:T(8,128)(2,1)S(1)} custom-call(bf16[128,512]{1,0:T(8,128)(2,1)} %refs_0_.1, bf16[128,512]{1,0:T(8,128)(2,1)} %refs_1_.2, bf16[128,512]{1,0:T(8,128)(2,1)} %refs_2_.1, f32[4,128]{1,0:T(4,128)} %bitcast.5, s32[1,128]{1,0:T(1,128)} %bitcast.6), custom_call_target="tpu_custom_call" | custom-call | tf_op jit(solution)/shard_map/pack/pallas_call | solution.py:120
  3.7 2.6 %collective-permute-start.5 = (bf16[2112,128]{1,0:T(8,128)(2,1)S(1)}, bf16[2112,128]{1,0:T(8,128)(2,1)S(1)}, u32[]{:S(2)}, u32[]{:S(2)}) collective-permute-start(bf16[2112,128]{1,0:T(8,128)(2,1)S(1)} %pack_chip.1), channel_id=1, source_target_pairs={{8,0},{17,1},{0,8},{25,9},{24,16},{1,17},{16,24},{9,25},{10,2},{19... | collective-permute-start | bytes 1622024 | tf_op jit(solution)/shard_map/ppermute | solution.py:45
  6.3 3.6 %collective-permute-start.6 = (bf16[128,256]{1,0:T(8,128)(2,1)S(1)}, bf16[128,256]{1,0:T(8,128)(2,1)S(1)}, u32[]{:S(2)}, u32[]{:S(2)}) collective-permute-start(bf16[128,256]{1,0:T(8,128)(2,1)S(1)} %copy-done), channel_id=1, source_target_pairs={{6,0},{4,2},{2,4},{0,6},{7,1},{5,3},{3,5},{1,7},{14,8},{12,10},{10... | collective-permute-start | bytes 196616 | tf_op jit(solution)/shard_map/ppermute | solution.py:55
  10.0 0.8 %collective-permute-start.9 = (bf16[128,256]{1,0:T(8,128)(2,1)S(1)}, bf16[128,256]{1,0:T(8,128)(2,1)S(1)}, u32[]{:S(2)}, u32[]{:S(2)}) collective-permute-start(bf16[128,256]{1,0:T(8,128)(2,1)S(1)} %copy-done), channel_id=1, source_target_pairs={{2,0},{0,2},{6,4},{4,6},{3,1},{1,3},{7,5},{5,7},{10,8},{8,10},{14,... | collective-permute-start | bytes 196616 | tf_op jit(solution)/shard_map/ppermute | solution.py:55
  10.7 1.5 %collective-permute-start.12 = (bf16[1056,128]{1,0:T(8,128)(2,1)S(1)}, bf16[1056,128]{1,0:T(8,128)(2,1)S(1)}, u32[]{:S(2)}, u32[]{:S(2)}) collective-permute-start(bf16[1056,128]{1,0:T(8,128)(2,1)S(1)} %pack.1.refs_0_), channel_id=1, source_target_pairs={{24,0},{25,1},{16,8},{17,9},{8,16},{9,17},{0,24},{1,25},{26,2},{27... | collective-permute-start | bytes 811016 | tf_op jit(solution)/shard_map/ppermute | solution.py:45
  12.6 3.2 %collective-permute-done.7.refs_1_ = bf16[128,256]{1,0:T(8,128)(2,1)S(1)} collective-permute-done((bf16[128,256]{1,0:T(8,128)(2,1)S(1)}, bf16[128,256]{1,0:T(8,128)(2,1)S(1)}, u32[]{:S(2)}, u32[]{:S(2)}) %collective-permute-start.7) | collective-permute-done | bytes 65568 | tf_op jit(solution)/shard_map/ppermute | solution.py:55
  16.0 0.5 %collective-permute-start.10 = (bf16[256,256]{1,0:T(8,128)(2,1)S(1)}, bf16[256,256]{1,0:T(8,128)(2,1)S(1)}, u32[]{:S(2)}, u32[]{:S(2)}) collective-permute-start(bf16[256,256]{1,0:T(8,128)(2,1)S(1)} %stack.3.refs_3_), channel_id=1, source_target_pairs={{0,1},{1,0},{2,3},{3,2},{4,5},{5,4},{6,7},{7,6},{8,9},{9,8},{10,11... | collective-permute-start | bytes 393224 | tf_op jit(solution)/shard_map/ppermute | solution.py:64
  16.5 1.7 %visit.4 = (f32[128,512]{1,0:T(8,128)S(1)}, f32[128,512]{1,0:T(8,128)S(1)}, f32[128,512]{1,0:T(8,128)S(1)}, f32[512,256]{1,0:T(8,128)S(1)}, bf16[512,128]{1,0:T(...) custom-call(bf16[1056,128]{1,0:T(8,128)(2,1)S(1)} %pack.1.refs_0_, ...), custom_call_target="tpu_custom_call" | custom-call | flops 450000000 | bytes 1000 | tf_op jit(solution)/shard_map/visit/pallas_call | solution.py:353
  18.3 1.9 %visit.5 = (f32[128,512]{1,0:T(8,128)S(1)}, bf16[256,512]{1,0:T(8,128)(2,1)S(1)}, f32[512,256]{1,0:T(8,128)S(1)}, bf16[512,128]{1,0:T(8,128)(2,1)S(1)}, bf16[512...) custom-call(bf16[1056,128]{1,0:T(8,128)(2,1)S(1)} %pack.1.refs_0_, ...), custom_call_target="tpu_custom_call" | custom-call | flops 450000000 | bytes 1000 | tf_op jit(solution)/shard_map/visit/pallas_call | solution.py:353
  20.2 1.2 %collective-permute-start.11 = (bf16[256,512]{1,0:T(8,128)(2,1)S(1)}, bf16[256,512]{1,0:T(8,128)(2,1)S(1)}, u32[]{:S(2)}, u32[]{:S(2)}) collective-permute-start(bf16[256,512]{1,0:T(8,128)(2,1)S(1)} %get-tuple-element.32), channel_id=1, source_target_pairs={{0,8},{1,17},{8,0},{9,25},{16,24},{17,1},{24,16},{25,9},{2,10},{3,... | collective-permute-start | bytes 786440 | tf_op jit(solution)/shard_map/ppermute | solution.py:50
  21.5 0.7 %visit.6 = (f32[128,512]{1,0:T(8,128)S(1)}, bf16[256,256]{1,0:T(8,128)(2,1)S(1)}, bf16[256,256]{1,0:T(8,128)(2,1)S(1)}) custom-call(bf16[1056,128]{1,0:T(8,128)(2,1)S(1)} %collective-permute-done.12.refs_0_, bf16[512,128]{1,0:T(8,128)(2,1)S(1)} %get-tuple-element.37.refs_1_, bf16[512,128]{1,0:T(8,128)(2,1)S(1)} %get-tuple-element.38.refs_2_, ...), custom_call_target="tpu_custom_call" | custom-call | flops 150000000 | bytes 1000 | tf_op jit(solution)/shard_map/visit/pallas_call | solution.py:353
  22.3 0.5 %collective-permute-start.14 = (bf16[256,256]{1,0:T(8,128)(2,1)S(1)}, bf16[256,256]{1,0:T(8,128)(2,1)S(1)}, u32[]{:S(2)}, u32[]{:S(2)}) collective-permute-start(bf16[256,256]{1,0:T(8,128)(2,1)S(1)} %get-tuple-element.44), channel_id=1, source_target_pairs={{0,1},{1,0},{2,3},{3,2},{4,5},{5,4},{6,7},{7,6},{8,9},{9,8},{10,11... | collective-permute-start | bytes 393224 | tf_op jit(solution)/shard_map/ppermute | solution.py:64
  22.8 0.8 %visit.7 = (bf16[128,512]{1,0:T(8,128)(2,1)S(1)}, f32[512,256]{1,0:T(8,128)S(1)}) custom-call(bf16[1056,128]{1,0:T(8,128)(2,1)S(1)} %collective-permute-done.12.refs_0_, bf16[512,128]{1,0:T(8,128)(2,1)S(1)} %get-tuple-element.33.refs_1_, bf16[512,128]{1,0:T(8,128)(2,1)S(1)} %get-tuple-element.34.refs_2_, bf16[128,512]{1,0:T(8,128)(2,1)S(1)} %get-tuple-element.35.refs_3_, ...), custom_call_target="tpu_custom_call" | custom-call | flops 150000000 | bytes 1000 | tf_op jit(solution)/shard_map/visit/pallas_call | solution.py:353
  23.8 2.2 %collective-permute-start.15 = (bf16[128,256]{1,0:T(8,128)(2,1)S(1)}, bf16[128,256]{1,0:T(8,128)(2,1)S(1)}, u32[]{:S(2)}, u32[]{:S(2)}) collective-permute-start(bf16[128,256]{1,0:T(8,128)(2,1)S(1)} %get-tuple-element.45), channel_id=1, source_target_pairs={{0,4},{2,6},{4,0},{6,2},{1,5},{3,7},{5,1},{7,3},{8,12},{10,14},{12... | collective-permute-start | bytes 196616 | tf_op jit(solution)/shard_map/ppermute | solution.py:60
  26.0 1.7 %collective-permute-start.18 = (bf16[128,512]{1,0:T(8,128)(2,1)S(1)}, bf16[128,512]{1,0:T(8,128)(2,1)S(1)}, u32[]{:S(2)}, u32[]{:S(2)}) collective-permute-start(bf16[128,512]{1,0:T(8,128)(2,1)S(1)} %get-tuple-element.49), channel_id=1, source_target_pairs={{0,24},{1,25},{8,16},{9,17},{16,8},{17,9},{24,0},{25,1},{2,26},{3,... | collective-permute-start | bytes 393224 | tf_op jit(solution)/shard_map/ppermute | solution.py:50
  27.7 1.2 %collective-permute-start.19 = (bf16[128,256]{1,0:T(8,128)(2,1)S(1)}, bf16[128,256]{1,0:T(8,128)(2,1)S(1)}, u32[]{:S(2)}, u32[]{:S(2)}) collective-permute-start(bf16[128,256]{1,0:T(8,128)(2,1)S(1)} %get-tuple-element.51), channel_id=1, source_target_pairs={{0,6},{2,4},{4,2},{6,0},{1,7},{3,5},{5,3},{7,1},{8,14},{10,12},{12... | collective-permute-start | bytes 196616 | tf_op jit(solution)/shard_map/ppermute | solution.py:60
  29.1 1.4 %collective-permute-done.15.refs_7_ = bf16[128,256]{1,0:T(8,128)(2,1)S(1)} collective-permute-done((bf16[128,256]{1,0:T(8,128)(2,1)S(1)}, bf16[128,256]{1,0:T(8,128)(2,1)S(1)}, u32[]{:S(2)}, u32[]{:S(2)}) %collective-permute-start.15) | collective-permute-done | bytes 65568 | tf_op jit(solution)/shard_map/ppermute | solution.py:60
  30.6 0.5 %collective-permute-start.17 = (bf16[64,512]{1,0:T(8,128)(2,1)S(1)}, bf16[64,512]{1,0:T(8,128)(2,1)S(1)}, u32[]{:S(2)}, u32[]{:S(2)}) collective-permute-start(bf16[64,512]{1,0:T(8,128)(2,1)S(1)} %get-tuple-element.48), channel_id=1, source_target_pairs={{0,1},{1,0},{2,3},{3,2},{4,5},{5,4},{6,7},{7,6},{8,9},{9,8},{10,11... | collective-permute-start | bytes 196616 | tf_op jit(solution)/shard_map/ppermute | solution.py:64
  31.1 1.2 %collective-permute-done.18.refs_4_ = bf16[128,512]{1,0:T(8,128)(2,1)S(1)} collective-permute-done((bf16[128,512]{1,0:T(8,128)(2,1)S(1)}, bf16[128,512]{1,0:T(8,128)(2,1)S(1)}, u32[]{:S(2)}, u32[]{:S(2)}) %collective-permute-start.18) | collective-permute-done | bytes 131104 | tf_op jit(solution)/shard_map/ppermute | solution.py:50
  32.3 1.7 %collective-permute-done.19.refs_6_ = bf16[128,256]{1,0:T(8,128)(2,1)S(1)} collective-permute-done((bf16[128,256]{1,0:T(8,128)(2,1)S(1)}, bf16[128,256]{1,0:T(8,128)(2,1)S(1)}, u32[]{:S(2)}, u32[]{:S(2)}) %collective-permute-start.19) | collective-permute-done | bytes 65568 | tf_op jit(solution)/shard_map/ppermute | solution.py:60
  34.0 0.7 %totals.1 = (bf16[128,512]{1,0:T(8,128)(2,1)}, bf16[128,256]{1,0:T(8,128)(2,1)}) custom-call(f32[128,512]{1,0:T(8,128)S(1)} %get-tuple-element.31.refs_0_, bf16[256,512]{1,0:T(8,128)(2,1)S(1)} %collective-permute-done.11.ref.refs_1_, bf16[64,512]{1,0:T(8,128)(2,1)S(1)} %collective-permute-done.16.refs_2_, ...), custom_call_target="tpu_custom_call" | custom-call | tf_op jit(solution)/shard_map/totals/pallas_call | solution.py:437
  (33 shorter events, 1.4 us)
Async XLA Ops:
  0.6 1.1 %copy-start.1 = (s32[128]{0:T(128)S(1)}, s32[128]{0:T(128)}, u32[]{:S(2)}) copy-start(s32[128]{0:T(128)} %param.11) | copy-start | bytes 1540
  0.6 2.8 %collective-permute-start = (bf16[128,512]{1,0:T(8,128)(2,1)}, bf16[128,512]{1,0:T(8,128)(2,1)S(1)}, u32[]{:S(2)}, u32[]{:S(2)}) collective-permute-start(bf16[128,512]{1,0:T(8,128)(2,1)} %refs_0_.1), channel_id=1, source_target_pairs={{0,1},{1,0},{2,3},{3,2},{4,5},{5,4},{6,7},{7,6},{8,9},{9,8},{10,11... | collective-permute-start | bytes 393224 | tf_op jit(solution)/shard_map/ppermute | solution.py:64
  1.2 2.3 %collective-permute-start.1 = (bf16[128,512]{1,0:T(8,128)(2,1)}, bf16[128,512]{1,0:T(8,128)(2,1)S(1)}, u32[]{:S(2)}, u32[]{:S(2)}) collective-permute-start(bf16[128,512]{1,0:T(8,128)(2,1)} %refs_1_.2), channel_id=1, source_target_pairs={{0,1},{1,0},{2,3},{3,2},{4,5},{5,4},{6,7},{7,6},{8,9},{9,8},{10,11... | collective-permute-start | bytes 393224 | tf_op jit(solution)/shard_map/ppermute | solution.py:64
  1.2 2.3 %collective-permute-start.2 = (bf16[128,512]{1,0:T(8,128)(2,1)}, bf16[128,512]{1,0:T(8,128)(2,1)S(1)}, u32[]{:S(2)}, u32[]{:S(2)}) collective-permute-start(bf16[128,512]{1,0:T(8,128)(2,1)} %refs_2_.1), channel_id=1, source_target_pairs={{0,1},{1,0},{2,3},{3,2},{4,5},{5,4},{6,7},{7,6},{8,9},{9,8},{10,11... | collective-permute-start | bytes 393224 | tf_op jit(solution)/shard_map/ppermute | solution.py:64
  1.7 1.8 %collective-permute-start.3 = (f32[4,128]{1,0:T(4,128)}, f32[4,128]{1,0:T(4,128)S(1)}, u32[]{:S(2)}, u32[]{:S(2)}) collective-permute-start(f32[4,128]{1,0:T(4,128)} %bitcast.4), channel_id=1, source_target_pairs={{0,1},{1,0},{2,3},{3,2},{4,5},{5,4},{6,7},{7,6},{8,9},{9,8},{10,11... | collective-permute-start | bytes 6152 | tf_op jit(solution)/shard_map/ppermute | solution.py:64
  1.8 1.7 %collective-permute-start.4 = (s32[128]{0:T(128)S(1)}, s32[128]{0:T(128)S(1)}, u32[]{:S(2)}, u32[]{:S(2)}) collective-permute-start(s32[128]{0:T(128)S(1)} %copy-done.1), channel_id=1, source_target_pairs={{0,1},{1,0},{2,3},{3,2},{4,5},{5,4},{6,7},{7,6},{8,9},{9,8},{10,11... | collective-permute-start | bytes 1544 | tf_op jit(solution)/shard_map/ppermute | solution.py:64
  3.5 2.8 %copy-start = (bf16[128,256]{1,0:T(8,128)(2,1)S(1)}, bf16[128,256]{1,0:T(8,128)(2,1)}, u32[]{:S(2)}) copy-start(bf16[128,256]{1,0:T(8,128)(2,1)} %refs_1_.3) | copy-start | bytes 196612
  3.7 12.8 %collective-permute-start.5 = (bf16[2112,128]{1,0:T(8,128)(2,1)S(1)}, bf16[2112,128]{1,0:T(8,128)(2,1)S(1)}, u32[]{:S(2)}, u32[]{:S(2)}) collective-permute-start(bf16[2112,128]{1,0:T(8,128)(2,1)S(1)} %pack_chip.1), channel_id=1, source_target_pairs={{8,0},{17,1},{0,8},{25,9},{24,16},{1,17},{16,24},{9,25},{10,2},{19... | collective-permute-start | bytes 1622024 | tf_op jit(solution)/shard_map/ppermute | solution.py:45
  6.3 6.3 %collective-permute-start.6 = (bf16[128,256]{1,0:T(8,128)(2,1)S(1)}, bf16[128,256]{1,0:T(8,128)(2,1)S(1)}, u32[]{:S(2)}, u32[]{:S(2)}) collective-permute-start(bf16[128,256]{1,0:T(8,128)(2,1)S(1)} %copy-done), channel_id=1, source_target_pairs={{6,0},{4,2},{2,4},{0,6},{7,1},{5,3},{3,5},{1,7},{14,8},{12,10},{10... | collective-permute-start | bytes 196616 | tf_op jit(solution)/shard_map/ppermute | solution.py:55
  9.9 5.9 %collective-permute-start.7 = (bf16[128,256]{1,0:T(8,128)(2,1)S(1)}, bf16[128,256]{1,0:T(8,128)(2,1)S(1)}, u32[]{:S(2)}, u32[]{:S(2)}) collective-permute-start(bf16[128,256]{1,0:T(8,128)(2,1)S(1)} %copy-done), channel_id=1, source_target_pairs={{4,0},{6,2},{0,4},{2,6},{5,1},{7,3},{1,5},{3,7},{12,8},{14,10},{8,... | collective-permute-start | bytes 196616 | tf_op jit(solution)/shard_map/ppermute | solution.py:55
  10.0 6.0 %collective-permute-start.9 = (bf16[128,256]{1,0:T(8,128)(2,1)S(1)}, bf16[128,256]{1,0:T(8,128)(2,1)S(1)}, u32[]{:S(2)}, u32[]{:S(2)}) collective-permute-start(bf16[128,256]{1,0:T(8,128)(2,1)S(1)} %copy-done), channel_id=1, source_target_pairs={{2,0},{0,2},{6,4},{4,6},{3,1},{1,3},{7,5},{5,7},{10,8},{8,10},{14,... | collective-permute-start | bytes 196616 | tf_op jit(solution)/shard_map/ppermute | solution.py:55
  10.7 10.7 %collective-permute-start.12 = (bf16[1056,128]{1,0:T(8,128)(2,1)S(1)}, bf16[1056,128]{1,0:T(8,128)(2,1)S(1)}, u32[]{:S(2)}, u32[]{:S(2)}) collective-permute-start(bf16[1056,128]{1,0:T(8,128)(2,1)S(1)} %pack.1.refs_0_), channel_id=1, source_target_pairs={{24,0},{25,1},{16,8},{17,9},{8,16},{9,17},{0,24},{1,25},{26,2},{27... | collective-permute-start | bytes 811016 | tf_op jit(solution)/shard_map/ppermute | solution.py:45
  15.9 2.4 %collective-permute-start.8 = (bf16[256,256]{1,0:T(8,128)(2,1)S(1)}, bf16[256,256]{1,0:T(8,128)(2,1)S(1)}, u32[]{:S(2)}, u32[]{:S(2)}) collective-permute-start(bf16[256,256]{1,0:T(8,128)(2,1)S(1)} %stack.2.refs_2_), channel_id=1, source_target_pairs={{0,1},{1,0},{2,3},{3,2},{4,5},{5,4},{6,7},{7,6},{8,9},{9,8},{10,11... | collective-permute-start | bytes 393224 | tf_op jit(solution)/shard_map/ppermute | solution.py:64
  16.0 2.3 %collective-permute-start.10 = (bf16[256,256]{1,0:T(8,128)(2,1)S(1)}, bf16[256,256]{1,0:T(8,128)(2,1)S(1)}, u32[]{:S(2)}, u32[]{:S(2)}) collective-permute-start(bf16[256,256]{1,0:T(8,128)(2,1)S(1)} %stack.3.refs_3_), channel_id=1, source_target_pairs={{0,1},{1,0},{2,3},{3,2},{4,5},{5,4},{6,7},{7,6},{8,9},{9,8},{10,11... | collective-permute-start | bytes 393224 | tf_op jit(solution)/shard_map/ppermute | solution.py:64
  20.2 10.3 %collective-permute-start.11 = (bf16[256,512]{1,0:T(8,128)(2,1)S(1)}, bf16[256,512]{1,0:T(8,128)(2,1)S(1)}, u32[]{:S(2)}, u32[]{:S(2)}) collective-permute-start(bf16[256,512]{1,0:T(8,128)(2,1)S(1)} %get-tuple-element.32), channel_id=1, source_target_pairs={{0,8},{1,17},{8,0},{9,25},{16,24},{17,1},{24,16},{25,9},{2,10},{3,... | collective-permute-start | bytes 786440 | tf_op jit(solution)/shard_map/ppermute | solution.py:50
  22.2 1.4 %collective-permute-start.13 = (bf16[256,256]{1,0:T(8,128)(2,1)S(1)}, bf16[256,256]{1,0:T(8,128)(2,1)S(1)}, u32[]{:S(2)}, u32[]{:S(2)}) collective-permute-start(bf16[256,256]{1,0:T(8,128)(2,1)S(1)} %get-tuple-element.43), channel_id=1, source_target_pairs={{0,1},{1,0},{2,3},{3,2},{4,5},{5,4},{6,7},{7,6},{8,9},{9,8},{10,11... | collective-permute-start | bytes 393224 | tf_op jit(solution)/shard_map/ppermute | solution.py:64
  22.3 1.5 %collective-permute-start.14 = (bf16[256,256]{1,0:T(8,128)(2,1)S(1)}, bf16[256,256]{1,0:T(8,128)(2,1)S(1)}, u32[]{:S(2)}, u32[]{:S(2)}) collective-permute-start(bf16[256,256]{1,0:T(8,128)(2,1)S(1)} %get-tuple-element.44), channel_id=1, source_target_pairs={{0,1},{1,0},{2,3},{3,2},{4,5},{5,4},{6,7},{7,6},{8,9},{9,8},{10,11... | collective-permute-start | bytes 393224 | tf_op jit(solution)/shard_map/ppermute | solution.py:64
  23.8 6.7 %collective-permute-start.15 = (bf16[128,256]{1,0:T(8,128)(2,1)S(1)}, bf16[128,256]{1,0:T(8,128)(2,1)S(1)}, u32[]{:S(2)}, u32[]{:S(2)}) collective-permute-start(bf16[128,256]{1,0:T(8,128)(2,1)S(1)} %get-tuple-element.45), channel_id=1, source_target_pairs={{0,4},{2,6},{4,0},{6,2},{1,5},{3,7},{5,1},{7,3},{8,12},{10,14},{12... | collective-permute-start | bytes 196616 | tf_op jit(solution)/shard_map/ppermute | solution.py:60
  26.0 6.3 %collective-permute-start.18 = (bf16[128,512]{1,0:T(8,128)(2,1)S(1)}, bf16[128,512]{1,0:T(8,128)(2,1)S(1)}, u32[]{:S(2)}, u32[]{:S(2)}) collective-permute-start(bf16[128,512]{1,0:T(8,128)(2,1)S(1)} %get-tuple-element.49), channel_id=1, source_target_pairs={{0,24},{1,25},{8,16},{9,17},{16,8},{17,9},{24,0},{25,1},{2,26},{3,... | collective-permute-start | bytes 393224 | tf_op jit(solution)/shard_map/ppermute | solution.py:50
  27.7 6.3 %collective-permute-start.19 = (bf16[128,256]{1,0:T(8,128)(2,1)S(1)}, bf16[128,256]{1,0:T(8,128)(2,1)S(1)}, u32[]{:S(2)}, u32[]{:S(2)}) collective-permute-start(bf16[128,256]{1,0:T(8,128)(2,1)S(1)} %get-tuple-element.51), channel_id=1, source_target_pairs={{0,6},{2,4},{4,2},{6,0},{1,7},{3,5},{5,3},{7,1},{8,14},{10,12},{12... | collective-permute-start | bytes 196616 | tf_op jit(solution)/shard_map/ppermute | solution.py:60
  29.0 5.1 %collective-permute-start.20 = (bf16[128,256]{1,0:T(8,128)(2,1)S(1)}, bf16[128,256]{1,0:T(8,128)(2,1)S(1)}, u32[]{:S(2)}, u32[]{:S(2)}) collective-permute-start(bf16[128,256]{1,0:T(8,128)(2,1)S(1)} %get-tuple-element.53), channel_id=1, source_target_pairs={{0,2},{2,0},{4,6},{6,4},{1,3},{3,1},{5,7},{7,5},{8,10},{10,8},{12,... | collective-permute-start | bytes 196616 | tf_op jit(solution)/shard_map/ppermute | solution.py:60
  30.6 3.5 %collective-permute-start.16 = (bf16[64,512]{1,0:T(8,128)(2,1)S(1)}, bf16[64,512]{1,0:T(8,128)(2,1)S(1)}, u32[]{:S(2)}, u32[]{:S(2)}) collective-permute-start(bf16[64,512]{1,0:T(8,128)(2,1)S(1)} %get-tuple-element.47), channel_id=1, source_target_pairs={{0,1},{1,0},{2,3},{3,2},{4,5},{5,4},{6,7},{7,6},{8,9},{9,8},{10,11... | collective-permute-start | bytes 196616 | tf_op jit(solution)/shard_map/ppermute | solution.py:64
  30.6 3.4 %collective-permute-start.17 = (bf16[64,512]{1,0:T(8,128)(2,1)S(1)}, bf16[64,512]{1,0:T(8,128)(2,1)S(1)}, u32[]{:S(2)}, u32[]{:S(2)}) collective-permute-start(bf16[64,512]{1,0:T(8,128)(2,1)S(1)} %get-tuple-element.48), channel_id=1, source_target_pairs={{0,1},{1,0},{2,3},{3,2},{4,5},{5,4},{6,7},{7,6},{8,9},{9,8},{10,11... | collective-permute-start | bytes 196616 | tf_op jit(solution)/shard_map/ppermute | solution.py:64

commit v8 on v7

--- a/solution.py
+++ b/solution.py
@@ -11,7 +11,7 @@
 
 LOG2E = math.log2(math.e)
 STATS = 8
-SENDS = 2
+SENDS = 1
 KEY_SENDS = 2
 PIECES = 2
 PART_COST = 150000000
@@ -317,10 +317,15 @@
         dq_ref = dq_refs[group]
         for late in range(2):
             part = slice(late * lanes, (late + 1) * lanes)
-            turned = ((dqt_ref[:, part] + partials[at][:, part]) * scale).T.astype(dq_ref.dtype)
-            to = slice(second * tok + late * half, second * tok + (late + 1) * half)
-            for h in range(heads):
-                dq_ref[to, h * width : (h + 1) * width] = turned[h * half : (h + 1) * half]
+            exact = ((dqt_ref[:, part] + partials[at][:, part]) * scale).T
+            turned = exact.astype(dq_ref.dtype)
+            blocks = [(2 * second, turned)]
+            if len(steps) == 2 and not second:
+                blocks.append((1, (exact - turned.astype(F32)).astype(dq_ref.dtype)))
+            for block, value in blocks:
+                to = slice(block * tok + late * half, block * tok + (late + 1) * half)
+                for h in range(heads):
+                    dq_ref[to, h * width : (h + 1) * width] = value[h * half : (h + 1) * half]
 
     if finish:
         each = sum_refs[0].shape[0]
@@ -337,7 +342,7 @@
     keys = zed * tok
     if resume:
         outs = [
-            jax.ShapeDtypeStruct((max(1, len(steps)) * tok, heads * width), BF16 if steps else F32) for steps in groups
+            jax.ShapeDtypeStruct(((1, 1, 3)[len(steps)] * tok, heads * width), BF16 if steps else F32) for steps in groups
         ]
     else:
         outs = [jax.ShapeDtypeStruct((width, heads * tok), F32)] * jobs
@@ -399,7 +404,7 @@
 
 def split(value, pieces):
     rows, columns = value.shape
-    one = jax.ShapeDtypeStruct((rows // 2 // pieces, columns), value.dtype)
+    one = jax.ShapeDtypeStruct((rows // 3 // pieces, columns), value.dtype)
     return pl.pallas_call(
         split_kernel,
         out_shape=[one] * pieces,
@@ -413,12 +418,15 @@
 def add_up(out, refs):
     rows = out.shape[0]
     whole = [ref for ref in refs if ref.shape[0] >= rows]
+    low_parts = [ref for ref in refs if ref.shape[0] == 3 * rows]
     pieces = [ref for ref in refs if ref.shape[0] < rows]
     step = pieces[0].shape[0] if pieces else rows
     for at in range(0, rows, step):
         value = whole[0][at : at + step, :].astype(F32)
         for ref in whole[1:]:
             value = value + ref[at : at + step, :].astype(F32)
+        for ref in low_parts:
+            value = value + ref[rows + at : rows + at + step, :].astype(F32)
         for n, ref in enumerate(pieces):
             if n * step % rows == at:
                 value = value + ref[...].astype(F32)

time: 34.9 us -> 34.9 us (level)
  starting transfers between devices: 18.3 us -> 17.8 us
  waiting for transfers between devices: 8.06 us -> 8.48 us
    ppermute x11 -> x10, waiting for transfers between devices: 0.19 us -> 0.69 us  [swap_cores(): return lax.ppermute(value, 'core', [(0, 1), (1, 0)])]
    ppermute x11 -> x10, starting transfers between devices: 3.29 us -> 2.8 us  [swap_cores(): return lax.ppermute(value, 'core', [(0, 1), (1, 0)])]
  transfers between devices with their start and end apart: 21 -> 20, of which waited for: 6 -> 6; matrix products, arithmetic and copies ran while one was open for 0% -> 0% of each run, Pallas kernels for 19% -> 19%
where the time goes in v8:
time: 34.9 us; the launch traced here: 34.7 us
  starting transfers between devices  17.8 us (51%)
  waiting for transfers between devices  8.48 us (24%)
  Pallas kernels  7.6 us (22%)
  between operations  0.8 us (2%)
    pallas_call x4, Pallas kernels, visit(): pl.pallas_call(functools.partial(visit_kernel, groups, side, fresh, resum...  5.29 us
    ppermute x3, starting transfers between devices, fetch_z(): lax.ppermute(value, 'z', [(peer(z, step, count), z) for z in range(count)])  4.39 us
    ppermute x2, starting transfers between devices, fetch(): lax.ppermute(value, ('inner', 'core'), inner_pairs(steps, lax.axis_size('...  4.16 us
    ppermute x3, waiting for transfers between devices, fetch_z(): lax.ppermute(value, 'z', [(peer(z, step, count), z) for z in range(count)])  3.57 us
    ppermute x3, starting transfers between devices, give_back_z(): lax.ppermute(value, 'z', [(z, peer(z, step, count)) for z in range(count)])  3.54 us
    ppermute x3, waiting for transfers between devices, give_back_z(): lax.ppermute(value, 'z', [(z, peer(z, step, count)) for z in range(count)])  3.02 us
    ppermute x2, starting transfers between devices, give_back(): return lax.ppermute(value, ('inner', 'core'), [(b, a) for a, b in pairs])  2.93 us
    ppermute x10, starting transfers between devices, swap_cores(): return lax.ppermute(value, 'core', [(0, 1), (1, 0)])  2.8 us
  transfers between devices with their start and end apart: 20, of which 6 were waited for; matrix products, arithmetic and copies ran while one was open for 0% of the time, Pallas kernels for 19%

profile of v8, /device:TPU:0, one launch (start us, length us, event | category | flops | bytes accessed | tf_op | source)
XLA Modules:
  0.0 34.7 jit_solution(2657590053053380570)
XLA Ops:
  0.6 0.5 %collective-permute-start = (bf16[128,512]{1,0:T(8,128)(2,1)}, bf16[128,512]{1,0:T(8,128)(2,1)S(1)}, u32[]{:S(2)}, u32[]{:S(2)}) collective-permute-start(bf16[128,512]{1,0:T(8,128)(2,1)} %refs_0_.1), channel_id=1, source_target_pairs={{0,1},{1,0},{2,3},{3,2},{4,5},{5,4},{6,7},{7,6},{8,9},{9,8},{10,11... | collective-permute-start | bytes 393224 | tf_op jit(solution)/shard_map/ppermute | solution.py:64
  1.2 0.4 %collective-permute-start.2 = (bf16[128,512]{1,0:T(8,128)(2,1)}, bf16[128,512]{1,0:T(8,128)(2,1)S(1)}, u32[]{:S(2)}, u32[]{:S(2)}) collective-permute-start(bf16[128,512]{1,0:T(8,128)(2,1)} %refs_2_.1), channel_id=1, source_target_pairs={{0,1},{1,0},{2,3},{3,2},{4,5},{5,4},{6,7},{7,6},{8,9},{9,8},{10,11... | collective-permute-start | bytes 393224 | tf_op jit(solution)/shard_map/ppermute | solution.py:64
  1.8 0.4 %collective-permute-start.4 = (s32[128]{0:T(128)S(1)}, s32[128]{0:T(128)S(1)}, u32[]{:S(2)}, u32[]{:S(2)}) collective-permute-start(s32[128]{0:T(128)S(1)} %copy-done.1), channel_id=1, source_target_pairs={{0,1},{1,0},{2,3},{3,2},{4,5},{5,4},{6,7},{7,6},{8,9},{9,8},{10,11... | collective-permute-start | bytes 1544 | tf_op jit(solution)/shard_map/ppermute | solution.py:64
  2.2 1.3 %pack.1.refs_0_ = bf16[1056,128]{1,0:T(8,128)(2,1)S(1)} custom-call(bf16[128,512]{1,0:T(8,128)(2,1)} %refs_0_.1, bf16[128,512]{1,0:T(8,128)(2,1)} %refs_1_.2, bf16[128,512]{1,0:T(8,128)(2,1)} %refs_2_.1, f32[4,128]{1,0:T(4,128)} %bitcast.5, s32[1,128]{1,0:T(1,128)} %bitcast.6), custom_call_target="tpu_custom_call" | custom-call | tf_op jit(solution)/shard_map/pack/pallas_call | solution.py:120
  3.7 2.6 %collective-permute-start.5 = (bf16[2112,128]{1,0:T(8,128)(2,1)S(1)}, bf16[2112,128]{1,0:T(8,128)(2,1)S(1)}, u32[]{:S(2)}, u32[]{:S(2)}) collective-permute-start(bf16[2112,128]{1,0:T(8,128)(2,1)S(1)} %pack_chip.1), channel_id=1, source_target_pairs={{8,0},{17,1},{0,8},{25,9},{24,16},{1,17},{16,24},{9,25},{10,2},{19... | collective-permute-start | bytes 1622024 | tf_op jit(solution)/shard_map/ppermute | solution.py:45
  6.3 3.6 %collective-permute-start.6 = (bf16[128,256]{1,0:T(8,128)(2,1)S(1)}, bf16[128,256]{1,0:T(8,128)(2,1)S(1)}, u32[]{:S(2)}, u32[]{:S(2)}) collective-permute-start(bf16[128,256]{1,0:T(8,128)(2,1)S(1)} %copy-done), channel_id=1, source_target_pairs={{6,0},{4,2},{2,4},{0,6},{7,1},{5,3},{3,5},{1,7},{14,8},{12,10},{10... | collective-permute-start | bytes 196616 | tf_op jit(solution)/shard_map/ppermute | solution.py:55
  10.0 0.8 %collective-permute-start.9 = (bf16[128,256]{1,0:T(8,128)(2,1)S(1)}, bf16[128,256]{1,0:T(8,128)(2,1)S(1)}, u32[]{:S(2)}, u32[]{:S(2)}) collective-permute-start(bf16[128,256]{1,0:T(8,128)(2,1)S(1)} %copy-done), channel_id=1, source_target_pairs={{2,0},{0,2},{6,4},{4,6},{3,1},{1,3},{7,5},{5,7},{10,8},{8,10},{14,... | collective-permute-start | bytes 196616 | tf_op jit(solution)/shard_map/ppermute | solution.py:55
  10.7 1.5 %collective-permute-start.12 = (bf16[1056,128]{1,0:T(8,128)(2,1)S(1)}, bf16[1056,128]{1,0:T(8,128)(2,1)S(1)}, u32[]{:S(2)}, u32[]{:S(2)}) collective-permute-start(bf16[1056,128]{1,0:T(8,128)(2,1)S(1)} %pack.1.refs_0_), channel_id=1, source_target_pairs={{24,0},{25,1},{16,8},{17,9},{8,16},{9,17},{0,24},{1,25},{26,2},{27... | collective-permute-start | bytes 811016 | tf_op jit(solution)/shard_map/ppermute | solution.py:45
  12.6 3.2 %collective-permute-done.7.refs_1_ = bf16[128,256]{1,0:T(8,128)(2,1)S(1)} collective-permute-done((bf16[128,256]{1,0:T(8,128)(2,1)S(1)}, bf16[128,256]{1,0:T(8,128)(2,1)S(1)}, u32[]{:S(2)}, u32[]{:S(2)}) %collective-permute-start.7) | collective-permute-done | bytes 65568 | tf_op jit(solution)/shard_map/ppermute | solution.py:55
  16.0 0.5 %collective-permute-start.10 = (bf16[256,256]{1,0:T(8,128)(2,1)S(1)}, bf16[256,256]{1,0:T(8,128)(2,1)S(1)}, u32[]{:S(2)}, u32[]{:S(2)}) collective-permute-start(bf16[256,256]{1,0:T(8,128)(2,1)S(1)} %stack.3.refs_3_), channel_id=1, source_target_pairs={{0,1},{1,0},{2,3},{3,2},{4,5},{5,4},{6,7},{7,6},{8,9},{9,8},{10,11... | collective-permute-start | bytes 393224 | tf_op jit(solution)/shard_map/ppermute | solution.py:64
  16.5 1.7 %visit.4 = (f32[128,512]{1,0:T(8,128)S(1)}, f32[128,512]{1,0:T(8,128)S(1)}, f32[128,512]{1,0:T(8,128)S(1)}, f32[512,256]{1,0:T(8,128)S(1)}, bf16[512,128]{1,0:T(...) custom-call(bf16[1056,128]{1,0:T(8,128)(2,1)S(1)} %pack.1.refs_0_, ...), custom_call_target="tpu_custom_call" | custom-call | flops 450000000 | bytes 1000 | tf_op jit(solution)/shard_map/visit/pallas_call | solution.py:358
  18.3 2.0 %visit.5 = (f32[128,512]{1,0:T(8,128)S(1)}, bf16[384,512]{1,0:T(8,128)(2,1)S(1)}, f32[512,256]{1,0:T(8,128)S(1)}, bf16[512,128]{1,0:T(8,128)(2,1)S(1)}, bf16[512...) custom-call(bf16[1056,128]{1,0:T(8,128)(2,1)S(1)} %pack.1.refs_0_, ...), custom_call_target="tpu_custom_call" | custom-call | flops 450000000 | bytes 1000 | tf_op jit(solution)/shard_map/visit/pallas_call | solution.py:358
  20.2 1.2 %collective-permute-start.11 = (bf16[384,512]{1,0:T(8,128)(2,1)S(1)}, bf16[384,512]{1,0:T(8,128)(2,1)S(1)}, u32[]{:S(2)}, u32[]{:S(2)}) collective-permute-start(bf16[384,512]{1,0:T(8,128)(2,1)S(1)} %get-tuple-element.31), channel_id=1, source_target_pairs={{0,8},{1,17},{8,0},{9,25},{16,24},{17,1},{24,16},{25,9},{2,10},{3,... | collective-permute-start | bytes 1179656 | tf_op jit(solution)/shard_map/ppermute | solution.py:50
  21.5 0.7 %visit.6 = (f32[128,512]{1,0:T(8,128)S(1)}, bf16[512,256]{1,0:T(8,128)(2,1)S(1)}) custom-call(bf16[1056,128]{1,0:T(8,128)(2,1)S(1)} %collective-permute-done.12.refs_0_, bf16[512,128]{1,0:T(8,128)(2,1)S(1)} %get-tuple-element.36.refs_1_, bf16[512,128]{1,0:T(8,128)(2,1)S(1)} %get-tuple-element.37.refs_2_, bf16[128,512]{1,0:T(8,128)(2,1)S(1)} %get-tuple-element.38.refs_3_, ...), custom_call_target="tpu_custom_call" | custom-call | flops 150000000 | bytes 1000 | tf_op jit(solution)/shard_map/visit/pallas_call | solution.py:358
  22.3 0.8 %visit.7 = (bf16[128,512]{1,0:T(8,128)(2,1)S(1)}, f32[512,256]{1,0:T(8,128)S(1)}) custom-call(bf16[1056,128]{1,0:T(8,128)(2,1)S(1)} %collective-permute-done.12.refs_0_, bf16[512,128]{1,0:T(8,128)(2,1)S(1)} %get-tuple-element.32.refs_1_, bf16[512,128]{1,0:T(8,128)(2,1)S(1)} %get-tuple-element.33.refs_2_, bf16[128,512]{1,0:T(8,128)(2,1)S(1)} %get-tuple-element.34.refs_3_, ...), custom_call_target="tpu_custom_call" | custom-call | flops 150000000 | bytes 1000 | tf_op jit(solution)/shard_map/visit/pallas_call | solution.py:358
  23.1 0.7 %collective-permute-done.13.refs_0_ = bf16[512,256]{1,0:T(8,128)(2,1)S(1)} collective-permute-done((bf16[512,256]{1,0:T(8,128)(2,1)S(1)}, bf16[512,256]{1,0:T(8,128)(2,1)S(1)}, u32[]{:S(2)}, u32[]{:S(2)}) %collective-permute-start.13) | collective-permute-done | bytes 262176 | tf_op jit(solution)/shard_map/ppermute | solution.py:64
  23.9 2.1 %collective-permute-start.14 = (bf16[128,256]{1,0:T(8,128)(2,1)S(1)}, bf16[128,256]{1,0:T(8,128)(2,1)S(1)}, u32[]{:S(2)}, u32[]{:S(2)}) collective-permute-start(bf16[128,256]{1,0:T(8,128)(2,1)S(1)} %get-tuple-element.43), channel_id=1, source_target_pairs={{0,4},{2,6},{4,0},{6,2},{1,5},{3,7},{5,1},{7,3},{8,12},{10,14},{12... | collective-permute-start | bytes 196616 | tf_op jit(solution)/shard_map/ppermute | solution.py:60
  26.0 1.7 %collective-permute-start.17 = (bf16[128,512]{1,0:T(8,128)(2,1)S(1)}, bf16[128,512]{1,0:T(8,128)(2,1)S(1)}, u32[]{:S(2)}, u32[]{:S(2)}) collective-permute-start(bf16[128,512]{1,0:T(8,128)(2,1)S(1)} %get-tuple-element.47), channel_id=1, source_target_pairs={{0,24},{1,25},{8,16},{9,17},{16,8},{17,9},{24,0},{25,1},{2,26},{3,... | collective-permute-start | bytes 393224 | tf_op jit(solution)/shard_map/ppermute | solution.py:50
  27.7 1.2 %collective-permute-start.18 = (bf16[128,256]{1,0:T(8,128)(2,1)S(1)}, bf16[128,256]{1,0:T(8,128)(2,1)S(1)}, u32[]{:S(2)}, u32[]{:S(2)}) collective-permute-start(bf16[128,256]{1,0:T(8,128)(2,1)S(1)} %get-tuple-element.49), channel_id=1, source_target_pairs={{0,6},{2,4},{4,2},{6,0},{1,7},{3,5},{5,3},{7,1},{8,14},{10,12},{12... | collective-permute-start | bytes 196616 | tf_op jit(solution)/shard_map/ppermute | solution.py:60
  29.1 1.2 %collective-permute-done.14.refs_7_ = bf16[128,256]{1,0:T(8,128)(2,1)S(1)} collective-permute-done((bf16[128,256]{1,0:T(8,128)(2,1)S(1)}, bf16[128,256]{1,0:T(8,128)(2,1)S(1)}, u32[]{:S(2)}, u32[]{:S(2)}) %collective-permute-start.14) | collective-permute-done | bytes 65568 | tf_op jit(solution)/shard_map/ppermute | solution.py:60
  30.5 0.5 %collective-permute-start.16 = (bf16[64,512]{1,0:T(8,128)(2,1)S(1)}, bf16[64,512]{1,0:T(8,128)(2,1)S(1)}, u32[]{:S(2)}, u32[]{:S(2)}) collective-permute-start(bf16[64,512]{1,0:T(8,128)(2,1)S(1)} %get-tuple-element.46), channel_id=1, source_target_pairs={{0,1},{1,0},{2,3},{3,2},{4,5},{5,4},{6,7},{7,6},{8,9},{9,8},{10,11... | collective-permute-start | bytes 196616 | tf_op jit(solution)/shard_map/ppermute | solution.py:64
  31.0 1.2 %collective-permute-done.17.refs_4_ = bf16[128,512]{1,0:T(8,128)(2,1)S(1)} collective-permute-done((bf16[128,512]{1,0:T(8,128)(2,1)S(1)}, bf16[128,512]{1,0:T(8,128)(2,1)S(1)}, u32[]{:S(2)}, u32[]{:S(2)}) %collective-permute-start.17) | collective-permute-done | bytes 131104 | tf_op jit(solution)/shard_map/ppermute | solution.py:50
  32.2 1.7 %collective-permute-done.18.refs_6_ = bf16[128,256]{1,0:T(8,128)(2,1)S(1)} collective-permute-done((bf16[128,256]{1,0:T(8,128)(2,1)S(1)}, bf16[128,256]{1,0:T(8,128)(2,1)S(1)}, u32[]{:S(2)}, u32[]{:S(2)}) %collective-permute-start.18) | collective-permute-done | bytes 65568 | tf_op jit(solution)/shard_map/ppermute | solution.py:60
  34.0 0.8 %totals.1 = (bf16[128,512]{1,0:T(8,128)(2,1)}, bf16[128,256]{1,0:T(8,128)(2,1)}) custom-call(f32[128,512]{1,0:T(8,128)S(1)} %get-tuple-element.30.refs_0_, bf16[384,512]{1,0:T(8,128)(2,1)S(1)} %collective-permute-done.11.ref.refs_1_, bf16[64,512]{1,0:T(8,128)(2,1)S(1)} %collective-permute-done.15.refs_2_, ...), custom_call_target="tpu_custom_call" | custom-call | tf_op jit(solution)/shard_map/totals/pallas_call | solution.py:445
  (31 shorter events, 1.3 us)
Async XLA Ops:
  0.6 1.1 %copy-start.1 = (s32[128]{0:T(128)S(1)}, s32[128]{0:T(128)}, u32[]{:S(2)}) copy-start(s32[128]{0:T(128)} %param.11) | copy-start | bytes 1540
  0.6 2.8 %collective-permute-start = (bf16[128,512]{1,0:T(8,128)(2,1)}, bf16[128,512]{1,0:T(8,128)(2,1)S(1)}, u32[]{:S(2)}, u32[]{:S(2)}) collective-permute-start(bf16[128,512]{1,0:T(8,128)(2,1)} %refs_0_.1), channel_id=1, source_target_pairs={{0,1},{1,0},{2,3},{3,2},{4,5},{5,4},{6,7},{7,6},{8,9},{9,8},{10,11... | collective-permute-start | bytes 393224 | tf_op jit(solution)/shard_map/ppermute | solution.py:64
  1.2 2.3 %collective-permute-start.1 = (bf16[128,512]{1,0:T(8,128)(2,1)}, bf16[128,512]{1,0:T(8,128)(2,1)S(1)}, u32[]{:S(2)}, u32[]{:S(2)}) collective-permute-start(bf16[128,512]{1,0:T(8,128)(2,1)} %refs_1_.2), channel_id=1, source_target_pairs={{0,1},{1,0},{2,3},{3,2},{4,5},{5,4},{6,7},{7,6},{8,9},{9,8},{10,11... | collective-permute-start | bytes 393224 | tf_op jit(solution)/shard_map/ppermute | solution.py:64
  1.2 2.3 %collective-permute-start.2 = (bf16[128,512]{1,0:T(8,128)(2,1)}, bf16[128,512]{1,0:T(8,128)(2,1)S(1)}, u32[]{:S(2)}, u32[]{:S(2)}) collective-permute-start(bf16[128,512]{1,0:T(8,128)(2,1)} %refs_2_.1), channel_id=1, source_target_pairs={{0,1},{1,0},{2,3},{3,2},{4,5},{5,4},{6,7},{7,6},{8,9},{9,8},{10,11... | collective-permute-start | bytes 393224 | tf_op jit(solution)/shard_map/ppermute | solution.py:64
  1.7 1.8 %collective-permute-start.3 = (f32[4,128]{1,0:T(4,128)}, f32[4,128]{1,0:T(4,128)S(1)}, u32[]{:S(2)}, u32[]{:S(2)}) collective-permute-start(f32[4,128]{1,0:T(4,128)} %bitcast.4), channel_id=1, source_target_pairs={{0,1},{1,0},{2,3},{3,2},{4,5},{5,4},{6,7},{7,6},{8,9},{9,8},{10,11... | collective-permute-start | bytes 6152 | tf_op jit(solution)/shard_map/ppermute | solution.py:64
  1.8 1.7 %collective-permute-start.4 = (s32[128]{0:T(128)S(1)}, s32[128]{0:T(128)S(1)}, u32[]{:S(2)}, u32[]{:S(2)}) collective-permute-start(s32[128]{0:T(128)S(1)} %copy-done.1), channel_id=1, source_target_pairs={{0,1},{1,0},{2,3},{3,2},{4,5},{5,4},{6,7},{7,6},{8,9},{9,8},{10,11... | collective-permute-start | bytes 1544 | tf_op jit(solution)/shard_map/ppermute | solution.py:64
  3.5 2.8 %copy-start = (bf16[128,256]{1,0:T(8,128)(2,1)S(1)}, bf16[128,256]{1,0:T(8,128)(2,1)}, u32[]{:S(2)}) copy-start(bf16[128,256]{1,0:T(8,128)(2,1)} %refs_1_.3) | copy-start | bytes 196612
  3.7 12.8 %collective-permute-start.5 = (bf16[2112,128]{1,0:T(8,128)(2,1)S(1)}, bf16[2112,128]{1,0:T(8,128)(2,1)S(1)}, u32[]{:S(2)}, u32[]{:S(2)}) collective-permute-start(bf16[2112,128]{1,0:T(8,128)(2,1)S(1)} %pack_chip.1), channel_id=1, source_target_pairs={{8,0},{17,1},{0,8},{25,9},{24,16},{1,17},{16,24},{9,25},{10,2},{19... | collective-permute-start | bytes 1622024 | tf_op jit(solution)/shard_map/ppermute | solution.py:45
  6.3 6.3 %collective-permute-start.6 = (bf16[128,256]{1,0:T(8,128)(2,1)S(1)}, bf16[128,256]{1,0:T(8,128)(2,1)S(1)}, u32[]{:S(2)}, u32[]{:S(2)}) collective-permute-start(bf16[128,256]{1,0:T(8,128)(2,1)S(1)} %copy-done), channel_id=1, source_target_pairs={{6,0},{4,2},{2,4},{0,6},{7,1},{5,3},{3,5},{1,7},{14,8},{12,10},{10... | collective-permute-start | bytes 196616 | tf_op jit(solution)/shard_map/ppermute | solution.py:55
  9.9 5.9 %collective-permute-start.7 = (bf16[128,256]{1,0:T(8,128)(2,1)S(1)}, bf16[128,256]{1,0:T(8,128)(2,1)S(1)}, u32[]{:S(2)}, u32[]{:S(2)}) collective-permute-start(bf16[128,256]{1,0:T(8,128)(2,1)S(1)} %copy-done), channel_id=1, source_target_pairs={{4,0},{6,2},{0,4},{2,6},{5,1},{7,3},{1,5},{3,7},{12,8},{14,10},{8,... | collective-permute-start | bytes 196616 | tf_op jit(solution)/shard_map/ppermute | solution.py:55
  10.0 6.0 %collective-permute-start.9 = (bf16[128,256]{1,0:T(8,128)(2,1)S(1)}, bf16[128,256]{1,0:T(8,128)(2,1)S(1)}, u32[]{:S(2)}, u32[]{:S(2)}) collective-permute-start(bf16[128,256]{1,0:T(8,128)(2,1)S(1)} %copy-done), channel_id=1, source_target_pairs={{2,0},{0,2},{6,4},{4,6},{3,1},{1,3},{7,5},{5,7},{10,8},{8,10},{14,... | collective-permute-start | bytes 196616 | tf_op jit(solution)/shard_map/ppermute | solution.py:55
  10.7 10.7 %collective-permute-start.12 = (bf16[1056,128]{1,0:T(8,128)(2,1)S(1)}, bf16[1056,128]{1,0:T(8,128)(2,1)S(1)}, u32[]{:S(2)}, u32[]{:S(2)}) collective-permute-start(bf16[1056,128]{1,0:T(8,128)(2,1)S(1)} %pack.1.refs_0_), channel_id=1, source_target_pairs={{24,0},{25,1},{16,8},{17,9},{8,16},{9,17},{0,24},{1,25},{26,2},{27... | collective-permute-start | bytes 811016 | tf_op jit(solution)/shard_map/ppermute | solution.py:45
  15.9 2.4 %collective-permute-start.8 = (bf16[256,256]{1,0:T(8,128)(2,1)S(1)}, bf16[256,256]{1,0:T(8,128)(2,1)S(1)}, u32[]{:S(2)}, u32[]{:S(2)}) collective-permute-start(bf16[256,256]{1,0:T(8,128)(2,1)S(1)} %stack.2.refs_2_), channel_id=1, source_target_pairs={{0,1},{1,0},{2,3},{3,2},{4,5},{5,4},{6,7},{7,6},{8,9},{9,8},{10,11... | collective-permute-start | bytes 393224 | tf_op jit(solution)/shard_map/ppermute | solution.py:64
  16.0 2.3 %collective-permute-start.10 = (bf16[256,256]{1,0:T(8,128)(2,1)S(1)}, bf16[256,256]{1,0:T(8,128)(2,1)S(1)}, u32[]{:S(2)}, u32[]{:S(2)}) collective-permute-start(bf16[256,256]{1,0:T(8,128)(2,1)S(1)} %stack.3.refs_3_), channel_id=1, source_target_pairs={{0,1},{1,0},{2,3},{3,2},{4,5},{5,4},{6,7},{7,6},{8,9},{9,8},{10,11... | collective-permute-start | bytes 393224 | tf_op jit(solution)/shard_map/ppermute | solution.py:64
  20.2 10.1 %collective-permute-start.11 = (bf16[384,512]{1,0:T(8,128)(2,1)S(1)}, bf16[384,512]{1,0:T(8,128)(2,1)S(1)}, u32[]{:S(2)}, u32[]{:S(2)}) collective-permute-start(bf16[384,512]{1,0:T(8,128)(2,1)S(1)} %get-tuple-element.31), channel_id=1, source_target_pairs={{0,8},{1,17},{8,0},{9,25},{16,24},{17,1},{24,16},{25,9},{2,10},{3,... | collective-permute-start | bytes 1179656 | tf_op jit(solution)/shard_map/ppermute | solution.py:50
  22.2 1.6 %collective-permute-start.13 = (bf16[512,256]{1,0:T(8,128)(2,1)S(1)}, bf16[512,256]{1,0:T(8,128)(2,1)S(1)}, u32[]{:S(2)}, u32[]{:S(2)}) collective-permute-start(bf16[512,256]{1,0:T(8,128)(2,1)S(1)} %get-tuple-element.42), channel_id=1, source_target_pairs={{0,1},{1,0},{2,3},{3,2},{4,5},{5,4},{6,7},{7,6},{8,9},{9,8},{10,11... | collective-permute-start | bytes 786440 | tf_op jit(solution)/shard_map/ppermute | solution.py:64
  23.9 6.5 %collective-permute-start.14 = (bf16[128,256]{1,0:T(8,128)(2,1)S(1)}, bf16[128,256]{1,0:T(8,128)(2,1)S(1)}, u32[]{:S(2)}, u32[]{:S(2)}) collective-permute-start(bf16[128,256]{1,0:T(8,128)(2,1)S(1)} %get-tuple-element.43), channel_id=1, source_target_pairs={{0,4},{2,6},{4,0},{6,2},{1,5},{3,7},{5,1},{7,3},{8,12},{10,14},{12... | collective-permute-start | bytes 196616 | tf_op jit(solution)/shard_map/ppermute | solution.py:60
  26.0 6.2 %collective-permute-start.17 = (bf16[128,512]{1,0:T(8,128)(2,1)S(1)}, bf16[128,512]{1,0:T(8,128)(2,1)S(1)}, u32[]{:S(2)}, u32[]{:S(2)}) collective-permute-start(bf16[128,512]{1,0:T(8,128)(2,1)S(1)} %get-tuple-element.47), channel_id=1, source_target_pairs={{0,24},{1,25},{8,16},{9,17},{16,8},{17,9},{24,0},{25,1},{2,26},{3,... | collective-permute-start | bytes 393224 | tf_op jit(solution)/shard_map/ppermute | solution.py:50
  27.7 6.2 %collective-permute-start.18 = (bf16[128,256]{1,0:T(8,128)(2,1)S(1)}, bf16[128,256]{1,0:T(8,128)(2,1)S(1)}, u32[]{:S(2)}, u32[]{:S(2)}) collective-permute-start(bf16[128,256]{1,0:T(8,128)(2,1)S(1)} %get-tuple-element.49), channel_id=1, source_target_pairs={{0,6},{2,4},{4,2},{6,0},{1,7},{3,5},{5,3},{7,1},{8,14},{10,12},{12... | collective-permute-start | bytes 196616 | tf_op jit(solution)/shard_map/ppermute | solution.py:60
  29.0 5.0 %collective-permute-start.19 = (bf16[128,256]{1,0:T(8,128)(2,1)S(1)}, bf16[128,256]{1,0:T(8,128)(2,1)S(1)}, u32[]{:S(2)}, u32[]{:S(2)}) collective-permute-start(bf16[128,256]{1,0:T(8,128)(2,1)S(1)} %get-tuple-element.51), channel_id=1, source_target_pairs={{0,2},{2,0},{4,6},{6,4},{1,3},{3,1},{5,7},{7,5},{8,10},{10,8},{12,... | collective-permute-start | bytes 196616 | tf_op jit(solution)/shard_map/ppermute | solution.py:60
  30.4 3.6 %collective-permute-start.15 = (bf16[64,512]{1,0:T(8,128)(2,1)S(1)}, bf16[64,512]{1,0:T(8,128)(2,1)S(1)}, u32[]{:S(2)}, u32[]{:S(2)}) collective-permute-start(bf16[64,512]{1,0:T(8,128)(2,1)S(1)} %get-tuple-element.45), channel_id=1, source_target_pairs={{0,1},{1,0},{2,3},{3,2},{4,5},{5,4},{6,7},{7,6},{8,9},{9,8},{10,11... | collective-permute-start | bytes 196616 | tf_op jit(solution)/shard_map/ppermute | solution.py:64
  30.5 3.5 %collective-permute-start.16 = (bf16[64,512]{1,0:T(8,128)(2,1)S(1)}, bf16[64,512]{1,0:T(8,128)(2,1)S(1)}, u32[]{:S(2)}, u32[]{:S(2)}) collective-permute-start(bf16[64,512]{1,0:T(8,128)(2,1)S(1)} %get-tuple-element.46), channel_id=1, source_target_pairs={{0,1},{1,0},{2,3},{3,2},{4,5},{5,4},{6,7},{7,6},{8,9},{9,8},{10,11... | collective-permute-start | bytes 196616 | tf_op jit(solution)/shard_map/ppermute | solution.py:64

commit v9 on v8

--- a/solution.py
+++ b/solution.py
@@ -487,7 +487,7 @@
     for steps, back in zip(rounds, returned):
         dq_parts.append(back)
         if len(steps) == 2:
-            last = min(2, zed - 1)
+            last = min(1, zed - 1)
             back, dkv_parts[last] = lax.optimization_barrier((back, dkv_parts[last]))
             dq_parts += [swap_cores(piece) for piece in split(back, PIECES)]
     return tuple(totals([dq_parts, dkv_parts], tok))

time: 34.9 us -> 34.7 us (level)
  waiting for transfers between devices: 8.48 us -> 7.82 us
  starting transfers between devices: 17.8 us -> 18.3 us
    ppermute x3, waiting for transfers between devices: 3.02 us -> 1.03 us  [give_back_z(): lax.ppermute(value, 'z', [(z, peer(z, step, count)) for z in range(count)])]
    ppermute x2, waiting for transfers between devices: 1.2 us -> 2.53 us  [give_back(): return lax.ppermute(value, ('inner', 'core'), [(b, a) for a, b in pairs])]
    ppermute x3, starting transfers between devices: 3.54 us -> 4.18 us  [give_back_z(): lax.ppermute(value, 'z', [(z, peer(z, step, count)) for z in range(count)])]
where the time goes in v9:
time: 34.7 us; the launch traced here: 34.5 us
  starting transfers between devices  18.3 us (53%)
  waiting for transfers between devices  7.82 us (23%)
  Pallas kernels  7.6 us (22%)
  between operations  0.8 us (2%)
    pallas_call x4, Pallas kernels, visit(): pl.pallas_call(functools.partial(visit_kernel, groups, side, fresh, resum...  5.29 us
    ppermute x3, starting transfers between devices, fetch_z(): lax.ppermute(value, 'z', [(peer(z, step, count), z) for z in range(count)])  4.39 us
    ppermute x3, starting transfers between devices, give_back_z(): lax.ppermute(value, 'z', [(z, peer(z, step, count)) for z in range(count)])  4.18 us
    ppermute x2, starting transfers between devices, fetch(): lax.ppermute(value, ('inner', 'core'), inner_pairs(steps, lax.axis_size('...  4.16 us
    ppermute x3, waiting for transfers between devices, fetch_z(): lax.ppermute(value, 'z', [(peer(z, step, count), z) for z in range(count)])  3.57 us
    ppermute x10, starting transfers between devices, swap_cores(): return lax.ppermute(value, 'core', [(0, 1), (1, 0)])  2.8 us
    ppermute x2, starting transfers between devices, give_back(): return lax.ppermute(value, ('inner', 'core'), [(b, a) for a, b in pairs])  2.76 us
    ppermute x2, waiting for transfers between devices, give_back(): return lax.ppermute(value, ('inner', 'core'), [(b, a) for a, b in pairs])  2.53 us
  transfers between devices with their start and end apart: 20, of which 6 were waited for; matrix products, arithmetic and copies ran while one was open for 0% of the time, Pallas kernels for 19%

profile of v9, /device:TPU:0, one launch (start us, length us, event | category | flops | bytes accessed | tf_op | source)
XLA Modules:
  0.0 34.5 jit_solution(11433144900595968007)
XLA Ops:
  0.6 0.5 %collective-permute-start = (bf16[128,512]{1,0:T(8,128)(2,1)}, bf16[128,512]{1,0:T(8,128)(2,1)S(1)}, u32[]{:S(2)}, u32[]{:S(2)}) collective-permute-start(bf16[128,512]{1,0:T(8,128)(2,1)} %refs_0_.1), channel_id=1, source_target_pairs={{0,1},{1,0},{2,3},{3,2},{4,5},{5,4},{6,7},{7,6},{8,9},{9,8},{10,11... | collective-permute-start | bytes 393224 | tf_op jit(solution)/shard_map/ppermute | solution.py:64
  1.2 0.4 %collective-permute-start.2 = (bf16[128,512]{1,0:T(8,128)(2,1)}, bf16[128,512]{1,0:T(8,128)(2,1)S(1)}, u32[]{:S(2)}, u32[]{:S(2)}) collective-permute-start(bf16[128,512]{1,0:T(8,128)(2,1)} %refs_2_.1), channel_id=1, source_target_pairs={{0,1},{1,0},{2,3},{3,2},{4,5},{5,4},{6,7},{7,6},{8,9},{9,8},{10,11... | collective-permute-start | bytes 393224 | tf_op jit(solution)/shard_map/ppermute | solution.py:64
  1.8 0.4 %collective-permute-start.4 = (s32[128]{0:T(128)S(1)}, s32[128]{0:T(128)S(1)}, u32[]{:S(2)}, u32[]{:S(2)}) collective-permute-start(s32[128]{0:T(128)S(1)} %copy-done.1), channel_id=1, source_target_pairs={{0,1},{1,0},{2,3},{3,2},{4,5},{5,4},{6,7},{7,6},{8,9},{9,8},{10,11... | collective-permute-start | bytes 1544 | tf_op jit(solution)/shard_map/ppermute | solution.py:64
  2.2 1.3 %pack.1.refs_0_ = bf16[1056,128]{1,0:T(8,128)(2,1)S(1)} custom-call(bf16[128,512]{1,0:T(8,128)(2,1)} %refs_0_.1, bf16[128,512]{1,0:T(8,128)(2,1)} %refs_1_.2, bf16[128,512]{1,0:T(8,128)(2,1)} %refs_2_.1, f32[4,128]{1,0:T(4,128)} %bitcast.5, s32[1,128]{1,0:T(1,128)} %bitcast.6), custom_call_target="tpu_custom_call" | custom-call | tf_op jit(solution)/shard_map/pack/pallas_call | solution.py:120
  3.7 2.6 %collective-permute-start.5 = (bf16[2112,128]{1,0:T(8,128)(2,1)S(1)}, bf16[2112,128]{1,0:T(8,128)(2,1)S(1)}, u32[]{:S(2)}, u32[]{:S(2)}) collective-permute-start(bf16[2112,128]{1,0:T(8,128)(2,1)S(1)} %pack_chip.1), channel_id=1, source_target_pairs={{8,0},{17,1},{0,8},{25,9},{24,16},{1,17},{16,24},{9,25},{10,2},{19... | collective-permute-start | bytes 1622024 | tf_op jit(solution)/shard_map/ppermute | solution.py:45
  6.3 3.6 %collective-permute-start.6 = (bf16[128,256]{1,0:T(8,128)(2,1)S(1)}, bf16[128,256]{1,0:T(8,128)(2,1)S(1)}, u32[]{:S(2)}, u32[]{:S(2)}) collective-permute-start(bf16[128,256]{1,0:T(8,128)(2,1)S(1)} %copy-done), channel_id=1, source_target_pairs={{6,0},{4,2},{2,4},{0,6},{7,1},{5,3},{3,5},{1,7},{14,8},{12,10},{10... | collective-permute-start | bytes 196616 | tf_op jit(solution)/shard_map/ppermute | solution.py:55
  10.0 0.8 %collective-permute-start.9 = (bf16[128,256]{1,0:T(8,128)(2,1)S(1)}, bf16[128,256]{1,0:T(8,128)(2,1)S(1)}, u32[]{:S(2)}, u32[]{:S(2)}) collective-permute-start(bf16[128,256]{1,0:T(8,128)(2,1)S(1)} %copy-done), channel_id=1, source_target_pairs={{2,0},{0,2},{6,4},{4,6},{3,1},{1,3},{7,5},{5,7},{10,8},{8,10},{14,... | collective-permute-start | bytes 196616 | tf_op jit(solution)/shard_map/ppermute | solution.py:55
  10.7 1.5 %collective-permute-start.12 = (bf16[1056,128]{1,0:T(8,128)(2,1)S(1)}, bf16[1056,128]{1,0:T(8,128)(2,1)S(1)}, u32[]{:S(2)}, u32[]{:S(2)}) collective-permute-start(bf16[1056,128]{1,0:T(8,128)(2,1)S(1)} %pack.1.refs_0_), channel_id=1, source_target_pairs={{24,0},{25,1},{16,8},{17,9},{8,16},{9,17},{0,24},{1,25},{26,2},{27... | collective-permute-start | bytes 811016 | tf_op jit(solution)/shard_map/ppermute | solution.py:45
  12.6 3.2 %collective-permute-done.7.refs_1_ = bf16[128,256]{1,0:T(8,128)(2,1)S(1)} collective-permute-done((bf16[128,256]{1,0:T(8,128)(2,1)S(1)}, bf16[128,256]{1,0:T(8,128)(2,1)S(1)}, u32[]{:S(2)}, u32[]{:S(2)}) %collective-permute-start.7) | collective-permute-done | bytes 65568 | tf_op jit(solution)/shard_map/ppermute | solution.py:55
  16.0 0.5 %collective-permute-start.10 = (bf16[256,256]{1,0:T(8,128)(2,1)S(1)}, bf16[256,256]{1,0:T(8,128)(2,1)S(1)}, u32[]{:S(2)}, u32[]{:S(2)}) collective-permute-start(bf16[256,256]{1,0:T(8,128)(2,1)S(1)} %stack.3.refs_3_), channel_id=1, source_target_pairs={{0,1},{1,0},{2,3},{3,2},{4,5},{5,4},{6,7},{7,6},{8,9},{9,8},{10,11... | collective-permute-start | bytes 393224 | tf_op jit(solution)/shard_map/ppermute | solution.py:64
  16.5 1.7 %visit.4 = (f32[128,512]{1,0:T(8,128)S(1)}, f32[128,512]{1,0:T(8,128)S(1)}, f32[128,512]{1,0:T(8,128)S(1)}, f32[512,256]{1,0:T(8,128)S(1)}, bf16[512,128]{1,0:T(...) custom-call(bf16[1056,128]{1,0:T(8,128)(2,1)S(1)} %pack.1.refs_0_, ...), custom_call_target="tpu_custom_call" | custom-call | flops 450000000 | bytes 1000 | tf_op jit(solution)/shard_map/visit/pallas_call | solution.py:358
  18.3 2.0 %visit.5 = (f32[128,512]{1,0:T(8,128)S(1)}, bf16[384,512]{1,0:T(8,128)(2,1)S(1)}, f32[512,256]{1,0:T(8,128)S(1)}, bf16[512,128]{1,0:T(8,128)(2,1)S(1)}, bf16[512...) custom-call(bf16[1056,128]{1,0:T(8,128)(2,1)S(1)} %pack.1.refs_0_, ...), custom_call_target="tpu_custom_call" | custom-call | flops 450000000 | bytes 1000 | tf_op jit(solution)/shard_map/visit/pallas_call | solution.py:358
  20.2 1.2 %collective-permute-start.11 = (bf16[384,512]{1,0:T(8,128)(2,1)S(1)}, bf16[384,512]{1,0:T(8,128)(2,1)S(1)}, u32[]{:S(2)}, u32[]{:S(2)}) collective-permute-start(bf16[384,512]{1,0:T(8,128)(2,1)S(1)} %get-tuple-element.31), channel_id=1, source_target_pairs={{0,8},{1,17},{8,0},{9,25},{16,24},{17,1},{24,16},{25,9},{2,10},{3,... | collective-permute-start | bytes 1179656 | tf_op jit(solution)/shard_map/ppermute | solution.py:50
  21.5 0.7 %visit.6 = (f32[128,512]{1,0:T(8,128)S(1)}, bf16[512,256]{1,0:T(8,128)(2,1)S(1)}) custom-call(bf16[1056,128]{1,0:T(8,128)(2,1)S(1)} %collective-permute-done.12.refs_0_, bf16[512,128]{1,0:T(8,128)(2,1)S(1)} %get-tuple-element.36.refs_1_, bf16[512,128]{1,0:T(8,128)(2,1)S(1)} %get-tuple-element.37.refs_2_, bf16[128,512]{1,0:T(8,128)(2,1)S(1)} %get-tuple-element.38.refs_3_, ...), custom_call_target="tpu_custom_call" | custom-call | flops 150000000 | bytes 1000 | tf_op jit(solution)/shard_map/visit/pallas_call | solution.py:358
  22.3 0.8 %visit.7 = (bf16[128,512]{1,0:T(8,128)(2,1)S(1)}, f32[512,256]{1,0:T(8,128)S(1)}) custom-call(bf16[1056,128]{1,0:T(8,128)(2,1)S(1)} %collective-permute-done.12.refs_0_, bf16[512,128]{1,0:T(8,128)(2,1)S(1)} %get-tuple-element.32.refs_1_, bf16[512,128]{1,0:T(8,128)(2,1)S(1)} %get-tuple-element.33.refs_2_, bf16[128,512]{1,0:T(8,128)(2,1)S(1)} %get-tuple-element.34.refs_3_, ...), custom_call_target="tpu_custom_call" | custom-call | flops 150000000 | bytes 1000 | tf_op jit(solution)/shard_map/visit/pallas_call | solution.py:358
  23.1 0.7 %collective-permute-done.13.refs_0_ = bf16[512,256]{1,0:T(8,128)(2,1)S(1)} collective-permute-done((bf16[512,256]{1,0:T(8,128)(2,1)S(1)}, bf16[512,256]{1,0:T(8,128)(2,1)S(1)}, u32[]{:S(2)}, u32[]{:S(2)}) %collective-permute-start.13) | collective-permute-done | bytes 262176 | tf_op jit(solution)/shard_map/ppermute | solution.py:64
  23.9 3.1 %collective-permute-start.14 = (bf16[128,256]{1,0:T(8,128)(2,1)S(1)}, bf16[128,256]{1,0:T(8,128)(2,1)S(1)}, u32[]{:S(2)}, u32[]{:S(2)}) collective-permute-start(bf16[128,256]{1,0:T(8,128)(2,1)S(1)} %get-tuple-element.43), channel_id=1, source_target_pairs={{0,6},{2,4},{4,2},{6,0},{1,7},{3,5},{5,3},{7,1},{8,14},{10,12},{12... | collective-permute-start | bytes 196616 | tf_op jit(solution)/shard_map/ppermute | solution.py:60
  27.0 1.5 %collective-permute-start.17 = (bf16[128,512]{1,0:T(8,128)(2,1)S(1)}, bf16[128,512]{1,0:T(8,128)(2,1)S(1)}, u32[]{:S(2)}, u32[]{:S(2)}) collective-permute-start(bf16[128,512]{1,0:T(8,128)(2,1)S(1)} %get-tuple-element.47), channel_id=1, source_target_pairs={{0,24},{1,25},{8,16},{9,17},{16,8},{17,9},{24,0},{25,1},{2,26},{3,... | collective-permute-start | bytes 393224 | tf_op jit(solution)/shard_map/ppermute | solution.py:50
  28.6 1.0 %collective-permute-start.19 = (bf16[128,256]{1,0:T(8,128)(2,1)S(1)}, bf16[128,256]{1,0:T(8,128)(2,1)S(1)}, u32[]{:S(2)}, u32[]{:S(2)}) collective-permute-start(bf16[128,256]{1,0:T(8,128)(2,1)S(1)} %get-tuple-element.51), channel_id=1, source_target_pairs={{0,2},{2,0},{4,6},{6,4},{1,3},{3,1},{5,7},{7,5},{8,10},{10,8},{12,... | collective-permute-start | bytes 196616 | tf_op jit(solution)/shard_map/ppermute | solution.py:60
  29.6 0.5 %collective-permute-done.14.refs_6_ = bf16[128,256]{1,0:T(8,128)(2,1)S(1)} collective-permute-done((bf16[128,256]{1,0:T(8,128)(2,1)S(1)}, bf16[128,256]{1,0:T(8,128)(2,1)S(1)}, u32[]{:S(2)}, u32[]{:S(2)}) %collective-permute-start.14) | collective-permute-done | bytes 65568 | tf_op jit(solution)/shard_map/ppermute | solution.py:60
  30.2 0.5 %collective-permute-start.16 = (bf16[64,512]{1,0:T(8,128)(2,1)S(1)}, bf16[64,512]{1,0:T(8,128)(2,1)S(1)}, u32[]{:S(2)}, u32[]{:S(2)}) collective-permute-start(bf16[64,512]{1,0:T(8,128)(2,1)S(1)} %get-tuple-element.46), channel_id=1, source_target_pairs={{0,1},{1,0},{2,3},{3,2},{4,5},{5,4},{6,7},{7,6},{8,9},{9,8},{10,11... | collective-permute-start | bytes 196616 | tf_op jit(solution)/shard_map/ppermute | solution.py:64
  30.7 2.5 %collective-permute-done.17.refs_4_ = bf16[128,512]{1,0:T(8,128)(2,1)S(1)} collective-permute-done((bf16[128,512]{1,0:T(8,128)(2,1)S(1)}, bf16[128,512]{1,0:T(8,128)(2,1)S(1)}, u32[]{:S(2)}, u32[]{:S(2)}) %collective-permute-start.17) | collective-permute-done | bytes 131104 | tf_op jit(solution)/shard_map/ppermute | solution.py:50
  33.2 0.6 %collective-permute-done.18.refs_7_ = bf16[128,256]{1,0:T(8,128)(2,1)S(1)} collective-permute-done((bf16[128,256]{1,0:T(8,128)(2,1)S(1)}, bf16[128,256]{1,0:T(8,128)(2,1)S(1)}, u32[]{:S(2)}, u32[]{:S(2)}) %collective-permute-start.18) | collective-permute-done | bytes 65568 | tf_op jit(solution)/shard_map/ppermute | solution.py:60
  33.8 0.8 %totals.1 = (bf16[128,512]{1,0:T(8,128)(2,1)}, bf16[128,256]{1,0:T(8,128)(2,1)}) custom-call(f32[128,512]{1,0:T(8,128)S(1)} %get-tuple-element.30.refs_0_, bf16[384,512]{1,0:T(8,128)(2,1)S(1)} %collective-permute-done.11.ref.refs_1_, bf16[64,512]{1,0:T(8,128)(2,1)S(1)} %collective-permute-done.15.refs_2_, ...), custom_call_target="tpu_custom_call" | custom-call | tf_op jit(solution)/shard_map/totals/pallas_call | solution.py:445
  (31 shorter events, 1.1 us)
Async XLA Ops:
  0.6 1.1 %copy-start.1 = (s32[128]{0:T(128)S(1)}, s32[128]{0:T(128)}, u32[]{:S(2)}) copy-start(s32[128]{0:T(128)} %param.11) | copy-start | bytes 1540
  0.6 2.8 %collective-permute-start = (bf16[128,512]{1,0:T(8,128)(2,1)}, bf16[128,512]{1,0:T(8,128)(2,1)S(1)}, u32[]{:S(2)}, u32[]{:S(2)}) collective-permute-start(bf16[128,512]{1,0:T(8,128)(2,1)} %refs_0_.1), channel_id=1, source_target_pairs={{0,1},{1,0},{2,3},{3,2},{4,5},{5,4},{6,7},{7,6},{8,9},{9,8},{10,11... | collective-permute-start | bytes 393224 | tf_op jit(solution)/shard_map/ppermute | solution.py:64
  1.2 2.3 %collective-permute-start.1 = (bf16[128,512]{1,0:T(8,128)(2,1)}, bf16[128,512]{1,0:T(8,128)(2,1)S(1)}, u32[]{:S(2)}, u32[]{:S(2)}) collective-permute-start(bf16[128,512]{1,0:T(8,128)(2,1)} %refs_1_.2), channel_id=1, source_target_pairs={{0,1},{1,0},{2,3},{3,2},{4,5},{5,4},{6,7},{7,6},{8,9},{9,8},{10,11... | collective-permute-start | bytes 393224 | tf_op jit(solution)/shard_map/ppermute | solution.py:64
  1.2 2.3 %collective-permute-start.2 = (bf16[128,512]{1,0:T(8,128)(2,1)}, bf16[128,512]{1,0:T(8,128)(2,1)S(1)}, u32[]{:S(2)}, u32[]{:S(2)}) collective-permute-start(bf16[128,512]{1,0:T(8,128)(2,1)} %refs_2_.1), channel_id=1, source_target_pairs={{0,1},{1,0},{2,3},{3,2},{4,5},{5,4},{6,7},{7,6},{8,9},{9,8},{10,11... | collective-permute-start | bytes 393224 | tf_op jit(solution)/shard_map/ppermute | solution.py:64
  1.7 1.8 %collective-permute-start.3 = (f32[4,128]{1,0:T(4,128)}, f32[4,128]{1,0:T(4,128)S(1)}, u32[]{:S(2)}, u32[]{:S(2)}) collective-permute-start(f32[4,128]{1,0:T(4,128)} %bitcast.4), channel_id=1, source_target_pairs={{0,1},{1,0},{2,3},{3,2},{4,5},{5,4},{6,7},{7,6},{8,9},{9,8},{10,11... | collective-permute-start | bytes 6152 | tf_op jit(solution)/shard_map/ppermute | solution.py:64
  1.8 1.7 %collective-permute-start.4 = (s32[128]{0:T(128)S(1)}, s32[128]{0:T(128)S(1)}, u32[]{:S(2)}, u32[]{:S(2)}) collective-permute-start(s32[128]{0:T(128)S(1)} %copy-done.1), channel_id=1, source_target_pairs={{0,1},{1,0},{2,3},{3,2},{4,5},{5,4},{6,7},{7,6},{8,9},{9,8},{10,11... | collective-permute-start | bytes 1544 | tf_op jit(solution)/shard_map/ppermute | solution.py:64
  3.5 2.8 %copy-start = (bf16[128,256]{1,0:T(8,128)(2,1)S(1)}, bf16[128,256]{1,0:T(8,128)(2,1)}, u32[]{:S(2)}) copy-start(bf16[128,256]{1,0:T(8,128)(2,1)} %refs_1_.3) | copy-start | bytes 196612
  3.7 12.8 %collective-permute-start.5 = (bf16[2112,128]{1,0:T(8,128)(2,1)S(1)}, bf16[2112,128]{1,0:T(8,128)(2,1)S(1)}, u32[]{:S(2)}, u32[]{:S(2)}) collective-permute-start(bf16[2112,128]{1,0:T(8,128)(2,1)S(1)} %pack_chip.1), channel_id=1, source_target_pairs={{8,0},{17,1},{0,8},{25,9},{24,16},{1,17},{16,24},{9,25},{10,2},{19... | collective-permute-start | bytes 1622024 | tf_op jit(solution)/shard_map/ppermute | solution.py:45
  6.3 6.3 %collective-permute-start.6 = (bf16[128,256]{1,0:T(8,128)(2,1)S(1)}, bf16[128,256]{1,0:T(8,128)(2,1)S(1)}, u32[]{:S(2)}, u32[]{:S(2)}) collective-permute-start(bf16[128,256]{1,0:T(8,128)(2,1)S(1)} %copy-done), channel_id=1, source_target_pairs={{6,0},{4,2},{2,4},{0,6},{7,1},{5,3},{3,5},{1,7},{14,8},{12,10},{10... | collective-permute-start | bytes 196616 | tf_op jit(solution)/shard_map/ppermute | solution.py:55
  9.9 5.9 %collective-permute-start.7 = (bf16[128,256]{1,0:T(8,128)(2,1)S(1)}, bf16[128,256]{1,0:T(8,128)(2,1)S(1)}, u32[]{:S(2)}, u32[]{:S(2)}) collective-permute-start(bf16[128,256]{1,0:T(8,128)(2,1)S(1)} %copy-done), channel_id=1, source_target_pairs={{4,0},{6,2},{0,4},{2,6},{5,1},{7,3},{1,5},{3,7},{12,8},{14,10},{8,... | collective-permute-start | bytes 196616 | tf_op jit(solution)/shard_map/ppermute | solution.py:55
  10.0 6.0 %collective-permute-start.9 = (bf16[128,256]{1,0:T(8,128)(2,1)S(1)}, bf16[128,256]{1,0:T(8,128)(2,1)S(1)}, u32[]{:S(2)}, u32[]{:S(2)}) collective-permute-start(bf16[128,256]{1,0:T(8,128)(2,1)S(1)} %copy-done), channel_id=1, source_target_pairs={{2,0},{0,2},{6,4},{4,6},{3,1},{1,3},{7,5},{5,7},{10,8},{8,10},{14,... | collective-permute-start | bytes 196616 | tf_op jit(solution)/shard_map/ppermute | solution.py:55
  10.7 10.7 %collective-permute-start.12 = (bf16[1056,128]{1,0:T(8,128)(2,1)S(1)}, bf16[1056,128]{1,0:T(8,128)(2,1)S(1)}, u32[]{:S(2)}, u32[]{:S(2)}) collective-permute-start(bf16[1056,128]{1,0:T(8,128)(2,1)S(1)} %pack.1.refs_0_), channel_id=1, source_target_pairs={{24,0},{25,1},{16,8},{17,9},{8,16},{9,17},{0,24},{1,25},{26,2},{27... | collective-permute-start | bytes 811016 | tf_op jit(solution)/shard_map/ppermute | solution.py:45
  15.9 2.4 %collective-permute-start.8 = (bf16[256,256]{1,0:T(8,128)(2,1)S(1)}, bf16[256,256]{1,0:T(8,128)(2,1)S(1)}, u32[]{:S(2)}, u32[]{:S(2)}) collective-permute-start(bf16[256,256]{1,0:T(8,128)(2,1)S(1)} %stack.2.refs_2_), channel_id=1, source_target_pairs={{0,1},{1,0},{2,3},{3,2},{4,5},{5,4},{6,7},{7,6},{8,9},{9,8},{10,11... | collective-permute-start | bytes 393224 | tf_op jit(solution)/shard_map/ppermute | solution.py:64
  16.0 2.3 %collective-permute-start.10 = (bf16[256,256]{1,0:T(8,128)(2,1)S(1)}, bf16[256,256]{1,0:T(8,128)(2,1)S(1)}, u32[]{:S(2)}, u32[]{:S(2)}) collective-permute-start(bf16[256,256]{1,0:T(8,128)(2,1)S(1)} %stack.3.refs_3_), channel_id=1, source_target_pairs={{0,1},{1,0},{2,3},{3,2},{4,5},{5,4},{6,7},{7,6},{8,9},{9,8},{10,11... | collective-permute-start | bytes 393224 | tf_op jit(solution)/shard_map/ppermute | solution.py:64
  20.2 9.8 %collective-permute-start.11 = (bf16[384,512]{1,0:T(8,128)(2,1)S(1)}, bf16[384,512]{1,0:T(8,128)(2,1)S(1)}, u32[]{:S(2)}, u32[]{:S(2)}) collective-permute-start(bf16[384,512]{1,0:T(8,128)(2,1)S(1)} %get-tuple-element.31), channel_id=1, source_target_pairs={{0,8},{1,17},{8,0},{9,25},{16,24},{17,1},{24,16},{25,9},{2,10},{3,... | collective-permute-start | bytes 1179656 | tf_op jit(solution)/shard_map/ppermute | solution.py:50
  22.2 1.6 %collective-permute-start.13 = (bf16[512,256]{1,0:T(8,128)(2,1)S(1)}, bf16[512,256]{1,0:T(8,128)(2,1)S(1)}, u32[]{:S(2)}, u32[]{:S(2)}) collective-permute-start(bf16[512,256]{1,0:T(8,128)(2,1)S(1)} %get-tuple-element.42), channel_id=1, source_target_pairs={{0,1},{1,0},{2,3},{3,2},{4,5},{5,4},{6,7},{7,6},{8,9},{9,8},{10,11... | collective-permute-start | bytes 786440 | tf_op jit(solution)/shard_map/ppermute | solution.py:64
  23.9 6.2 %collective-permute-start.14 = (bf16[128,256]{1,0:T(8,128)(2,1)S(1)}, bf16[128,256]{1,0:T(8,128)(2,1)S(1)}, u32[]{:S(2)}, u32[]{:S(2)}) collective-permute-start(bf16[128,256]{1,0:T(8,128)(2,1)S(1)} %get-tuple-element.43), channel_id=1, source_target_pairs={{0,6},{2,4},{4,2},{6,0},{1,7},{3,5},{5,3},{7,1},{8,14},{10,12},{12... | collective-permute-start | bytes 196616 | tf_op jit(solution)/shard_map/ppermute | solution.py:60
  27.0 6.2 %collective-permute-start.17 = (bf16[128,512]{1,0:T(8,128)(2,1)S(1)}, bf16[128,512]{1,0:T(8,128)(2,1)S(1)}, u32[]{:S(2)}, u32[]{:S(2)}) collective-permute-start(bf16[128,512]{1,0:T(8,128)(2,1)S(1)} %get-tuple-element.47), channel_id=1, source_target_pairs={{0,24},{1,25},{8,16},{9,17},{16,8},{17,9},{24,0},{25,1},{2,26},{3,... | collective-permute-start | bytes 393224 | tf_op jit(solution)/shard_map/ppermute | solution.py:50
  28.6 5.2 %collective-permute-start.18 = (bf16[128,256]{1,0:T(8,128)(2,1)S(1)}, bf16[128,256]{1,0:T(8,128)(2,1)S(1)}, u32[]{:S(2)}, u32[]{:S(2)}) collective-permute-start(bf16[128,256]{1,0:T(8,128)(2,1)S(1)} %get-tuple-element.50), channel_id=1, source_target_pairs={{0,4},{2,6},{4,0},{6,2},{1,5},{3,7},{5,1},{7,3},{8,12},{10,14},{12... | collective-permute-start | bytes 196616 | tf_op jit(solution)/shard_map/ppermute | solution.py:60
  28.6 5.2 %collective-permute-start.19 = (bf16[128,256]{1,0:T(8,128)(2,1)S(1)}, bf16[128,256]{1,0:T(8,128)(2,1)S(1)}, u32[]{:S(2)}, u32[]{:S(2)}) collective-permute-start(bf16[128,256]{1,0:T(8,128)(2,1)S(1)} %get-tuple-element.51), channel_id=1, source_target_pairs={{0,2},{2,0},{4,6},{6,4},{1,3},{3,1},{5,7},{7,5},{8,10},{10,8},{12,... | collective-permute-start | bytes 196616 | tf_op jit(solution)/shard_map/ppermute | solution.py:60
  30.1 3.7 %collective-permute-start.15 = (bf16[64,512]{1,0:T(8,128)(2,1)S(1)}, bf16[64,512]{1,0:T(8,128)(2,1)S(1)}, u32[]{:S(2)}, u32[]{:S(2)}) collective-permute-start(bf16[64,512]{1,0:T(8,128)(2,1)S(1)} %get-tuple-element.45), channel_id=1, source_target_pairs={{0,1},{1,0},{2,3},{3,2},{4,5},{5,4},{6,7},{7,6},{8,9},{9,8},{10,11... | collective-permute-start | bytes 196616 | tf_op jit(solution)/shard_map/ppermute | solution.py:64
  30.2 3.6 %collective-permute-start.16 = (bf16[64,512]{1,0:T(8,128)(2,1)S(1)}, bf16[64,512]{1,0:T(8,128)(2,1)S(1)}, u32[]{:S(2)}, u32[]{:S(2)}) collective-permute-start(bf16[64,512]{1,0:T(8,128)(2,1)S(1)} %get-tuple-element.46), channel_id=1, source_target_pairs={{0,1},{1,0},{2,3},{3,2},{4,5},{5,4},{6,7},{7,6},{8,9},{9,8},{10,11... | collective-permute-start | bytes 196616 | tf_op jit(solution)/shard_map/ppermute | solution.py:64
